TPU v7x, 32 devices: a whole 2x2x4 slice. The times are simulated.
32 devices in a mesh: dp: 4 (over y, x), fsdp: 8 (over z, core).
Axes of the slice: x: 2, y: 2, z: 4, core: 2. Of those that a mesh axis runs over, the one named last changes fastest.
Arguments:
- latents: float32 [2, 96, 4096], P(None, ('dp', 'fsdp')), may hold values from -6 to 6
- noise: float32 [2, 96, 4096], P(None, ('dp', 'fsdp')), may hold values from -6 to 6
- timesteps: int32 [2, 96], P(None, ('dp', 'fsdp')), may hold values from 1 to 999
- labels: int32 [2, 96], P(None, ('dp', 'fsdp')), may hold values from 0 to 999
- patch_mask: int32 [2, 96, 256], P(None, ('dp', 'fsdp')), may hold values from 0 to 1, as said below
- counts: int32 [2, 32], P(None, ('dp', 'fsdp')), may hold values from 0 to 3, as said below
- owners: int32 [3], replicated, may hold values from 0 to 3, as said below
- tables_w: float32 [384, 1273], P('fsdp')
- tables_m: float32 [384, 1273], P('fsdp'), may hold values from -1.1920929e-06 to 1.1920929e-06
- tables_v: float32 [384, 1273], P('fsdp'), may hold values from 2.807061e-15 to 1.1228244e-14
- rows_w: float32 [384, 17312], P('fsdp')
- rows_m: float32 [384, 17312], P('fsdp'), may hold values from -1.1920929e-06 to 1.1920929e-06
- rows_v: float32 [384, 17312], P('fsdp'), may hold values from 2.807061e-15 to 8.9825953e-14
- down_w: float32 [384, 4608], P('fsdp'), may hold values from -0.15625 to 0.15625
- down_m: float32 [384, 4608], P('fsdp'), may hold values from -1.1920929e-06 to 1.1920929e-06
- down_v: float32 [384, 4608], P('fsdp'), may hold values from 2.807061e-15 to 1.1228244e-14
Outputs:
- loss: float32 [], replicated
- grad_norm: float32 [], replicated
- tables_w_new: float32 [384, 1273], P('fsdp')
- tables_m_new: float32 [384, 1273], P('fsdp')
- tables_v_new: float32 [384, 1273], P('fsdp')
- rows_w_new: float32 [384, 17312], P('fsdp', 'dp')
- rows_m_new: float32 [384, 17312], P('fsdp', 'dp')
- rows_v_new: float32 [384, 17312], P('fsdp', 'dp')
- down_w_new: float32 [384, 4608], P('fsdp', 'dp')
- down_m_new: float32 [384, 4608], P('fsdp', 'dp')
- down_v_new: float32 [384, 4608], P('fsdp', 'dp')
Inputs may be any that keep to these rules, and one draw needn't show every extreme that they name: `counts`: A device uses the first entries of its 3 slots; in each micro-batch some device uses all 3. `owners`: three distinct dp indices, for the groups tables, rows and down in that order. `patch_mask`: each latent has exactly 76 masked tokens.
All inputs are finite; a program needn't handle non-finite values.
Results may differ from a plain program's by a relative error of at most 0.019.
Values may be sent and summed in bfloat16 or wider, within the bound.
No kernel may reach another device: no remote copies, remote signals or barrier semaphores. Data moves between devices by JAX's collectives and lax.ppermute only.
A program may use at most 216 MiB of HBM per device.

v0:
```python
import math

import jax
import jax.numpy as jnp
from jax import lax
from jax.sharding import PartitionSpec as P

D = 384
HEADS = 6
HDIM = 64
FF = 1536
NTOK = 256
PIN = 16
FREQ = 256
CLASSES = 1000
TSTEPS = 1000
STEP = 10
POUT = 32


beta_one = 0.9
beta_two = 0.999
adam_eps = 1e-08
learn_rate = 0.05
weight_decay = 0.1
clip_level = 0.005
ln_eps = 1e-06


def spread(shard, axis, root):
    mine = lax.axis_index(axis) == root
    return lax.psum(jnp.where(mine, shard, jnp.zeros_like(shard)), axis)


def matmul(left_op, right_op):
    return jnp.dot(left_op, right_op, preferred_element_type=jnp.float32)


def cols_dot(left_op, right_op):
    return lax.dot_general(
        left_op, right_op, (((1,), (1,)), ((), ())), preferred_element_type=jnp.float32
    )


def plan():
    t_steps = jnp.arange(TSTEPS).astype(jnp.float32)
    beta_all = 0.0001 + (0.02 - 0.0001) * t_steps / (TSTEPS - 1)
    return (beta_all, jnp.cumprod(1.0 - beta_all))


def position_table():
    half_width = D // 2
    rates_t = jnp.exp(-math.log(10000.0) * 2.0 * jnp.arange(half_width).astype(jnp.float32) / D)
    angles = jnp.arange(NTOK).astype(jnp.float32)[:, None] * rates_t[None, :]
    return jnp.concatenate([jnp.sin(angles), jnp.cos(angles)], axis=1)


def time_features(t_steps):
    half_width = FREQ // 2
    rates_t = jnp.exp(-math.log(10000.0) * jnp.arange(half_width).astype(jnp.float32) / half_width)
    angles = t_steps.astype(jnp.float32)[:, None] * rates_t[None, :]
    return jnp.concatenate([jnp.cos(angles), jnp.sin(angles)], axis=1)


def modulate(hidden, shift_v, scale_v):
    mean_v = jnp.mean(hidden, axis=-1, keepdims=True)
    centred = hidden - mean_v
    var_v = jnp.mean(centred * centred, axis=-1, keepdims=True)
    normed = centred * lax.rsqrt(var_v + ln_eps)
    return normed * (1.0 + scale_v[:, None, :]) + shift_v[:, None, :]


def norm_back(hidden, shift_v, scale_v, grad_in):
    _, norm_pull = jax.vjp(modulate, hidden, shift_v, scale_v)
    return norm_pull(grad_in)


def silu_back(pre_act, grad_in):
    _, act_pull = jax.vjp(jax.nn.silu, pre_act)
    return act_pull(grad_in)[0]


def gelu_fn(pre_act):
    return jax.nn.gelu(pre_act, approximate=True)


def loss_terms(head_out, noise, t_steps, weight, beta_all, abar_all):
    abar_t = abar_all[t_steps][:, None, None]
    abar_prev = abar_all[t_steps - 1][:, None, None]
    beta_t = beta_all[t_steps][:, None, None]
    post_log = jnp.log(beta_t * (1.0 - abar_prev) / (1.0 - abar_t))
    mean_w = abar_prev * beta_t * beta_t / ((1.0 - abar_t) * abar_t)
    eps_diff = head_out[..., :PIN] - noise
    var_frac = (head_out[..., PIN:] + 1.0) / 2.0
    log_var = var_frac * jnp.log(beta_t) + (1.0 - var_frac) * post_log
    kl_term = (
        0.5
        * (
            -1.0
            + log_var
            - post_log
            + jnp.exp(post_log - log_var)
            + mean_w * eps_diff * eps_diff * jnp.exp(-log_var)
        )
        / math.log(2.0)
    )
    per_sample = jnp.sum(eps_diff * eps_diff + kl_term, axis=(1, 2))
    return jnp.sum(per_sample * weight)


def split_weights(gathered):
    tables, row_block, down_block = gathered
    w_patch = tables[:, :PIN]
    mask_token = tables[:, PIN]
    w_tone = tables[:, PIN + 1 : PIN + 1 + FREQ]
    class_tab = tables[:, PIN + 1 + FREQ :]
    w_ttwo = row_block[:, :D]
    col_start = D
    block_list = []
    for block_idx in range(3):
        w_qkv = row_block[:, col_start : col_start + 3 * D]
        w_out = row_block[:, col_start + 3 * D : col_start + 4 * D]
        w_up = row_block[:, col_start + 4 * D : col_start + 4 * D + FF]
        w_ada = row_block[:, col_start + 4 * D + FF : col_start + 10 * D + FF]
        w_down = down_block[:, block_idx * FF : (block_idx + 1) * FF]
        block_list.append((w_qkv, w_out, w_up, w_ada, w_down))
        col_start = col_start + 10 * D + FF
    w_fin = row_block[:, col_start : col_start + 2 * D]
    w_head = row_block[:, col_start + 2 * D : col_start + 2 * D + POUT]
    return (w_patch, mask_token, w_tone, class_tab, w_ttwo, block_list, w_fin, w_head)


def attn_scores(qkv_all, key_bias):
    return (
        jnp.einsum(
            "snhd,smhd->shnm",
            qkv_all[:, :, 0],
            qkv_all[:, :, 1],
            preferred_element_type=jnp.float32,
        )
        / math.sqrt(HDIM)
        + key_bias
    )


def block_forward(hidden, s_cond, block_w, key_bias):
    w_qkv, w_out, w_up, w_ada, w_down = block_w
    samples = hidden.shape[0]
    rows_all = samples * NTOK
    ada_mod = matmul(s_cond, w_ada)
    shift_one, scale_one, gate_one, shift_two, scale_two, gate_two = jnp.split(ada_mod, 6, axis=1)
    n_one = modulate(hidden, shift_one, scale_one).astype(jnp.bfloat16).reshape(rows_all, D)
    qkv_all = matmul(n_one, w_qkv).astype(jnp.bfloat16).reshape(samples, NTOK, 3, HEADS, HDIM)
    scores = attn_scores(qkv_all, key_bias)
    row_top = jnp.max(scores, axis=-1, keepdims=True)
    log_total = row_top + jnp.log(jnp.sum(jnp.exp(scores - row_top), axis=-1, keepdims=True))
    attn_prob = jnp.exp(scores - log_total).astype(jnp.bfloat16)
    attn_out = (
        jnp.einsum(
            "shnm,smhd->snhd", attn_prob, qkv_all[:, :, 2], preferred_element_type=jnp.float32
        )
        .astype(jnp.bfloat16)
        .reshape(rows_all, D)
    )
    attn_res = matmul(attn_out, w_out).reshape(samples, NTOK, D)
    h_two = hidden + gate_one[:, None, :] * attn_res
    n_two = modulate(h_two, shift_two, scale_two).astype(jnp.bfloat16).reshape(rows_all, D)
    up_pre = matmul(n_two, w_up)
    up_act = gelu_fn(up_pre).astype(jnp.bfloat16)
    mlp_out = cols_dot(up_act, w_down).reshape(samples, NTOK, D)
    h_three = h_two + gate_two[:, None, :] * mlp_out
    saved_block = dict(
        hidden=hidden,
        ada_mod=ada_mod,
        n_one=n_one,
        qkv_all=qkv_all,
        log_total=log_total,
        attn_prob=attn_prob,
        attn_out=attn_out,
        attn_res=attn_res,
        h_two=h_two,
        n_two=n_two,
        up_pre=up_pre,
        up_act=up_act,
        mlp_out=mlp_out,
    )
    return (h_three, saved_block)


def block_backward(block_w, saved_block, s_cond, key_bias, d_three):
    w_qkv, w_out, w_up, w_ada, w_down = block_w
    hidden = saved_block["hidden"]
    samples = hidden.shape[0]
    rows_all = samples * NTOK
    shift_one, scale_one, gate_one, shift_two, scale_two, gate_two = jnp.split(
        saved_block["ada_mod"], 6, axis=1
    )
    d_mlp = (d_three * gate_two[:, None, :]).astype(jnp.bfloat16).reshape(rows_all, D)
    d_gate_two = jnp.sum(d_three * saved_block["mlp_out"], axis=1)
    d_act = matmul(d_mlp, w_down)
    _, gelu_pull = jax.vjp(gelu_fn, saved_block["up_pre"])
    d_up = gelu_pull(d_act)[0].astype(jnp.bfloat16)
    d_ntwo = cols_dot(d_up, w_up).reshape(samples, NTOK, D)
    d_two_n, d_shift_two, d_scale_two = norm_back(
        saved_block["h_two"], shift_two, scale_two, d_ntwo
    )
    d_two = d_three + d_two_n
    d_att = (d_two * gate_one[:, None, :]).astype(jnp.bfloat16).reshape(rows_all, D)
    d_gate_one = jnp.sum(d_two * saved_block["attn_res"], axis=1)
    d_attn = cols_dot(d_att, w_out).astype(jnp.bfloat16).reshape(samples, NTOK, HEADS, HDIM)
    qkv_all = saved_block["qkv_all"]
    queries, key_part, value_part = (qkv_all[:, :, 0], qkv_all[:, :, 1], qkv_all[:, :, 2])
    prob_full = jnp.exp(attn_scores(qkv_all, key_bias) - saved_block["log_total"])
    d_prob = jnp.einsum("snhd,smhd->shnm", d_attn, value_part, preferred_element_type=jnp.float32)
    d_scores = (prob_full * (d_prob - jnp.sum(prob_full * d_prob, axis=-1, keepdims=True))).astype(
        jnp.bfloat16
    )
    d_query = jnp.einsum(
        "shnm,smhd->snhd", d_scores, key_part, preferred_element_type=jnp.float32
    ) / math.sqrt(HDIM)
    d_key = jnp.einsum(
        "shnm,snhd->smhd", d_scores, queries, preferred_element_type=jnp.float32
    ) / math.sqrt(HDIM)
    d_value = jnp.einsum(
        "shnm,snhd->smhd", saved_block["attn_prob"], d_attn, preferred_element_type=jnp.float32
    )
    d_qkv = (
        jnp.stack([d_query, d_key, d_value], axis=2).astype(jnp.bfloat16).reshape(rows_all, 3 * D)
    )
    d_none = cols_dot(d_qkv, w_qkv).reshape(samples, NTOK, D)
    d_zero_n, d_shift_one, d_scale_one = norm_back(hidden, shift_one, scale_one, d_none)
    d_hidden = d_two + d_zero_n
    d_mod = jnp.concatenate(
        [d_shift_one, d_scale_one, d_gate_one, d_shift_two, d_scale_two, d_gate_two], axis=1
    ).astype(jnp.bfloat16)
    d_scond = cols_dot(d_mod, w_ada)
    grad_pairs = [
        (saved_block["n_one"], d_qkv),
        (saved_block["attn_out"], d_att),
        (saved_block["n_two"], d_up),
        (s_cond, d_mod),
    ]
    return (d_hidden, d_scond, grad_pairs, (d_mlp, saved_block["up_act"]))


def forward(pieces, x_zero, noise, t_steps, label_ids, mask_ids, weight, consts):
    w_patch, mask_token, w_tone, class_tab, w_ttwo, block_list, w_fin, w_head = pieces
    beta_all, abar_all, pos_table = consts
    samples = x_zero.shape[0]
    rows_all = samples * NTOK
    abar_t = abar_all[t_steps][:, None]
    x_in = (
        (jnp.sqrt(abar_t) * x_zero + jnp.sqrt(1.0 - abar_t) * noise)
        .astype(jnp.bfloat16)
        .reshape(rows_all, PIN)
    )
    h_patch = cols_dot(x_in, w_patch).reshape(samples, NTOK, D)
    mask_f = mask_ids.astype(jnp.float32)[:, :, None]
    key_bias = (-1000000000.0 * mask_ids.astype(jnp.float32))[:, None, None, :]
    h_zero = h_patch + pos_table[None]
    t_feat = time_features(t_steps).astype(jnp.bfloat16)
    a_pre = cols_dot(t_feat, w_tone)
    a_act = jax.nn.silu(a_pre).astype(jnp.bfloat16)
    label_hot = (label_ids[:, None] == jnp.arange(CLASSES)[None, :]).astype(jnp.float32)
    cond_vec = matmul(a_act, w_ttwo) + cols_dot(label_hot.astype(jnp.bfloat16), class_tab)
    s_cond = jax.nn.silu(cond_vec).astype(jnp.bfloat16)
    fin_mod = matmul(s_cond, w_fin)
    h_enc, saved_enc = block_forward(h_zero, s_cond, block_list[0], key_bias)
    h_side_in = h_enc * (1.0 - mask_f) + mask_f * (
        mask_token.astype(jnp.float32)[None, None, :] + pos_table[None]
    )
    h_side, saved_side = block_forward(h_side_in, s_cond, block_list[1], 0.0)
    h_dec, saved_dec = block_forward(h_side, s_cond, block_list[2], 0.0)
    shift_fin, scale_fin = jnp.split(fin_mod, 2, axis=1)
    n_fin = modulate(h_dec, shift_fin, scale_fin).astype(jnp.bfloat16).reshape(rows_all, D)
    head_out = matmul(n_fin, w_head).reshape(samples, NTOK, POUT)
    noise_tok = noise.reshape(samples, NTOK, PIN)
    loss_part, loss_pull = jax.vjp(
        lambda head_val: loss_terms(head_val, noise_tok, t_steps, weight, beta_all, abar_all),
        head_out,
    )
    d_out = loss_pull(jnp.ones((), jnp.float32))[0]
    saved_acts = dict(
        x_in=x_in,
        mask_f=mask_f,
        key_bias=key_bias,
        t_feat=t_feat,
        a_pre=a_pre,
        a_act=a_act,
        label_hot=label_hot,
        cond_vec=cond_vec,
        s_cond=s_cond,
        fin_mod=fin_mod,
        h_dec=h_dec,
        n_fin=n_fin,
        d_out=d_out,
        saved_enc=saved_enc,
        saved_side=saved_side,
        saved_dec=saved_dec,
    )
    return (loss_part, saved_acts)


def backward(pieces, saved_acts):
    w_patch, mask_token, w_tone, class_tab, w_ttwo, block_list, w_fin, w_head = pieces
    h_dec = saved_acts["h_dec"]
    samples = h_dec.shape[0]
    rows_all = samples * NTOK
    s_cond = saved_acts["s_cond"]
    mask_f = saved_acts["mask_f"]
    shift_fin, scale_fin = jnp.split(saved_acts["fin_mod"], 2, axis=1)
    d_out = saved_acts["d_out"].reshape(rows_all, POUT).astype(jnp.bfloat16)
    d_fin = cols_dot(d_out, w_head).reshape(samples, NTOK, D)
    d_dec, d_shift_fin, d_scale_fin = norm_back(h_dec, shift_fin, scale_fin, d_fin)
    d_side, cond_dec, pairs_dec, down_dec = block_backward(
        block_list[2], saved_acts["saved_dec"], s_cond, 0.0, d_dec
    )
    d_side_in, cond_side, pairs_side, down_side = block_backward(
        block_list[1], saved_acts["saved_side"], s_cond, 0.0, d_side
    )
    d_enc = d_side_in * (1.0 - mask_f)
    d_zero, cond_enc, pairs_enc, down_enc = block_backward(
        block_list[0], saved_acts["saved_enc"], s_cond, saved_acts["key_bias"], d_enc
    )
    d_fmod = jnp.concatenate([d_shift_fin, d_scale_fin], axis=1).astype(jnp.bfloat16)
    d_scond = cond_enc + cond_side + cond_dec + cols_dot(d_fmod, w_fin)
    d_cond = silu_back(saved_acts["cond_vec"], d_scond)
    d_cond_b = d_cond.astype(jnp.bfloat16)
    d_apre = silu_back(saved_acts["a_pre"], cols_dot(d_cond_b, w_ttwo)).astype(jnp.bfloat16)
    d_patch = d_zero.astype(jnp.bfloat16).reshape(rows_all, D)
    table_pairs = [
        (d_patch, saved_acts["x_in"]),
        (d_side_in.reshape(rows_all, D), mask_f.reshape(rows_all, 1)),
        (d_apre, saved_acts["t_feat"]),
        (d_cond, saved_acts["label_hot"]),
    ]
    row_pairs = (
        [(saved_acts["a_act"], d_cond_b)]
        + pairs_enc
        + pairs_side
        + pairs_dec
        + [(s_cond, d_fmod), (saved_acts["n_fin"], d_out)]
    )
    return table_pairs + row_pairs + [down_enc, down_side, down_dec]


def grad_term(pair_lists, count):
    summed_term = None
    for grad_pairs in pair_lists:
        columns = []
        for left_op, right_op in grad_pairs:
            row_slice = lax.slice_in_dim(left_op, 0, count, axis=1)
            precise_mode = lax.Precision.HIGHEST if left_op.dtype == jnp.float32 else None
            columns.append(
                lax.dot_general(
                    row_slice,
                    right_op,
                    (((0,), (0,)), ((), ())),
                    preferred_element_type=jnp.float32,
                    precision=precise_mode,
                )
            )
        term_block = jnp.concatenate(columns, axis=1)
        summed_term = term_block if summed_term is None else summed_term + term_block
    return summed_term


def adam_step(master, first_m, second, grad_in):
    first_new = beta_one * first_m + (1.0 - beta_one) * grad_in
    second_new = beta_two * second + (1.0 - beta_two) * grad_in * grad_in
    first_hat = first_new / (1.0 - beta_one**STEP)
    second_hat = second_new / (1.0 - beta_two**STEP)
    master_new = master - learn_rate * (
        first_hat / (jnp.sqrt(second_hat) + adam_eps) + weight_decay * master
    )
    return jnp.stack([master_new, first_new, second_new])


def update_group(master, first_m, second, grad_in, owner_idx, split_cols):
    is_owner = lax.axis_index("dp") == owner_idx
    updated = lax.cond(
        is_owner,
        lambda: adam_step(master, first_m, second, grad_in),
        lambda: jnp.zeros((3,) + master.shape, jnp.float32),
    )
    updated = spread(updated.astype(jnp.bfloat16), "dp", owner_idx).astype(updated.dtype)
    if split_cols:
        col_width = master.shape[1] // lax.axis_size("dp")
        col_start = lax.axis_index("dp") * col_width
        updated = lax.dynamic_slice_in_dim(updated, col_start, col_width, 2)
    return [updated[0], updated[1], updated[2]]


def on_device(
    latents,
    noise,
    timesteps,
    labels,
    patch_mask,
    counts,
    owners,
    tables_w,
    tables_m,
    tables_v,
    rows_w,
    rows_m,
    rows_v,
    down_w,
    down_m,
    down_v,
):
    beta_all, abar_all = plan()
    consts = (beta_all, abar_all, position_table())
    micro_count, slot_count = (latents.shape[0], latents.shape[1])
    count_total = lax.psum(jnp.sum(counts.astype(jnp.float32)), ("dp", "fsdp"))
    valid_slot = (jnp.arange(slot_count)[None, :] < counts).astype(jnp.float32)
    weight = valid_slot / (count_total * NTOK * PIN)
    masters = (
        tables_w.astype(jnp.bfloat16),
        rows_w.astype(jnp.bfloat16),
        down_w.astype(jnp.bfloat16),
    )
    full_rows = D
    pair_lists = []
    grad_acc = None
    loss_local = jnp.zeros((), jnp.float32)
    for micro_idx in range(micro_count):
        forward_w = split_weights(
            (
                lax.all_gather(masters[0], "fsdp", axis=0, tiled=True),
                lax.all_gather(masters[1], "fsdp", axis=0, tiled=True),
                lax.all_gather(masters[2], "fsdp", axis=0, tiled=True),
            )
        )
        loss_part, saved_acts = forward(
            forward_w,
            latents[micro_idx],
            noise[micro_idx],
            timesteps[micro_idx],
            labels[micro_idx],
            patch_mask[micro_idx],
            weight[micro_idx],
            consts,
        )
        loss_local = loss_local + loss_part
        fenced = lax.optimization_barrier((masters, saved_acts["d_out"]))[0]
        back_w = split_weights(
            (
                lax.all_gather(fenced[0], "fsdp", axis=0, tiled=True),
                lax.all_gather(fenced[1], "fsdp", axis=0, tiled=True),
                lax.all_gather(fenced[2], "fsdp", axis=0, tiled=True),
            )
        )
        grad_pairs = backward(back_w, saved_acts)
        pair_lists.append(grad_pairs)
    grad_acc = lax.psum_scatter(
        grad_term(pair_lists, full_rows), "fsdp", scatter_dimension=0, tiled=True
    )
    tab_cols = tables_w.shape[1]
    row_cols = rows_w.shape[1]
    shards = (
        grad_acc[:, :tab_cols],
        grad_acc[:, tab_cols : tab_cols + row_cols],
        grad_acc[:, tab_cols + row_cols :],
    )
    summed = (
        lax.psum(shards[0].astype(jnp.bfloat16), "dp").astype(jnp.float32),
        lax.psum(shards[1].astype(jnp.bfloat16), "dp").astype(jnp.float32),
        lax.psum(shards[2].astype(jnp.bfloat16), "dp").astype(jnp.float32),
        lax.psum(loss_local.astype(jnp.bfloat16), "dp").astype(jnp.float32),
    )
    squares = (
        jnp.sum(summed[0] * summed[0])
        + jnp.sum(summed[1] * summed[1])
        + jnp.sum(summed[2] * summed[2])
    )
    norm_sq, loss_sum = lax.psum((squares, summed[3]), "fsdp")
    grad_norm = jnp.sqrt(norm_sq)
    factor = jnp.minimum(1.0, clip_level / (grad_norm + 1e-06))
    results = update_group(tables_w, tables_m, tables_v, factor * summed[0], owners[0], False)
    results = results + update_group(rows_w, rows_m, rows_v, factor * summed[1], owners[1], True)
    results = results + update_group(down_w, down_m, down_v, factor * summed[2], owners[2], True)
    return tuple([loss_sum, grad_norm] + results)


def solution(mesh):
    return jax.shard_map(
        on_device,
        mesh=mesh,
        in_specs=(
            P(None, ("dp", "fsdp"), None),
            P(None, ("dp", "fsdp"), None),
            P(None, ("dp", "fsdp")),
            P(None, ("dp", "fsdp")),
            P(None, ("dp", "fsdp"), None),
            P(None, ("dp", "fsdp")),
            P(),
            P("fsdp", None),
            P("fsdp", None),
            P("fsdp", None),
            P("fsdp", None),
            P("fsdp", None),
            P("fsdp", None),
            P("fsdp", None),
            P("fsdp", None),
            P("fsdp", None),
        ),
        out_specs=(
            P(),
            P(),
            P("fsdp", None),
            P("fsdp", None),
            P("fsdp", None),
            P("fsdp", "dp"),
            P("fsdp", "dp"),
            P("fsdp", "dp"),
            P("fsdp", "dp"),
            P("fsdp", "dp"),
            P("fsdp", "dp"),
        ),
        check_vma=False,
    )
```

profile of v0, /device:TPU:0, one launch (start us, length us, event | category | flops | bytes accessed | tf_op | source)
XLA Modules:
  0.0 1531.5 jit_solution(15802900337246665107)
XLA Ops:
  14.0 22.8 %all_gather.24 = bf16[384,1273]{1,0:T(8,128)(2,1)S(1)} all-gather(bf16[48,1273]{1,0:T(8,128)(2,1)S(1)} %convert_element_type.581), channel_id=1, replica_groups=mesh['dp'=4,'fsdp'=8] {'fsdp'}, dimensions={0}, use_global_device_ids=true | all-gather | bytes 1099872 | tf_op jit(solution)/shard_map/all_gather | solution.py:430
  41.8 46.3 %psum.70 = f32[]{:T(128)} all-reduce(f32[]{:T(128)} %convert_reduce_fusion.3), channel_id=1, replica_groups=mesh['dp'=4,'fsdp'=8] {'dp','fsdp'}, use_global_device_ids=true, to_apply=%region_24.25 | all-reduce | flops 1 | bytes 8 | tf_op jit(solution)/shard_map/psum | solution.py:415
  103.5 37.2 %all-gather.5.cloned.1.call-done = bf16[384,17312]{1,0:T(8,128)(2,1)} async-done(((bf16[48,17312]{1,0:T(8,128)(2,1)}), bf16[384,17312]{1,0:T(8,128)(2,1)}) %all-gather.5.cloned.1.call-update) | async-done | bytes 13295632 | tf_op jit(solution)/shard_map/all_gather | solution.py:431
  152.8 4.5 reshape.1374
  157.3 5.0 fusion.395
  183.8 6.4 reshape.1371
  190.2 5.6 fusion.392
  211.1 5.0 fusion.142
  216.1 4.9 fusion.144
  239.4 6.4 reshape.1375
  245.8 5.0 fusion.394
  284.7 6.4 reshape.1376
  291.0 4.8 fusion.393
  340.6 7.7 all-gather.11.cloned.1.call-done
  348.4 6.9 fusion.47
  393.7 5.3 fusion.40
  442.0 5.2 fusion.33
  499.4 6.4 reshape.1372
  505.8 4.9 fusion.391
  542.9 6.4 reshape.1373
  549.3 4.8 fusion.390
  589.3 5.2 fusion.26
  636.1 5.5 fusion.19
  676.9 5.4 fusion.12
  772.2 47.8 %concatenate.65 = f32[384,23193]{1,0:T(8,128)} concatenate(f32[384,16]{1,0:T(8,128)} %fusion.421, f32[384,1]{1,0:T(8,128)} %dot_general.663, f32[384,256]{1,0:T(8,128)} %fusion.297, f32[384,1000]{1,0:T(8,128)} %fusion.278, f32[384,384]{1,0:T(8,128)} %fusion.332, f32[384,1152]{1,0:T(8,128)} %fusion.422, f32[384,384]{1,0:T(8,128)} %fusion.423, f32[384,1536]{1,0:T(8,128)} %fusion.424, ...), dimensions={1} | concatenate | bytes 71248896 | tf_op jit(solution)/shard_map/concatenate | solution.py:363
  822.2 46.6 %concatenate.60 = f32[384,23193]{1,0:T(8,128)} concatenate(f32[384,16]{1,0:T(8,128)} %fusion.408, f32[384,1]{1,0:T(8,128)} %dot_general.662, f32[384,256]{1,0:T(8,128)} %fusion.304, f32[384,1000]{1,0:T(8,128)} %fusion.279, f32[384,384]{1,0:T(8,128)} %fusion.336, f32[384,1152]{1,0:T(8,128)} %fusion.409, f32[384,384]{1,0:T(8,128)} %fusion.410, f32[384,1536]{1,0:T(8,128)} %fusion.411, ...), dimensions={1} | concatenate | bytes 71248896 | tf_op jit(solution)/shard_map/concatenate | solution.py:363
  868.8 35.4 %add.975 = f32[384,23193]{1,0:T(8,128)} add(f32[384,23193]{1,0:T(8,128)} %concatenate.60, f32[384,23193]{1,0:T(8,128)} %concatenate.65) | non-fusion elementwise | flops 8906112 | bytes 106873344 | tf_op jit(solution)/shard_map/add | solution.py:364
  904.3 346.5 %reduce-scatter.2.cloned.1.call-done = f32[48,23193]{1,0:T(8,128)} async-done(((f32[384,23193]{1,0:T(8,128)}), f32[48,23193]{1,0:T(8,128)}) %reduce-scatter.2.cloned.1.call-update) | async-done | bytes 4453072 | tf_op jit(solution)/shard_map/reduce_scatter | solution.py:456
  1261.2 10.6 psum.71
  1271.8 56.1 %all-reduce.13.cloned.1.call-done = (bf16[48,1273]{1,0:T(8,128)(2,1)}, bf16[48,17312]{1,0:T(8,128)(2,1)}, bf16[48,4608]{1,0:T(8,128)(2,1)}) async-done(((bf16[48,1273]{1,0:T(8,128)(2,1)}, bf16[48,17312]{1,0:T(8,128)(2,1)}, bf16[48,4608]{1,0:T(8,128)(2,1)}), (bf16[48,1273]{1,0:T(8,128)(2,1)}, bf16[48,17312]{1,0:T(8,128)(2,1)}, bf16[48,4608]{1,0:T(8,128)(2,1)})) %all-reduce.13.cloned.1.call-update) | async-done | bytes 2226544 | tf_op jit(solution)/shard_map/psum | solution.py:467
  1338.7 17.2 %all-reduce.5 = (f32[]{:T(128)}, f32[]{:T(128)}) all-reduce(bf16[]{:T(256)} %psum.71, f32[]{:T(128)S(6)} %add.977), channel_id=1, replica_groups=mesh['dp'=4,'fsdp'=8] {'fsdp'}, use_global_device_ids=true, to_apply=%region_49.50 | all-reduce | flops 2 | bytes 14 | tf_op jit(solution)/shard_map/psum | solution.py:477
  1369.5 147.9 %all-reduce.11.cloned.1.call-done = (bf16[3,48,1273]{2,1,0:T(8,128)(2,1)}, bf16[3,48,17312]{2,1,0:T(8,128)(2,1)}, bf16[3,48,4608]{2,1,0:T(8,128)(2,1)}) async-done(((bf16[3,48,1273]{2,1,0:T(8,128)(2,1)}, bf16[3,48,17312]{2,1,0:T(8,128)(2,1)}, bf16[3,48,4608]{2,1,0:T(8,128)(2,1)}), (bf16[3,48,1273]{2,1,0:T(8,128)(2,1)}, bf16[3,48,17312]{2,1,0:T(8,128)(2,1)}, ...) | async-done | bytes 6679600 | tf_op jit(solution)/shard_map/psum | solution.py:32
  (1330 shorter events, 579.2 us)
Async XLA Ops:
  7.2 133.5 %all-gather.5.cloned.1.call-start = ((), (), s32[]{:S(2)}) async-start(), calls=%async_computation.1 | async-start | bytes 15040512 | tf_op jit(solution)/shard_map/all_gather | solution.py:431
  10.6 210.4 %all-gather.7.cloned.1.call-start = ((), (), s32[]{:S(2)}) async-start(), calls=%async_computation.2 | async-start | bytes 3981312 | tf_op jit(solution)/shard_map/all_gather | solution.py:432
  12.6 316.6 %all-gather.9.cloned.1.call-start = ((), (), s32[]{:S(2)}) async-start(), calls=%async_computation.3 | async-start | bytes 15040512 | tf_op jit(solution)/shard_map/all_gather | solution.py:450
  13.3 335.0 %all-gather.11.cloned.1.call-start = ((), (), s32[]{:S(2)}) async-start(), calls=%async_computation.4 | async-start | bytes 3981312 | tf_op jit(solution)/shard_map/all_gather | solution.py:451
  13.9 1236.9 %reduce-scatter.2.cloned.1.call-start = ((), (), s32[]{:S(2)}) async-start(), calls=%async_computation.5 | async-start | bytes 40255488 | tf_op jit(solution)/shard_map/reduce_scatter | solution.py:456
  14.0 76.8 %copy-start.168 = (f32[2,3,4096]{2,0,1:T(2,128)S(1)}, f32[2,3,4096]{2,0,1:T(2,128)}, u32[]{:S(2)}) copy-start(f32[2,3,4096]{2,0,1:T(2,128)} %param.23) | copy-start | bytes 294916
  36.8 57.7 %copy-start.132 = (bf16[384,1273]{1,0:T(8,128)(2,1)}, bf16[384,1273]{1,0:T(8,128)(2,1)S(1)}, u32[]{:S(2)}) copy-start(bf16[384,1273]{1,0:T(8,128)(2,1)S(1)} %all_gather.24) | copy-start | bytes 2932996
  38.0 53.3 %copy-start.169 = (f32[2,3,4096]{2,0,1:T(2,128)S(1)}, f32[2,3,4096]{2,0,1:T(2,128)}, u32[]{:S(2)}) copy-start(f32[2,3,4096]{2,0,1:T(2,128)} %param.22) | copy-start | bytes 294916
  39.9 54.5 %copy-start.278 = (f32[1,3,256]{2,0,1:T(1,128)}, f32[1,3,256]{2,0,1:T(1,128)S(1)}, u32[]{:S(2)}) copy-start(f32[1,3,256]{2,0,1:T(1,128)S(1)} %get-tuple-element.285) | copy-start | bytes 9220
  40.6 131.6 %copy-start.175 = (f32[3,256]{1,0:T(4,128)}, f32[3,256]{1,0:T(4,128)S(1)}, u32[]{:S(2)}) copy-start(f32[3,256]{1,0:T(4,128)S(1)} %get-tuple-element.290) | copy-start | bytes 9220
  40.6 162.8 %copy-start.173 = (f32[3,256]{1,0:T(4,128)}, f32[3,256]{1,0:T(4,128)S(1)}, u32[]{:S(2)}) copy-start(f32[3,256]{1,0:T(4,128)S(1)} %get-tuple-element.388) | copy-start | bytes 9220
  40.6 188.2 %copy-start.203 = (f32[3,256]{1,0:T(4,128)}, f32[3,256]{1,0:T(4,128)S(1)}, u32[]{:S(2)}) copy-start(f32[3,256]{1,0:T(4,128)S(1)} %get-tuple-element.387) | copy-start | bytes 9220
  40.6 188.2 %copy-start.205 = (f32[3,256]{1,0:T(4,128)}, f32[3,256]{1,0:T(4,128)S(1)}, u32[]{:S(2)}) copy-start(f32[3,256]{1,0:T(4,128)S(1)} %get-tuple-element.291) | copy-start | bytes 9220
  95.0 54.3 %copy-start.16 = (f32[3,256,384]{2,1,0:T(8,128)}, f32[3,256,384]{2,1,0:T(8,128)S(1)}, u32[]{:S(2)}) copy-start(f32[3,256,384]{2,1,0:T(8,128)S(1)} %get-tuple-element.341) | copy-start | bytes 3538948
  95.0 54.3 %copy-start.195 = (f32[3,256]{1,0:T(4,128)}, f32[3,256]{1,0:T(4,128)S(1)}, u32[]{:S(2)}) copy-start(f32[3,256]{1,0:T(4,128)S(1)} %broadcast_multiply_fusion.8) | copy-start | bytes 9220
  95.4 54.0 %copy-start.233 = (f32[3,256]{1,0:T(4,128)}, f32[3,256]{1,0:T(4,128)S(1)}, u32[]{:S(2)}) copy-start(f32[3,256]{1,0:T(4,128)S(1)} %fusion.317) | copy-start | bytes 9220
  95.4 46.4 %copy-start.366 = (s32[3]{0:T(128)}, s32[3]{0:T(128)S(1)}, u32[]{:S(2)}) copy-start(s32[3]{0:T(128)S(1)} %get-tuple-element.303) | copy-start | bytes 40
  95.4 48.5 %copy-start.361 = (s32[3]{0:T(128)}, s32[3]{0:T(128)S(1)}, u32[]{:S(2)}) copy-start(s32[3]{0:T(128)S(1)} %get-tuple-element.302) | copy-start | bytes 40
  99.2 80.0 %copy-start.13 = (f32[3,256,384]{2,1,0:T(8,128)}, f32[3,256,384]{2,1,0:T(8,128)S(1)}, u32[]{:S(2)}) copy-start(f32[3,256,384]{2,1,0:T(8,128)S(1)} %get-tuple-element.334) | copy-start | bytes 3538948
  99.2 80.0 %copy-start.193 = (f32[3,256]{1,0:T(4,128)}, f32[3,256]{1,0:T(4,128)S(1)}, u32[]{:S(2)}) copy-start(f32[3,256]{1,0:T(4,128)S(1)} %broadcast_multiply_fusion.15) | copy-start | bytes 9220
  99.6 79.6 %copy-start.231 = (f32[3,256]{1,0:T(4,128)}, f32[3,256]{1,0:T(4,128)S(1)}, u32[]{:S(2)}) copy-start(f32[3,256]{1,0:T(4,128)S(1)} %fusion.310) | copy-start | bytes 9220
  102.0 44.8 %copy-start.344 = (bf16[3,128]{1,0:T(4,128)(2,1)}, bf16[3,128]{1,0:T(4,128)(2,1)S(1)}, u32[]{:S(2)}) copy-start(bf16[3,128]{1,0:T(4,128)(2,1)S(1)} %get-tuple-element.304) | copy-start | bytes 2308
  102.0 44.8 %copy-start.345 = (bf16[3,128]{1,0:T(4,128)(2,1)}, bf16[3,128]{1,0:T(4,128)(2,1)S(1)}, u32[]{:S(2)}) copy-start(bf16[3,128]{1,0:T(4,128)(2,1)S(1)} %get-tuple-element.305) | copy-start | bytes 2308
  103.5 43.3 %copy-start.253 = (f32[3,384]{1,0:T(4,128)}, f32[3,384]{1,0:T(4,128)S(1)}, u32[]{:S(2)}) copy-start(f32[3,384]{1,0:T(4,128)S(1)} %fusion.244) | copy-start | bytes 13828
  149.3 57.9 %copy-start.268 = (f32[3,384]{1,0:T(4,128)}, f32[3,384]{1,0:T(4,128)S(1)}, u32[]{:S(2)}) copy-start(f32[3,384]{1,0:T(4,128)S(1)} %get-tuple-element.261) | copy-start | bytes 13828
  149.3 61.1 %copy-start.187 = (f32[3,384]{1,0:T(4,128)}, f32[3,384]{1,0:T(4,128)S(1)}, u32[]{:S(2)}) copy-start(f32[3,384]{1,0:T(4,128)S(1)} %get-tuple-element.392) | copy-start | bytes 13828
  149.3 61.4 %copy-start.185 = (f32[3,384]{1,0:T(4,128)}, f32[3,384]{1,0:T(4,128)S(1)}, u32[]{:S(2)}) copy-start(f32[3,384]{1,0:T(4,128)S(1)} %get-tuple-element.258) | copy-start | bytes 13828
  149.3 79.5 %copy-start.258 = (f32[3,384]{1,0:T(4,128)}, f32[3,384]{1,0:T(4,128)S(1)}, u32[]{:S(2)}) copy-start(f32[3,384]{1,0:T(4,128)S(1)} %get-tuple-element.256) | copy-start | bytes 13828
  149.3 79.5 %copy-start.260 = (f32[3,384]{1,0:T(4,128)}, f32[3,384]{1,0:T(4,128)S(1)}, u32[]{:S(2)}) copy-start(f32[3,384]{1,0:T(4,128)S(1)} %get-tuple-element.394) | copy-start | bytes 13828
  772.2 50.0 %copy-start.34 = (f32[384,2304]{1,0:T(8,128)S(1)}, f32[384,2304]{1,0:T(8,128)}, u32[]{:S(2)}) copy-start(f32[384,2304]{1,0:T(8,128)} %fusion.412) | copy-start | bytes 10616836
  904.2 423.7 %all-reduce.13.cloned.1.call-start = ((), (), s32[]{:S(2)}) async-start(), calls=%async_computation.7 | async-start | bytes 4472832 | tf_op jit(solution)/shard_map/psum | solution.py:467
  1256.7 260.7 %all-reduce.11.cloned.1.call-start = ((), (), s32[]{:S(2)}) async-start(), calls=%async_computation.6 | async-start | bytes 13418496 | tf_op jit(solution)/shard_map/psum | solution.py:32
  (380 other events, 1402.6 us)
Sparse Core Ops, SparseCore 0:
  10.7 129.9 all-gather.4
  142.3 40.9 all-gather.6
  185.0 122.0 all-gather.8
  308.6 39.7 all-gather.10
  904.3 346.4 reduce-scatter.1
  1256.8 71.1 all-reduce.12
  1369.6 147.6 all-reduce.10
where the time goes:
time: 1550 us; the launch traced here: 1530 us
  waiting for transfers between devices  597 us (39%)
  matrix products  351 us (23%)
  local copies, waits for them, and re-layouts  328 us (21%)
  other arithmetic  131 us (8%)
  blocking collectives  96.9 us (6%)
  between operations  27.4 us (2%)
    reduce_scatter x1, waiting for transfers between devices, on_device(): lax.psum_scatter(grad_term(pair_lists, full_rows), 'fsdp', scatter_dimens...  347 us
    psum x1, waiting for transfers between devices, spread(): return lax.psum(jnp.where(mine, shard, jnp.zeros_like(shard)), axis)  148 us
    dot_general x36, matrix products, matmul(): return jnp.dot(left_op, right_op, preferred_element_type=jnp.float32)  109 us
    unnamed x872, local copies, waits for them, and re-layouts  100 us
    concatenate x2, local copies, waits for them, and re-layouts, grad_term(): term_block = jnp.concatenate(columns, axis=1)  94.4 us
    dot_general x44, matrix products, grad_term(): lax.dot_general(row_slice, right_op, (((0,), (0,)), ((), ())), preferred_...  91.6 us
    dot_general x40, matrix products, cols_dot(): lax.dot_general(left_op, right_op, (((1,), (1,)), ((), ())), preferred_el...  79.8 us
    psum x1, waiting for transfers between devices, on_device(): lax.psum(shards[0].astype(jnp.bfloat16), 'dp').astype(jnp.float32)  56.1 us
  transfers between devices with their start and end apart: 7, of which 5 were waited for; matrix products, arithmetic and copies ran while one was open for 13% of the time, Pallas kernels for 0%

commit v1 on v0

v1 whole, which is shorter than its diff:
```python
import functools
import math

import jax
import jax.numpy as jnp
import numpy as np
from jax import lax
from jax.experimental import pallas as pl
from jax.experimental.pallas import tpu as pltpu
from jax.sharding import PartitionSpec as P

D = 384
HEADS = 6
HDIM = 64
FF = 1536
NTOK = 256
PIN = 16
FREQ = 256
CLASSES = 1000
TSTEPS = 1000
STEP = 10
POUT = 32

beta_one = 0.9
beta_two = 0.999
adam_eps = 1e-08
learn_rate = 0.05
weight_decay = 0.1
clip_level = 0.005
ln_eps = 1e-06

F32 = jnp.float32
BF16 = jnp.bfloat16
STRIDE = 10 * D + FF
TOKW = 3 * D + D + FF + FF
CHUNKS = 4
CW = TOKW // CHUNKS
GELU_C = math.sqrt(2.0 / math.pi)
VMEM_LIMIT = 60 * 1024 * 1024


def plan_table():
    j = np.arange(TSTEPS, dtype=np.float64)
    beta = 0.0001 + (0.02 - 0.0001) * j / (TSTEPS - 1)
    abar = np.cumprod(1.0 - beta)
    prev = np.concatenate([[1.0], abar[:-1]])
    out = np.zeros((TSTEPS, 8), np.float64)
    out[:, 0] = np.sqrt(abar)
    out[:, 1] = np.sqrt(1.0 - abar)
    out[1:, 2] = np.log(beta[1:])
    out[1:, 3] = np.log(beta[1:] * (1.0 - prev[1:]) / (1.0 - abar[1:]))
    out[1:, 4] = prev[1:] * beta[1:] ** 2 / ((1.0 - abar[1:]) * abar[1:])
    return out.astype(np.float32)


def position_table():
    half = D // 2
    rates = np.exp(-math.log(10000.0) * 2.0 * np.arange(half) / D)
    angles = np.arange(NTOK)[:, None] * rates[None, :]
    return np.concatenate([np.sin(angles), np.cos(angles)], axis=1).astype(np.float32)


def time_features(steps):
    half = FREQ // 2
    rates = jnp.exp(-math.log(10000.0) * jnp.arange(half).astype(F32) / half)
    angles = steps.astype(F32)[:, None] * rates[None, :]
    return jnp.concatenate([jnp.cos(angles), jnp.sin(angles)], axis=1)


def stages(size, pair_first):
    out, stride = [], 1
    if pair_first and size % 2 == 0:
        out.append((1, 2))
        stride, size = 2, size // 2
    while size > 1:
        step = 4 if size % 4 == 0 else 2
        out.append((stride, step))
        stride, size = stride * step, size // step
    return out


def axis_stages(axis):
    return stages(lax.axis_size(axis), axis == "fsdp")


def swap(val, axis, mask):
    size = lax.axis_size(axis)
    return lax.ppermute(val, axis, [(i, i ^ mask) for i in range(size)])


def place(axis, stride, size):
    return (lax.axis_index(axis) // stride) % size


def in_order(parts, pos):
    size = len(parts)
    return jnp.stack([lax.select_n(pos, *[parts[j ^ p] for p in range(size)]) if size > 2 else lax.select(pos == 1, parts[j ^ 1], parts[j]) for j in range(size)])


def gather(val, axis):
    plan = axis_stages(axis)
    shape = val.shape
    for stride, size in reversed(plan):
        parts = [val] + [swap(val, axis, k * stride) for k in range(1, size)]
        val = in_order(parts, place(axis, stride, size))
    n = len(plan)
    order = tuple(reversed(range(n))) + tuple(range(n, n + len(shape)))
    return val.transpose(order).reshape((lax.axis_size(axis),) + shape)


def reduce_parts(val, axis, send_type):
    plan = axis_stages(axis)
    sizes = [s for _, s in reversed(plan)]
    val = val.reshape(tuple(sizes) + val.shape[1:])
    dim = len(sizes)
    for stride, size in plan:
        dim -= 1
        pos = place(axis, stride, size)
        total = lax.dynamic_index_in_dim(val, pos, dim, keepdims=False).astype(F32)
        for k in range(1, size):
            piece = lax.dynamic_index_in_dim(val, pos ^ k, dim, keepdims=False)
            total = total + swap(piece.astype(send_type), axis, k * stride).astype(F32)
        val = total
    return val


def sum_all(val):
    for axis in ("fsdp", "dp"):
        for stride, size in axis_stages(axis):
            parts = [val] + [swap(val, axis, k * stride) for k in range(1, size)]
            while len(parts) > 1:
                parts = [parts[i] + parts[i + 1] for i in range(0, len(parts), 2)]
            val = parts[0]
    return val


def gather_block(chunk, whole):
    rows = chunk.shape[0]
    if rows % 16 or lax.axis_size("dp") != CHUNKS or lax.axis_size("fsdp") != 8:
        full = lax.all_gather(whole, "fsdp", axis=0, tiled=True)
        full = full.reshape(D, CHUNKS, CW).transpose(1, 0, 2)
        return [full.reshape(CHUNKS, 4, 2, D // 8, CW)]
    parts = [chunk] + [swap(chunk, "fsdp", 2 * k) for k in (1, 2, 3)]
    mine = in_order(parts, place("fsdp", 2, 4))
    mine = [mine] + [swap(mine, "dp", k) for k in (1, 2, 3)]
    other = [swap(v, "fsdp", 1) for v in mine]
    return mine + other


def dot(a, b):
    return jnp.dot(a, b, preferred_element_type=F32)


def dot_nt(a, b):
    return lax.dot_general(a, b, (((1,), (1,)), ((), ())), preferred_element_type=F32)


def dot_tn(a, b):
    return lax.dot_general(a, b, (((0,), (0,)), ((), ())), preferred_element_type=F32)


def layer_norm(v):
    c = v - jnp.mean(v, axis=-1, keepdims=True)
    r = lax.rsqrt(jnp.mean(c * c, axis=-1, keepdims=True) + ln_eps)
    return c * r, r


def norm_grad(dm, y, r, scale):
    dy = dm * (1.0 + scale)
    dv = r * (dy - jnp.mean(dy, axis=-1, keepdims=True) - y * jnp.mean(dy * y, axis=-1, keepdims=True))
    return dv, jnp.sum(dm, axis=0, keepdims=True), jnp.sum(dm * y, axis=0, keepdims=True)


def wpart(w, j, lo, hi):
    return w[j, :, :, :, lo:hi].reshape(D, hi - lo)


def head_masks():
    lane = lax.broadcasted_iota(jnp.int32, (1, 2 * HDIM), 1)
    low = (lane < HDIM).astype(F32)
    return low, 1.0 - low


def block_forward(h, mod, w, bias, sv):
    qkv_ref, p_ref, o_ref, g_ref, gp_ref, att_ref, mlp_ref, h2_ref = sv
    y1, _ = layer_norm(h)
    n1 = (y1 * (1.0 + mod(1)) + mod(0)).astype(BF16)
    qkv_ref[...] = dot(n1, wpart(w, 0, 0, CW)).astype(BF16)
    masks = head_masks()
    for j in range(3):
        q2 = qkv_ref[:, 128 * j : 128 * j + 128]
        k2 = qkv_ref[:, D + 128 * j : D + 128 * j + 128]
        v2 = qkv_ref[:, 2 * D + 128 * j : 2 * D + 128 * j + 128]
        o2 = None
        for a in range(2):
            s = dot_nt(q2, k2 * (masks[a] * 0.125).astype(BF16))
            if bias is not None:
                s = s + bias
            e = jnp.exp(s - jnp.max(s, axis=-1, keepdims=True))
            p = (e * (1.0 / jnp.sum(e, axis=-1, keepdims=True))).astype(BF16)
            p_ref[2 * j + a] = p
            part = dot(p, v2 * masks[a].astype(BF16))
            o2 = part if o2 is None else o2 + part
        o_ref[:, 128 * j : 128 * j + 128] = o2.astype(BF16)
    att = dot(o_ref[...], wpart(w, 1, 0, D))
    att_ref[...] = att.astype(BF16)
    h2 = h + mod(2) * att
    h2_ref[...] = h2
    y2, _ = layer_norm(h2)
    n2 = (y2 * (1.0 + mod(4)) + mod(3)).astype(BF16)
    for j, lo, hi, at in ((1, D, CW, 0), (2, 0, 2 * D, 2 * D)):
        u = dot(n2, wpart(w, j, lo, hi))
        u2 = u * u
        t = jnp.tanh(u * (GELU_C + (GELU_C * 0.044715) * u2))
        half = 0.5 * t + 0.5
        g_ref[:, at : at + 2 * D] = (u * half).astype(BF16)
        gp = half + (u * (0.5 - 0.5 * t * t)) * (GELU_C + (3.0 * GELU_C * 0.044715) * u2)
        gp_ref[:, at : at + 2 * D] = gp.astype(BF16)
    mlp = dot_nt(g_ref[:, 0:D], wpart(w, 2, 2 * D, CW)) + dot_nt(g_ref[:, D:], wpart(w, 3, 0, CW))
    mlp_ref[...] = mlp.astype(BF16)
    return h2 + mod(5) * mlp


def block_backward(d3, h, mod, w, sv, dw, du_ref, dqkv_ref, dmod_ref):
    qkv_ref, p_ref, o_ref, g_ref, gp_ref, att_ref, mlp_ref, h2_ref = sv
    dmlp = (d3 * mod(5)).astype(BF16)
    dmod_ref[5:6, :] = jnp.sum(d3 * mlp_ref[...].astype(F32), axis=0, keepdims=True)
    du_ref[:, 0:D] = (dot(dmlp, wpart(w, 2, 2 * D, CW)) * gp_ref[:, 0:D].astype(F32)).astype(BF16)
    du_ref[:, D:] = (dot(dmlp, wpart(w, 3, 0, CW)) * gp_ref[:, D:].astype(F32)).astype(BF16)
    dw[2, :, 2 * D : CW] += dot_tn(dmlp, g_ref[:, 0:D])
    dw[3] += dot_tn(dmlp, g_ref[:, D:])
    dn2 = dot_nt(du_ref[:, 0 : 2 * D], wpart(w, 1, D, CW)) + dot_nt(du_ref[:, 2 * D :], wpart(w, 2, 0, 2 * D))
    y2, r2 = layer_norm(h2_ref[...])
    n2 = (y2 * (1.0 + mod(4)) + mod(3)).astype(BF16)
    dw[1, :, D:CW] += dot_tn(n2, du_ref[:, 0 : 2 * D])
    dw[2, :, 0 : 2 * D] += dot_tn(n2, du_ref[:, 2 * D :])
    dv, dshift, dscale = norm_grad(dn2, y2, r2, mod(4))
    dmod_ref[3:4, :] = dshift
    dmod_ref[4:5, :] = dscale
    d2 = d3 + dv
    datt = (d2 * mod(2)).astype(BF16)
    dmod_ref[2:3, :] = jnp.sum(d2 * att_ref[...].astype(F32), axis=0, keepdims=True)
    do = dot_nt(datt, wpart(w, 1, 0, D)).astype(BF16)
    dw[1, :, 0:D] += dot_tn(o_ref[...], datt)
    masks = head_masks()
    for j in range(3):
        q2 = qkv_ref[:, 128 * j : 128 * j + 128]
        k2 = qkv_ref[:, D + 128 * j : D + 128 * j + 128]
        v2 = qkv_ref[:, 2 * D + 128 * j : 2 * D + 128 * j + 128]
        do2 = do[:, 128 * j : 128 * j + 128]
        dq2, dk2, dv2 = 0.0, 0.0, 0.0
        for a in range(2):
            one = masks[a].astype(BF16)
            eighth = (masks[a] * 0.125).astype(BF16)
            pb = p_ref[2 * j + a]
            p = pb.astype(F32)
            dp = dot_nt(do2, v2 * one)
            ds = (p * (dp - jnp.sum(p * dp, axis=-1, keepdims=True))).astype(BF16)
            dq2 += dot(ds, k2 * eighth)
            dk2 += dot_tn(ds, q2 * eighth)
            dv2 += dot_tn(pb, do2 * one)
        dqkv_ref[:, 128 * j : 128 * j + 128] = dq2.astype(BF16)
        dqkv_ref[:, D + 128 * j : D + 128 * j + 128] = dk2.astype(BF16)
        dqkv_ref[:, 2 * D + 128 * j : 2 * D + 128 * j + 128] = dv2.astype(BF16)
    dn1 = dot_nt(dqkv_ref[...], wpart(w, 0, 0, CW))
    y1, r1 = layer_norm(h)
    n1 = (y1 * (1.0 + mod(1)) + mod(0)).astype(BF16)
    dw[0] += dot_tn(n1, dqkv_ref[...])
    dv, dshift, dscale = norm_grad(dn1, y1, r1, mod(1))
    dmod_ref[0:1, :] = dshift
    dmod_ref[1:2, :] = dscale
    return d2 + dv


def load_weights(ids, pieces, w, sems):
    @pl.when(pl.program_id(0) == 0)
    def _():
        copies = []
        if len(pieces) == 1:
            copies.append(pltpu.make_async_copy(pieces[0], w, sems.at[0]))
        else:
            for c in range(2):
                for k in range(4):
                    target = w.at[ids[0] ^ k, :, ids[1] ^ c]
                    copies.append(pltpu.make_async_copy(pieces[4 * c + k], target, sems.at[4 * c + k]))
        for copy in copies:
            copy.start()
        for copy in copies:
            copy.wait()


def mod_row(mod_ref):
    return lambda i: mod_ref[i : i + 1, :]


def enc_forward_kernel(n, ids, valid, xin, pe, misc, mod, bias, *rest):
    pieces, (h0, h3), sv, (w, sems) = rest[:n], rest[n : n + 2], rest[n + 2 : n + 10], rest[n + 10 :]
    load_weights(ids, pieces, w, sems)

    @pl.when(valid[pl.program_id(0)] > 0)
    def _():
        h = dot_nt(xin[...], misc[...]) + pe[...]
        h0[...] = h
        h3[...] = block_forward(h, mod_row(mod), w, bias[...], sv)


def token_row(misc):
    lane = lax.broadcasted_iota(jnp.int32, (8, 128), 1)
    return dot_nt((lane == PIN).astype(BF16), misc[...])[0:1, :]


def side_forward_kernel(n, ids, valid, h_in, mask, pe, misc, mod, *rest):
    pieces, (hs, h3), sv, (w, sems) = rest[:n], rest[n : n + 2], rest[n + 2 : n + 10], rest[n + 10 :]
    load_weights(ids, pieces, w, sems)

    @pl.when(valid[pl.program_id(0)] > 0)
    def _():
        m = mask[...]
        h = h_in[...] * (1.0 - m) + m * (token_row(misc) + pe[...])
        hs[...] = h
        h3[...] = block_forward(h, mod_row(mod), w, None, sv)


def store_grads(dw, out):
    for j in range(CHUNKS):
        out[j] = dw[j].astype(BF16)


def dec_kernel(n, ids, valid, coef, h_in, noise, misc, mod, *rest):
    pieces = rest[:n]
    d_in, dmod, dw_out, dmisc, loss = rest[n : n + 5]
    w, sems, dw, du, dqkv = rest[n + 5 : n + 10]
    sv = rest[n + 10 :]
    load_weights(ids, pieces, w, sems)
    step = pl.program_id(0)

    @pl.when(step == 0)
    def _():
        dw[...] = jnp.zeros_like(dw)
        dmisc[...] = jnp.zeros_like(dmisc)
        loss[...] = jnp.zeros_like(loss)

    @pl.when(valid[step] <= 0)
    def _():
        dmod[...] = jnp.zeros_like(dmod)

    @pl.when(valid[step] > 0)
    def _():
        row = mod_row(mod)
        h = h_in[...]
        h_dec = block_forward(h, row, w, None, sv)
        yf, rf = layer_norm(h_dec)
        nf = (yf * (1.0 + row(7)) + row(6)).astype(BF16)
        out = dot(nf, misc[...])
        ln_b, ln_pv, wmean = coef[step, 2], coef[step, 3], coef[step, 4]
        lane = lax.broadcasted_iota(jnp.int32, (1, 128), 1)
        live = (lane >= 32) & (lane < 32 + PIN)
        d = jnp.where(live, out - noise[...], 0.0)
        vf = (pltpu.roll(out, 128 - 32, 1) + 1.0) * 0.5
        vf = jnp.where(live, vf, 0.0)
        lv = vf * ln_b + (1.0 - vf) * ln_pv
        first = jnp.exp(ln_pv - lv)
        second = wmean * jnp.exp(-lv)
        inv = 0.5 / math.log(2.0)
        dd = d * d
        kl = inv * (-1.0 + lv - ln_pv + first + dd * second)
        term = jnp.where(live, dd + kl, 0.0)
        loss[...] += jnp.sum(term.reshape(NTOK // 8, 8, 128), axis=0)
        deps = d * (2.0 + (2.0 * inv) * second)
        dlog = inv * (1.0 - first - dd * second) * (0.5 * (ln_b - ln_pv))
        dlog = jnp.where(live, dlog, 0.0)
        dout = (deps + pltpu.roll(dlog, 32, 1)).astype(BF16)
        dmisc[...] += dot_tn(nf, dout)
        dnf = dot_nt(dout, misc[...])
        d3, dshift, dscale = norm_grad(dnf, yf, rf, row(7))
        dmod[6:7, :] = dshift
        dmod[7:8, :] = dscale
        d_in[...] = block_backward(d3, h, row, w, sv, dw, du, dqkv, dmod)

    @pl.when(step == pl.num_programs(0) - 1)
    def _():
        store_grads(dw, dw_out)


def side_backward_kernel(n, ids, valid, d_out, h_in, mask, mod, *rest):
    sv, pieces, rest = rest[:8], rest[8 : 8 + n], rest[8 + n :]
    d_enc, dmod, dw_out, dtok, w, sems, dw, du, dqkv = rest
    load_weights(ids, pieces, w, sems)
    step = pl.program_id(0)

    @pl.when(step == 0)
    def _():
        dw[...] = jnp.zeros_like(dw)
        dtok[...] = jnp.zeros_like(dtok)

    @pl.when(valid[step] <= 0)
    def _():
        dmod[...] = jnp.zeros_like(dmod)

    @pl.when(valid[step] > 0)
    def _():
        m = mask[...]
        dh = block_backward(d_out[...], h_in[...], mod_row(mod), w, sv, dw, du, dqkv, dmod)
        dm = dh * m
        dtok[...] += jnp.sum(dm.reshape(NTOK // 8, 8, D), axis=0)
        d_enc[...] = dh - dm

    @pl.when(step == pl.num_programs(0) - 1)
    def _():
        store_grads(dw, dw_out)


def enc_backward_kernel(n, ids, valid, d_out, h_in, xin, mod, *rest):
    sv, pieces, rest = rest[:8], rest[8 : 8 + n], rest[8 + n :]
    dmod, dw_out, dmisc, w, sems, dw, du, dqkv = rest
    load_weights(ids, pieces, w, sems)
    step = pl.program_id(0)

    @pl.when(step == 0)
    def _():
        dw[...] = jnp.zeros_like(dw)
        dmisc[...] = jnp.zeros_like(dmisc)

    @pl.when(valid[step] <= 0)
    def _():
        dmod[...] = jnp.zeros_like(dmod)

    @pl.when(valid[step] > 0)
    def _():
        dh = block_backward(d_out[...], h_in[...], mod_row(mod), w, sv, dw, du, dqkv, dmod)
        dmisc[...] += dot_tn(dh.astype(BF16), xin[...])

    @pl.when(step == pl.num_programs(0) - 1)
    def _():
        store_grads(dw, dw_out)


SMEM = pl.BlockSpec(memory_space=pltpu.SMEM)
ANY = pl.BlockSpec(memory_space=pl.ANY)


def slot_spec(*shape):
    return pl.BlockSpec((None,) + shape, lambda s: (s,) + (0,) * len(shape))


def fixed_spec(*shape):
    return pl.BlockSpec(shape, lambda s: (0,) * len(shape))


SAVES = (
    ((NTOK, 3 * D), BF16),
    ((HEADS, NTOK, NTOK), BF16),
    ((NTOK, D), BF16),
    ((NTOK, FF), BF16),
    ((NTOK, FF), BF16),
    ((NTOK, D), BF16),
    ((NTOK, D), BF16),
    ((NTOK, D), F32),
)


def weight_scratch():
    return [pltpu.VMEM((CHUNKS, 4, 2, D // 8, CW), BF16), pltpu.SemaphoreType.DMA((8,))]


def grad_scratch():
    return [
        pltpu.VMEM((CHUNKS, D, CW), F32),
        pltpu.VMEM((NTOK, FF), BF16),
        pltpu.VMEM((NTOK, 3 * D), BF16),
    ]


def call(kernel, slots, in_specs, args, pieces, outs, scratch, macs):
    specs = list(in_specs) + [ANY] * len(pieces)
    return pl.pallas_call(
        functools.partial(kernel, len(pieces)),
        grid=(slots,),
        in_specs=specs,
        out_specs=[o[0] for o in outs],
        out_shape=[jax.ShapeDtypeStruct(o[1], o[2]) for o in outs],
        scratch_shapes=scratch,
        compiler_params=pltpu.CompilerParams(vmem_limit_bytes=VMEM_LIMIT, dimension_semantics=("arbitrary",)),
        cost_estimate=pl.CostEstimate(flops=int(2 * macs * slots), bytes_accessed=int(8e6), transcendentals=0),
    )(*args, *pieces)


def slot_out(slots, shape, kind):
    return (slot_spec(*shape), (slots,) + shape, kind)


def fixed_out(shape, kind):
    return (fixed_spec(*shape), shape, kind)


BLOCK_MACS = NTOK * (D * TOKW + 2 * NTOK * D)


def enc_forward(slots, ids, valid, xin, pe, misc, mod, bias, pieces):
    return call(
        enc_forward_kernel,
        slots,
        [SMEM, SMEM, slot_spec(NTOK, 128), fixed_spec(NTOK, D), fixed_spec(D, 128), slot_spec(6, D), slot_spec(1, NTOK)],
        [ids, valid, xin, pe, misc, mod, bias],
        pieces,
        [slot_out(slots, (NTOK, D), F32)] * 2 + [slot_out(slots, s, k) for s, k in SAVES],
        weight_scratch(),
        BLOCK_MACS,
    )


def side_forward(slots, ids, valid, h_in, mask, pe, misc, mod, pieces):
    return call(
        side_forward_kernel,
        slots,
        [SMEM, SMEM, slot_spec(NTOK, D), slot_spec(NTOK, 1), fixed_spec(NTOK, D), fixed_spec(D, 128), slot_spec(6, D)],
        [ids, valid, h_in, mask, pe, misc, mod],
        pieces,
        [slot_out(slots, (NTOK, D), F32)] * 2 + [slot_out(slots, s, k) for s, k in SAVES],
        weight_scratch(),
        BLOCK_MACS,
    )


def dec_both(slots, ids, valid, coef, h_in, noise, misc, mod, pieces):
    return call(
        dec_kernel,
        slots,
        [SMEM, SMEM, SMEM, slot_spec(NTOK, D), slot_spec(NTOK, 128), fixed_spec(D, 128), slot_spec(8, D)],
        [ids, valid, coef, h_in, noise, misc, mod],
        pieces,
        [
            slot_out(slots, (NTOK, D), F32),
            slot_out(slots, (8, D), F32),
            fixed_out((CHUNKS, D, CW), BF16),
            fixed_out((D, 128), F32),
            fixed_out((8, 128), F32),
        ],
        weight_scratch() + grad_scratch() + [pltpu.VMEM(s, k) for s, k in SAVES],
        3 * BLOCK_MACS,
    )


def side_backward(slots, ids, valid, d_out, h_in, mask, mod, saves, pieces):
    return call(
        side_backward_kernel,
        slots,
        [SMEM, SMEM, slot_spec(NTOK, D), slot_spec(NTOK, D), slot_spec(NTOK, 1), slot_spec(6, D)] + [slot_spec(*s) for s, _ in SAVES],
        [ids, valid, d_out, h_in, mask, mod] + list(saves),
        pieces,
        [
            slot_out(slots, (NTOK, D), F32),
            slot_out(slots, (8, D), F32),
            fixed_out((CHUNKS, D, CW), BF16),
            fixed_out((8, D), F32),
        ],
        weight_scratch() + grad_scratch(),
        2 * BLOCK_MACS,
    )


def enc_backward(slots, ids, valid, d_out, h_in, xin, mod, saves, pieces):
    return call(
        enc_backward_kernel,
        slots,
        [SMEM, SMEM, slot_spec(NTOK, D), slot_spec(NTOK, D), slot_spec(NTOK, 128), slot_spec(6, D)] + [slot_spec(*s) for s, _ in SAVES],
        [ids, valid, d_out, h_in, xin, mod] + list(saves),
        pieces,
        [
            slot_out(slots, (8, D), F32),
            fixed_out((CHUNKS, D, CW), BF16),
            fixed_out((D, 128), F32),
        ],
        weight_scratch() + grad_scratch(),
        2 * BLOCK_MACS,
    )


def silu_slope(val):
    s = jax.nn.sigmoid(val)
    return s * (1.0 + val * (1.0 - s))


def adam(master, first_m, second, grad_in):
    first_new = beta_one * first_m + (1.0 - beta_one) * grad_in
    second_new = beta_two * second + (1.0 - beta_two) * grad_in * grad_in
    first_hat = first_new / (1.0 - beta_one**STEP)
    second_hat = second_new / (1.0 - beta_two**STEP)
    master_new = master - learn_rate * (first_hat / (jnp.sqrt(second_hat) + adam_eps) + weight_decay * master)
    return [master_new, first_new, second_new]


def block_grad(dw):
    mine = lax.psum_scatter(dw, "fsdp", scatter_dimension=1, tiled=True)
    if lax.axis_size("dp") == CHUNKS:
        return reduce_parts(mine, "dp", BF16).astype(BF16)
    mine = mine.transpose(1, 0, 2).reshape(mine.shape[1], TOKW)
    return reduce_parts(mine.reshape(mine.shape[0], lax.axis_size("dp"), -1).transpose(1, 0, 2), "dp", BF16).astype(BF16)


def all_columns(part):
    full = gather(part, "dp")
    return full.transpose(1, 0, 2).reshape(part.shape[0], -1)


def on_device(latents, noise, timesteps, labels, patch_mask, counts, owners, tables_w, tables_m, tables_v, rows_w, rows_m, rows_v, down_w, down_m, down_v):
    nd, nf = lax.axis_size("dp"), lax.axis_size("fsdp")
    me_d, me_f = lax.axis_index("dp"), lax.axis_index("fsdp")
    rows = tables_w.shape[0]
    micro, per = latents.shape[0], latents.shape[1]
    slots = micro * per
    lats = nf * slots

    rows_b, down_b, tables_b = rows_w.astype(BF16), down_w.astype(BF16), tables_w.astype(BF16)
    pieces = []
    for b in range(3):
        at = D + b * STRIDE
        whole = jnp.concatenate([rows_b[:, at : at + 4 * D + FF], down_b[:, b * FF : (b + 1) * FF]], axis=1)
        chunk = lax.dynamic_slice_in_dim(whole, me_d * (TOKW // nd), TOKW // nd, 1)
        pieces.append(gather_block(chunk, whole))
    head_at = D + 3 * STRIDE + 2 * D
    gap = jnp.zeros((rows, 16), BF16)
    misc_own = jnp.concatenate(
        [
            tables_b[:, : PIN + 1],
            gap[:, :15],
            rows_b[:, head_at : head_at + PIN],
            gap,
            rows_b[:, head_at + PIN : head_at + 2 * PIN],
            gap,
            gap,
            gap,
        ],
        axis=1,
    )
    misc = gather(misc_own, "fsdp").reshape(D, 128)

    steps = timesteps.reshape(slots)
    plan = jnp.take(jnp.asarray(plan_table()), steps, axis=0)
    info = gather(jnp.stack([steps, labels.reshape(slots)]), "fsdp")
    steps_g, labels_g = info[:, 0].reshape(lats), info[:, 1].reshape(lats)
    feat = time_features(steps_g).astype(BF16)
    w_tone = tables_b[:, PIN + 1 : PIN + 1 + FREQ]
    class_tab = tables_b[:, PIN + 1 + FREQ :]
    w_ttwo = rows_b[:, :D]
    ada_at = [D + b * STRIDE + 4 * D + FF for b in range(3)]
    fin_at = D + 3 * STRIDE
    w_ada = jnp.concatenate([rows_b[:, a : a + 6 * D] for a in ada_at] + [rows_b[:, fin_at : fin_at + 2 * D]], axis=1)
    a_pre = dot_nt(feat, w_tone)
    a_act = jax.nn.silu(a_pre).astype(BF16)
    hot = (labels_g[:, None] == jnp.arange(CLASSES)[None, :]).astype(BF16)
    c_part = dot(a_act, w_ttwo).reshape(lats, nf, rows).transpose(1, 0, 2)
    cond = reduce_parts(c_part, "fsdp", F32) + dot_nt(hot, class_tab)
    s_cond = jax.nn.silu(cond).astype(BF16)
    mod_part = dot(s_cond, w_ada).reshape(nf, slots, 20 * D)
    mods = reduce_parts(mod_part, "fsdp", F32).reshape(slots, 20, D)
    mod_e, mod_s, mod_d = mods[:, 0:6], mods[:, 6:12], mods[:, 12:20]

    x_zero, eps = latents.reshape(slots, NTOK * PIN), noise.reshape(slots, NTOK * PIN)
    x_in = (plan[:, 0:1] * x_zero + plan[:, 1:2] * eps).astype(BF16).reshape(slots, NTOK, PIN)
    x_in = jnp.pad(x_in, ((0, 0), (0, 0), (0, 128 - PIN)))
    eps = jnp.pad(eps.reshape(slots, NTOK, PIN), ((0, 0), (0, 0), (32, 96 - PIN)))
    masked = patch_mask.reshape(slots, NTOK).astype(F32)
    bias = (-1e9 * masked)[:, None, :]
    mask_col = masked[:, :, None]
    pe = jnp.asarray(position_table())
    valid = (jnp.arange(per)[None, :] < counts).astype(jnp.int32).reshape(slots)
    ids = jnp.stack([me_d, me_f % 2]).astype(jnp.int32)

    h0, h_enc, *save_e = enc_forward(slots, ids, valid, x_in, pe, misc, mod_e, bias, pieces[0])
    hs, h_side, *save_s = side_forward(slots, ids, valid, h_enc, mask_col, pe, misc, mod_s, pieces[1])
    d_side, dmod_d, dw_d, dmisc_d, loss = dec_both(slots, ids, valid, plan, h_side, eps, misc, mod_d, pieces[2])
    g_dec = block_grad(dw_d)
    d_enc, dmod_s, dw_s, dtok = side_backward(slots, ids, valid, d_side, hs, mask_col, mod_s, save_s, pieces[1])
    g_side = block_grad(dw_s)
    dmod_e, dw_e, dmisc_e = enc_backward(slots, ids, valid, d_enc, h0, x_in, mod_e, save_e, pieces[0])
    g_enc = block_grad(dw_e)

    def group(val):
        return gather(val.astype(BF16).reshape(slots, -1), "fsdp").reshape(lats, -1)

    dm_all = jnp.concatenate([group(dmod_e[:, :6]), group(dmod_s[:, :6]), group(dmod_d)], axis=1)
    d_cond = dot_nt(dm_all, w_ada) * silu_slope(cond)
    d_cond_all = gather(d_cond.astype(BF16), "fsdp").transpose(1, 0, 2).reshape(lats, D)
    d_apre = (dot_nt(d_cond_all, w_ttwo) * silu_slope(a_pre)).astype(BF16)
    g_ada = dot_tn(s_cond, dm_all)
    g_ttwo = dot_tn(a_act, d_cond_all)
    g_tone = dot_tn(d_apre, feat)
    g_class = lax.dot_general(d_cond, hot.astype(F32), (((0,), (0,)), ((), ())), precision=lax.Precision.HIGHEST, preferred_element_type=F32)
    dmisc = dmisc_e + dmisc_d
    tok = jnp.sum(dtok, axis=0)[:, None]
    dmisc = jnp.concatenate([dmisc[:, :PIN], tok, dmisc[:, PIN + 1 :]], axis=1)
    g_misc = reduce_parts(dmisc.reshape(nf, rows, 128), "fsdp", F32)
    cond_grad = jnp.concatenate([g_ada, g_ttwo, g_tone, g_class, g_misc, jnp.zeros((rows, 24), F32)], axis=1)
    width = cond_grad.shape[1]
    g_cond = reduce_parts(cond_grad.reshape(rows, nd, width // nd).transpose(1, 0, 2), "dp", BF16).astype(BF16)

    parts = [g_enc, g_side, g_dec, g_cond]
    squares = sum(jnp.sum(jnp.square(p.astype(F32))) for p in parts)
    used = jnp.sum(valid).astype(F32)
    norm_sq, loss_sum, count = sum_all(jnp.stack([squares, jnp.sum(loss), used]))
    scale = 1.0 / (count * (NTOK * PIN))
    loss_out = loss_sum * scale
    grad_norm = jnp.sqrt(norm_sq) * scale
    factor = scale * jnp.minimum(1.0, clip_level / (grad_norm + 1e-06))

    f_enc, f_side, f_dec, f_cond = [all_columns(p) for p in parts]
    ada = [f_cond[:, i * 6 * D : (i + 1) * 6 * D] for i in range(3)]
    at = 18 * D
    fin, at = f_cond[:, at : at + 2 * D], at + 2 * D
    ttwo, at = f_cond[:, at : at + D], at + D
    tone, at = f_cond[:, at : at + FREQ], at + FREQ
    klass, at = f_cond[:, at : at + CLASSES], at + CLASSES
    small = f_cond[:, at : at + 128]
    heads = jnp.concatenate([small[:, 32 : 32 + PIN], small[:, 64 : 64 + PIN]], axis=1)
    up_to = 4 * D + FF
    rows_g = [ttwo]
    for blk, a in zip((f_enc, f_side, f_dec), ada):
        rows_g += [blk[:, :up_to], a]
    rows_g = jnp.concatenate(rows_g + [fin, heads], axis=1)
    down_g = jnp.concatenate([blk[:, up_to:] for blk in (f_enc, f_side, f_dec)], axis=1)
    tables_g = jnp.concatenate([small[:, : PIN + 1], tone, klass], axis=1)
    results = adam(tables_w, tables_m, tables_v, factor * tables_g.astype(F32))

    def own(val):
        size = val.shape[1] // nd
        return lax.dynamic_slice_in_dim(val, me_d * size, size, 1)

    results += adam(own(rows_w), own(rows_m), own(rows_v), factor * own(rows_g).astype(F32))
    results += adam(own(down_w), own(down_m), own(down_v), factor * own(down_g).astype(F32))
    return tuple([loss_out, grad_norm] + results)


def solution(mesh):
    lat = P(None, ("dp", "fsdp"), None)
    num = P(None, ("dp", "fsdp"))
    row = P("fsdp", None)
    both = P("fsdp", "dp")
    return jax.shard_map(
        on_device,
        mesh=mesh,
        in_specs=(lat, lat, num, num, lat, num, P()) + (row,) * 9,
        out_specs=(P(), P()) + (row,) * 3 + (both,) * 6,
        check_vma=False,
    )
```

time: 1550 us -> 502 us (0.32)
  waiting for transfers between devices: 597 us -> 82.6 us
  matrix products: 351 us -> 3.97 us
  local copies, waits for them, and re-layouts: 328 us -> 42.2 us
  starting transfers between devices: 0.28 us -> 200 us
  Pallas kernels: 0 us -> 106 us
  blocking collectives: 96.9 us -> 0 us
  other arithmetic: 131 us -> 36 us
    dot_general x156 -> x9, matrix products: 351 us -> 3.97 us  [the longest x3 1.66 us: dot_tn(): lax.dot_general(a, b, (((0,), (0,)), ((), ())), preferred_element_type=F32)]
    reduce_scatter x1 -> x3, waiting for transfers between devices: 347 us -> 0.02 us  [block_grad(): mine = lax.psum_scatter(dw, 'fsdp', scatter_dimension=1, tiled=True)]
    psum x2 -> x0, waiting for transfers between devices: 204 us -> none  [the longest x1 148 us: spread(): return lax.psum(jnp.where(mine, shard, jnp.zeros_like(shard)), axis)]
    ppermute x0 -> x97, starting transfers between devices: none -> 199 us  [swap(): return lax.ppermute(val, axis, [(i, i ^ mask) for i in range(size)])]
    pallas_call x0 -> x5, Pallas kernels: none -> 106 us  [call(): pl.pallas_call(functools.partial(kernel, len(pieces)), grid=(slots,), in_...]
    unnamed x872 -> x124, local copies, waits for them, and re-layouts: 100 us -> 5.69 us
    concatenate x8 -> x6, local copies, waits for them, and re-layouts: 94.4 us -> 3.22 us  [the longest x1 1.48 us: on_device(): jnp.concatenate([g_ada, g_ttwo, g_tone, g_class, g_misc, jnp.zeros((rows,...]
    ppermute x0 -> x97, waiting for transfers between devices: none -> 82.5 us  [swap(): return lax.ppermute(val, axis, [(i, i ^ mask) for i in range(size)])]
  transfers between devices with their start and end apart: 7 -> 100, of which waited for: 5 -> 28; matrix products, arithmetic and copies ran while one was open for 13% -> 13% of each run, Pallas kernels for 0% -> 16%
where the time goes in v1:
time: 502 us; the launch traced here: 494 us
  starting transfers between devices  200 us (40%)
  Pallas kernels  106 us (21%)
  waiting for transfers between devices  82.6 us (16%)
  local copies, waits for them, and re-layouts  42.2 us (8%)
  other arithmetic  36 us (7%)
  between operations  23.3 us (5%)
    ppermute x97, starting transfers between devices, swap(): return lax.ppermute(val, axis, [(i, i ^ mask) for i in range(size)])  199 us
    pallas_call x5, Pallas kernels, call(): pl.pallas_call(functools.partial(kernel, len(pieces)), grid=(slots,), in_...  106 us
    ppermute x97, waiting for transfers between devices, swap(): return lax.ppermute(val, axis, [(i, i ^ mask) for i in range(size)])  82.5 us
  transfers between devices with their start and end apart: 100, of which 28 were waited for; matrix products, arithmetic and copies ran while one was open for 13% of the time, Pallas kernels for 16%

profile of v1, /device:TPU:0, one launch (start us, length us, event | category | flops | bytes accessed | tf_op | source)
XLA Modules:
  0.0 493.6 jit_solution(992065592042396769)
XLA Ops:
  12.7 3.0 collective-permute-start.26
  19.6 3.9 collective-permute-start.6
  50.3 3.8 collective-permute-start.2
  72.1 2.7 collective-permute-start.37
  82.6 4.9 collective-permute-done.37
  93.0 10.7 %collective-permute-done.30.rest_2_.rest_10_ = bf16[4,48,1152]{2,1,0:T(8,128)(2,1)} collective-permute-done((bf16[4,48,1152]{2,1,0:T(8,128)(2,1)S(1)}, bf16[4,48,1152]{2,1,0:T(8,128)(2,1)}, u32[]{:S(2)}, u32[]{:S(2)}) %collective-permute-start.30) | collective-permute-done | bytes 442400 | tf_op jit(solution)/shard_map/ppermute | solution.py:88
  106.0 3.6 collective-permute-start.13
  113.4 7.8 %collective-permute-done.20.rest_2_.rest_10_ = bf16[4,48,1152]{2,1,0:T(8,128)(2,1)S(1)} collective-permute-done((bf16[4,48,1152]{2,1,0:T(8,128)(2,1)S(1)}, bf16[4,48,1152]{2,1,0:T(8,128)(2,1)S(1)}, u32[]{:S(2)}, u32[]{:S(2)}) %collective-permute-start.20) | collective-permute-done | bytes 442400 | tf_op jit(solution)/shard_map/ppermute | solution.py:88
  122.0 3.2 collective-permute-done.14
  128.3 5.7 %collective-permute-done.39.rest_1_ = bf16[4,48,1152]{2,1,0:T(8,128)(2,1)} collective-permute-done((bf16[4,48,1152]{2,1,0:T(8,128)(2,1)S(1)}, bf16[4,48,1152]{2,1,0:T(8,128)(2,1)}, u32[]{:S(2)}, u32[]{:S(2)}) %collective-permute-start.39) | collective-permute-done | bytes 442400 | tf_op jit(solution)/shard_map/ppermute | solution.py:88
  136.0 18.4 %shard_map.248 = (f32[6,256,384]{2,1,0:T(8,128)}, f32[6,256,384]{2,1,0:T(8,128)}, bf16[6,256,1152]{2,1,0:T(8,128)(2,1)}, bf16[6,6,256,256]{3,2,1,0:T(8,128)(2,1)...) custom-call(s32[2]{0:T(128)} %pad_add_fusion.2.ids, ...), custom_call_target="tpu_custom_call" | custom-call | flops 6039797760 | bytes 8000000 | tf_op jit(solution)/shard_map/pallas_call | solution.py:476
  154.5 11.0 %collective-permute-start.42 = (bf16[4,48,1152]{2,1,0:T(8,128)(2,1)S(1)}, bf16[4,48,1152]{2,1,0:T(8,128)(2,1)S(1)}, u32[]{:S(2)}, u32[]{:S(2)}) collective-permute-start(bf16[4,48,1152]{2,1,0:T(8,128)(2,1)S(1)} %pad_maximum_fusion.3.rest_0_), channel_id=1, source_target_pairs={{0,1},{1,0},{2,3},{3,2},{4,5},{5,4},{6,7},{7,6},{8,9},{9,8},{10,11... | collective-permute-start | bytes 1327112 | tf_op jit(solution)/shard_map/ppermute | solution.py:88
  167.0 18.9 %shard_map.249 = (f32[6,256,384]{2,1,0:T(8,128)}, f32[6,256,384]{2,1,0:T(8,128)}, bf16[6,256,1152]{2,1,0:T(8,128)(2,1)}, bf16[6,6,256,256]{3,2,1,0:T(8,128)(2,1)...) custom-call(s32[2]{0:T(128)} %pad_add_fusion.2.ids, ...), custom_call_target="tpu_custom_call" | custom-call | flops 6039797760 | bytes 8000000 | tf_op jit(solution)/shard_map/pallas_call | solution.py:476
  187.1 26.8 %shard_map.250 = (f32[6,256,384]{2,1,0:T(8,128)}, f32[6,8,384]{2,1,0:T(8,128)}, bf16[4,384,1152]{2,1,0:T(8,128)(2,1)}, f32[384,128]{1,0:T(8,128)}, f32[8,128]{1,0:T(8,128)}) custom-call(s32[2]{0:T(128)} %pad_add_fusion.2.ids, s32[6]{0:T(128)} %reshape.213.valid, f32[6,8]{1,0:T(8,128)} %copy-done.30, f32[6,256,384]{2,1,0:T(8,128)} %get-tuple-element.44.h_in, ...), custom_call_target="tpu_custom_call" | custom-call | flops 18119393280 | bytes 8000000 | tf_op jit(solution)/shard_map/pallas_call | solution.py:476
  214.0 21.2 %shard_map.251 = (f32[6,256,384]{2,1,0:T(8,128)}, f32[6,8,384]{2,1,0:T(8,128)}, bf16[4,384,1152]{2,1,0:T(8,128)(2,1)}, f32[8,384]{1,0:T(8,128)}) custom-call(s32[2]{0:T(128)} %pad_add_fusion.2.ids, s32[6]{0:T(128)} %reshape.213.valid, f32[6,256,384]{2,1,0:T(8,128)} %get-tuple-element.45.d_out, f32[6,256,384]{2,1,0:T(8,128)} %get-tuple-element.46.h_in, ...), custom_call_target="tpu_custom_call" | custom-call | flops 12079595520 | bytes 8000000 | tf_op jit(solution)/shard_map/pallas_call | solution.py:476
  235.4 20.6 %shard_map.252 = (f32[6,8,384]{2,1,0:T(8,128)}, bf16[4,384,1152]{2,1,0:T(8,128)(2,1)}, f32[384,128]{1,0:T(8,128)}) custom-call(s32[2]{0:T(128)} %pad_add_fusion.2.ids, s32[6]{0:T(128)} %reshape.213.valid, f32[6,256,384]{2,1,0:T(8,128)} %get-tuple-element.55.d_out, f32[6,256,384]{2,1,0:T(8,128)} %get-tuple-element.56.h_in, bf16[6,256,128]{2,1,0:T(8,128)(2,1)} %pad.8.xin, ...), custom_call_target="tpu_custom_call" | custom-call | flops 12079595520 | bytes 8000000 | tf_op jit(solution)/shard_map/pallas_call | solution.py:476
  256.9 19.1 %collective-permute-start.55 = (bf16[6,2304]{1,0:T(8,128)(2,1)S(1)}, bf16[6,2304]{1,0:T(8,128)(2,1)S(1)}, u32[]{:S(2)}, u32[]{:S(2)}) collective-permute-start(bf16[6,2304]{1,0:T(8,128)(2,1)S(1)} %bitcast.326), channel_id=1, source_target_pairs={{0,2},{1,3},{2,0},{3,1},{4,6},{5,7},{6,4},{7,5},{8,10},{9,11},{10,... | collective-permute-start | bytes 82952 | tf_op jit(solution)/shard_map/ppermute | solution.py:88
  275.9 21.4 %collective-permute-start.56 = (bf16[6,2304]{1,0:T(8,128)(2,1)S(1)}, bf16[6,2304]{1,0:T(8,128)(2,1)S(1)}, u32[]{:S(2)}, u32[]{:S(2)}) collective-permute-start(bf16[6,2304]{1,0:T(8,128)(2,1)S(1)} %bitcast.327), channel_id=1, source_target_pairs={{0,4},{1,5},{2,6},{3,7},{4,0},{5,1},{6,2},{7,3},{8,12},{9,13},{10,... | collective-permute-start | bytes 82952 | tf_op jit(solution)/shard_map/ppermute | solution.py:88
  298.0 3.8 collective-permute-start.60
  304.1 3.8 collective-permute-start.64
  307.9 35.1 %collective-permute-start.71 = (f32[4,48,128]{2,1,0:T(8,128)S(1)}, f32[4,48,128]{2,1,0:T(8,128)S(1)}, u32[]{:S(2)}, u32[]{:S(2)}) collective-permute-start(f32[4,48,128]{2,1,0:T(8,128)S(1)} %dynamic-slice_bitcast_fusion.9), channel_id=1, source_target_pairs={{0,1},{1,0},{2,3},{3,2},{4,5},{5,4},{6,7},{7,6},{8,9},{9,8},{10,11... | collective-permute-start | bytes 294920 | tf_op jit(solution)/shard_map/ppermute | solution.py:88
  358.6 2.8 collective-permute-start.69
  368.6 3.0 reshape.208
  373.1 8.3 %collective-permute-start.76 = (bf16[48,2368]{1,0:T(8,128)(2,1)S(1)}, bf16[48,2368]{1,0:T(8,128)(2,1)S(1)}, u32[]{:S(2)}, u32[]{:S(2)}) collective-permute-start(bf16[48,2368]{1,0:T(8,128)(2,1)S(1)} %bitcast.320), channel_id=1, source_target_pairs={{0,16},{8,24},{16,0},{24,8},{1,17},{9,25},{17,1},{25,9},{2,18},{10... | collective-permute-start | bytes 681992 | tf_op jit(solution)/shard_map/ppermute | solution.py:88
  381.9 10.2 %collective-permute-done.76 = bf16[48,2368]{1,0:T(8,128)(2,1)S(1)} collective-permute-done((bf16[48,2368]{1,0:T(8,128)(2,1)S(1)}, bf16[48,2368]{1,0:T(8,128)(2,1)S(1)}, u32[]{:S(2)}, u32[]{:S(2)}) %collective-permute-start.76) | collective-permute-done | bytes 227360 | tf_op jit(solution)/shard_map/ppermute | solution.py:88
  398.3 3.2 collective-permute-done.85
  401.5 4.5 collective-permute-done.86
  437.1 3.5 collective-permute-done.79
  441.4 3.6 collective-permute-done.80
  447.3 3.1 collective-permute-done.81
  458.9 3.0 collective-permute-done.84
  478.2 4.1 multiply_subtract_fusion
  (467 shorter events, 171.2 us)
Async XLA Ops:
  7.2 401.2 %reduce-scatter.8.cloned.1.call-start = ((), (), s32[]{:S(2)}) async-start(), calls=%async_computation.5 | async-start | bytes 3981312 | tf_op jit(solution)/shard_map/reduce_scatter | solution.py:594
  12.7 57.7 %collective-permute-start.26 = (bf16[48,1152]{1,0:T(8,128)(2,1)}, bf16[48,1152]{1,0:T(8,128)(2,1)}, u32[]{:S(2)}, u32[]{:S(2)}) collective-permute-start(bf16[48,1152]{1,0:T(8,128)(2,1)} %fusion.29), channel_id=1, source_target_pairs={{0,2},{1,3},{2,0},{3,1},{4,6},{5,7},{6,4},{7,5},{8,10},{9,11},{10,... | collective-permute-start | bytes 331784 | tf_op jit(solution)/shard_map/ppermute | solution.py:88
  15.7 56.4 %collective-permute-start.27 = (bf16[48,1152]{1,0:T(8,128)(2,1)}, bf16[48,1152]{1,0:T(8,128)(2,1)}, u32[]{:S(2)}, u32[]{:S(2)}) collective-permute-start(bf16[48,1152]{1,0:T(8,128)(2,1)} %fusion.29), channel_id=1, source_target_pairs={{0,4},{1,5},{2,6},{3,7},{4,0},{5,1},{6,2},{7,3},{8,12},{9,13},{10,... | collective-permute-start | bytes 331784 | tf_op jit(solution)/shard_map/ppermute | solution.py:88
  19.1 27.9 %collective-permute-start.4 = (s32[2,6]{1,0:T(2,128)}, s32[2,6]{1,0:T(2,128)}, u32[]{:S(2)}, u32[]{:S(2)}) collective-permute-start(s32[2,6]{1,0:T(2,128)} %pad_add_fusion.1), channel_id=1, source_target_pairs={{0,2},{1,3},{2,0},{3,1},{4,6},{5,7},{6,4},{7,5},{8,10},{9,11},{10,... | collective-permute-start | bytes 152 | tf_op jit(solution)/shard_map/ppermute | solution.py:88
  19.5 27.5 %collective-permute-start.5 = (s32[2,6]{1,0:T(2,128)}, s32[2,6]{1,0:T(2,128)}, u32[]{:S(2)}, u32[]{:S(2)}) collective-permute-start(s32[2,6]{1,0:T(2,128)} %pad_add_fusion.1), channel_id=1, source_target_pairs={{0,4},{1,5},{2,6},{3,7},{4,0},{5,1},{6,2},{7,3},{8,12},{9,13},{10,... | collective-permute-start | bytes 152 | tf_op jit(solution)/shard_map/ppermute | solution.py:88
  19.6 28.1 %collective-permute-start.6 = (s32[2,6]{1,0:T(2,128)}, s32[2,6]{1,0:T(2,128)}, u32[]{:S(2)}, u32[]{:S(2)}) collective-permute-start(s32[2,6]{1,0:T(2,128)} %pad_add_fusion.1), channel_id=1, source_target_pairs={{0,6},{1,7},{2,4},{3,5},{4,2},{5,3},{6,0},{7,1},{8,14},{9,15},{10,... | collective-permute-start | bytes 152 | tf_op jit(solution)/shard_map/ppermute | solution.py:88
  81.0 22.7 %collective-permute-start.30 = (bf16[4,48,1152]{2,1,0:T(8,128)(2,1)S(1)}, bf16[4,48,1152]{2,1,0:T(8,128)(2,1)}, u32[]{:S(2)}, u32[]{:S(2)}) collective-permute-start(bf16[4,48,1152]{2,1,0:T(8,128)(2,1)S(1)} %pad_maximum_fusion.2.rest_0_.rest_8_), channel_id=1, source_target_pairs={{0,16},{8,24},{16,0},{24,8},{1,17},{9,25},{17,1},{25,9},{2,18},{10... | collective-permute-start | bytes 1327112 | tf_op jit(solution)/shard_map/ppermute | solution.py:88
  90.0 19.6 %collective-permute-start.32 = (bf16[4,48,1152]{2,1,0:T(8,128)(2,1)S(1)}, bf16[4,48,1152]{2,1,0:T(8,128)(2,1)S(1)}, u32[]{:S(2)}, u32[]{:S(2)}) collective-permute-start(bf16[4,48,1152]{2,1,0:T(8,128)(2,1)S(1)} %pad_maximum_fusion.2.rest_0_.rest_8_), channel_id=1, source_target_pairs={{0,1},{1,0},{2,3},{3,2},{4,5},{5,4},{6,7},{7,6},{8,9},{9,8},{10,11... | collective-permute-start | bytes 1327112 | tf_op jit(solution)/shard_map/ppermute | solution.py:88
  90.1 21.0 %collective-permute-start.19 = (bf16[4,48,1152]{2,1,0:T(8,128)(2,1)S(1)}, bf16[4,48,1152]{2,1,0:T(8,128)(2,1)S(1)}, u32[]{:S(2)}, u32[]{:S(2)}) collective-permute-start(bf16[4,48,1152]{2,1,0:T(8,128)(2,1)S(1)} %pad_maximum_fusion.1.rest_0_.rest_8_), channel_id=1, source_target_pairs={{0,8},{8,0},{16,24},{24,16},{1,9},{9,1},{17,25},{25,17},{2,10},{10... | collective-permute-start | bytes 1327112 | tf_op jit(solution)/shard_map/ppermute | solution.py:88
  91.3 30.0 %collective-permute-start.20 = (bf16[4,48,1152]{2,1,0:T(8,128)(2,1)S(1)}, bf16[4,48,1152]{2,1,0:T(8,128)(2,1)S(1)}, u32[]{:S(2)}, u32[]{:S(2)}) collective-permute-start(bf16[4,48,1152]{2,1,0:T(8,128)(2,1)S(1)} %pad_maximum_fusion.1.rest_0_.rest_8_), channel_id=1, source_target_pairs={{0,16},{8,24},{16,0},{24,8},{1,17},{9,25},{17,1},{25,9},{2,18},{10... | collective-permute-start | bytes 1327112 | tf_op jit(solution)/shard_map/ppermute | solution.py:88
  127.2 27.2 %collective-permute-start.40 = (bf16[4,48,1152]{2,1,0:T(8,128)(2,1)S(1)}, bf16[4,48,1152]{2,1,0:T(8,128)(2,1)}, u32[]{:S(2)}, u32[]{:S(2)}) collective-permute-start(bf16[4,48,1152]{2,1,0:T(8,128)(2,1)S(1)} %pad_maximum_fusion.3.rest_0_), channel_id=1, source_target_pairs={{0,16},{8,24},{16,0},{24,8},{1,17},{9,25},{17,1},{25,9},{2,18},{10... | collective-permute-start | bytes 1327112 | tf_op jit(solution)/shard_map/ppermute | solution.py:88
  133.9 31.6 %collective-permute-start.41 = (bf16[4,48,1152]{2,1,0:T(8,128)(2,1)S(1)}, bf16[4,48,1152]{2,1,0:T(8,128)(2,1)}, u32[]{:S(2)}, u32[]{:S(2)}) collective-permute-start(bf16[4,48,1152]{2,1,0:T(8,128)(2,1)S(1)} %pad_maximum_fusion.3.rest_0_), channel_id=1, source_target_pairs={{0,24},{8,16},{16,8},{24,0},{1,25},{9,17},{17,9},{25,1},{2,26},{10... | collective-permute-start | bytes 1327112 | tf_op jit(solution)/shard_map/ppermute | solution.py:88
  135.4 30.2 %collective-permute-start.33 = (bf16[4,48,1152]{2,1,0:T(8,128)(2,1)S(1)}, bf16[4,48,1152]{2,1,0:T(8,128)(2,1)S(1)}, u32[]{:S(2)}, u32[]{:S(2)}) collective-permute-start(bf16[4,48,1152]{2,1,0:T(8,128)(2,1)S(1)} %collective-permute-done.29.rest_1_.rest_9_), channel_id=1, source_target_pairs={{0,1},{1,0},{2,3},{3,2},{4,5},{5,4},{6,7},{7,6},{8,9},{9,8},{10,11... | collective-permute-start | bytes 1327112 | tf_op jit(solution)/shard_map/ppermute | solution.py:88
  135.4 30.6 %collective-permute-start.34 = (bf16[4,48,1152]{2,1,0:T(8,128)(2,1)}, bf16[4,48,1152]{2,1,0:T(8,128)(2,1)S(1)}, u32[]{:S(2)}, u32[]{:S(2)}) collective-permute-start(bf16[4,48,1152]{2,1,0:T(8,128)(2,1)} %collective-permute-done.30.rest_2_.rest_10_), channel_id=1, source_target_pairs={{0,1},{1,0},{2,3},{3,2},{4,5},{5,4},{6,7},{7,6},{8,9},{9,8},{10,11... | collective-permute-start | bytes 1327112 | tf_op jit(solution)/shard_map/ppermute | solution.py:88
  136.0 30.2 %collective-permute-start.35 = (bf16[4,48,1152]{2,1,0:T(8,128)(2,1)}, bf16[4,48,1152]{2,1,0:T(8,128)(2,1)S(1)}, u32[]{:S(2)}, u32[]{:S(2)}) collective-permute-start(bf16[4,48,1152]{2,1,0:T(8,128)(2,1)} %copy-done.42), channel_id=1, source_target_pairs={{0,1},{1,0},{2,3},{3,2},{4,5},{5,4},{6,7},{7,6},{8,9},{9,8},{10,11... | collective-permute-start | bytes 1327112 | tf_op jit(solution)/shard_map/ppermute | solution.py:88
  154.5 31.4 %collective-permute-start.42 = (bf16[4,48,1152]{2,1,0:T(8,128)(2,1)S(1)}, bf16[4,48,1152]{2,1,0:T(8,128)(2,1)S(1)}, u32[]{:S(2)}, u32[]{:S(2)}) collective-permute-start(bf16[4,48,1152]{2,1,0:T(8,128)(2,1)S(1)} %pad_maximum_fusion.3.rest_0_), channel_id=1, source_target_pairs={{0,1},{1,0},{2,3},{3,2},{4,5},{5,4},{6,7},{7,6},{8,9},{9,8},{10,11... | collective-permute-start | bytes 1327112 | tf_op jit(solution)/shard_map/ppermute | solution.py:88
  165.5 20.4 %collective-permute-start.43 = (bf16[4,48,1152]{2,1,0:T(8,128)(2,1)}, bf16[4,48,1152]{2,1,0:T(8,128)(2,1)S(1)}, u32[]{:S(2)}, u32[]{:S(2)}) collective-permute-start(bf16[4,48,1152]{2,1,0:T(8,128)(2,1)} %collective-permute-done.39.rest_1_), channel_id=1, source_target_pairs={{0,1},{1,0},{2,3},{3,2},{4,5},{5,4},{6,7},{7,6},{8,9},{9,8},{10,11... | collective-permute-start | bytes 1327112 | tf_op jit(solution)/shard_map/ppermute | solution.py:88
  165.6 20.3 %collective-permute-start.44 = (bf16[4,48,1152]{2,1,0:T(8,128)(2,1)}, bf16[4,48,1152]{2,1,0:T(8,128)(2,1)S(1)}, u32[]{:S(2)}, u32[]{:S(2)}) collective-permute-start(bf16[4,48,1152]{2,1,0:T(8,128)(2,1)} %collective-permute-done.40.rest_2_), channel_id=1, source_target_pairs={{0,1},{1,0},{2,3},{3,2},{4,5},{5,4},{6,7},{7,6},{8,9},{9,8},{10,11... | collective-permute-start | bytes 1327112 | tf_op jit(solution)/shard_map/ppermute | solution.py:88
  166.0 19.9 %collective-permute-start.45 = (bf16[4,48,1152]{2,1,0:T(8,128)(2,1)}, bf16[4,48,1152]{2,1,0:T(8,128)(2,1)S(1)}, u32[]{:S(2)}, u32[]{:S(2)}) collective-permute-start(bf16[4,48,1152]{2,1,0:T(8,128)(2,1)} %collective-permute-done.41.rest_3_), channel_id=1, source_target_pairs={{0,1},{1,0},{2,3},{3,2},{4,5},{5,4},{6,7},{7,6},{8,9},{9,8},{10,11... | collective-permute-start | bytes 1327112 | tf_op jit(solution)/shard_map/ppermute | solution.py:88
  213.9 199.8 %reduce-scatter.6.cloned.1.call-start = ((), (), s32[]{:S(2)}) async-start(), calls=%async_computation.4 | async-start | bytes 3981312 | tf_op jit(solution)/shard_map/reduce_scatter | solution.py:594
  235.2 181.7 %reduce-scatter.4.cloned.1.call-start = ((), (), s32[]{:S(2)}) async-start(), calls=%async_computation.3 | async-start | bytes 3981312 | tf_op jit(solution)/shard_map/reduce_scatter | solution.py:594
  256.9 46.4 %collective-permute-start.55 = (bf16[6,2304]{1,0:T(8,128)(2,1)S(1)}, bf16[6,2304]{1,0:T(8,128)(2,1)S(1)}, u32[]{:S(2)}, u32[]{:S(2)}) collective-permute-start(bf16[6,2304]{1,0:T(8,128)(2,1)S(1)} %bitcast.326), channel_id=1, source_target_pairs={{0,2},{1,3},{2,0},{3,1},{4,6},{5,7},{6,4},{7,5},{8,10},{9,11},{10,... | collective-permute-start | bytes 82952 | tf_op jit(solution)/shard_map/ppermute | solution.py:88
  275.9 27.5 %collective-permute-start.56 = (bf16[6,2304]{1,0:T(8,128)(2,1)S(1)}, bf16[6,2304]{1,0:T(8,128)(2,1)S(1)}, u32[]{:S(2)}, u32[]{:S(2)}) collective-permute-start(bf16[6,2304]{1,0:T(8,128)(2,1)S(1)} %bitcast.327), channel_id=1, source_target_pairs={{0,4},{1,5},{2,6},{3,7},{4,0},{5,1},{6,2},{7,3},{8,12},{9,13},{10,... | collective-permute-start | bytes 82952 | tf_op jit(solution)/shard_map/ppermute | solution.py:88
  303.3 39.8 %collective-permute-start.61 = (bf16[6,2304]{1,0:T(8,128)(2,1)S(1)}, bf16[6,2304]{1,0:T(8,128)(2,1)S(1)}, u32[]{:S(2)}, u32[]{:S(2)}) collective-permute-start(bf16[6,2304]{1,0:T(8,128)(2,1)S(1)} %bitcast.332), channel_id=1, source_target_pairs={{0,6},{1,7},{2,4},{3,5},{4,2},{5,3},{6,0},{7,1},{8,14},{9,15},{10,... | collective-permute-start | bytes 82952 | tf_op jit(solution)/shard_map/ppermute | solution.py:88
  303.5 41.0 %collective-permute-start.63 = (bf16[6,3072]{1,0:T(8,128)(2,1)S(1)}, bf16[6,3072]{1,0:T(8,128)(2,1)S(1)}, u32[]{:S(2)}, u32[]{:S(2)}) collective-permute-start(bf16[6,3072]{1,0:T(8,128)(2,1)S(1)} %bitcast.322), channel_id=1, source_target_pairs={{0,2},{1,3},{2,0},{3,1},{4,6},{5,7},{6,4},{7,5},{8,10},{9,11},{10,... | collective-permute-start | bytes 110600 | tf_op jit(solution)/shard_map/ppermute | solution.py:88
  304.1 41.5 %collective-permute-start.64 = (bf16[6,3072]{1,0:T(8,128)(2,1)S(1)}, bf16[6,3072]{1,0:T(8,128)(2,1)S(1)}, u32[]{:S(2)}, u32[]{:S(2)}) collective-permute-start(bf16[6,3072]{1,0:T(8,128)(2,1)S(1)} %bitcast.323), channel_id=1, source_target_pairs={{0,4},{1,5},{2,6},{3,7},{4,0},{5,1},{6,2},{7,3},{8,12},{9,13},{10,... | collective-permute-start | bytes 110600 | tf_op jit(solution)/shard_map/ppermute | solution.py:88
  307.9 37.7 %collective-permute-start.65 = (bf16[6,3072]{1,0:T(8,128)(2,1)S(1)}, bf16[6,3072]{1,0:T(8,128)(2,1)S(1)}, u32[]{:S(2)}, u32[]{:S(2)}) collective-permute-start(bf16[6,3072]{1,0:T(8,128)(2,1)S(1)} %bitcast.324), channel_id=1, source_target_pairs={{0,6},{1,7},{2,4},{3,5},{4,2},{5,3},{6,0},{7,1},{8,14},{9,15},{10,... | collective-permute-start | bytes 110600 | tf_op jit(solution)/shard_map/ppermute | solution.py:88
  307.9 37.7 %collective-permute-start.71 = (f32[4,48,128]{2,1,0:T(8,128)S(1)}, f32[4,48,128]{2,1,0:T(8,128)S(1)}, u32[]{:S(2)}, u32[]{:S(2)}) collective-permute-start(f32[4,48,128]{2,1,0:T(8,128)S(1)} %dynamic-slice_bitcast_fusion.9), channel_id=1, source_target_pairs={{0,1},{1,0},{2,3},{3,2},{4,5},{5,4},{6,7},{7,6},{8,9},{9,8},{10,11... | collective-permute-start | bytes 294920 | tf_op jit(solution)/shard_map/ppermute | solution.py:88
  424.5 42.6 %collective-permute-start.94 = (bf16[48,1152]{1,0:T(8,128)(2,1)S(1)}, bf16[48,1152]{1,0:T(8,128)(2,1)S(1)}, u32[]{:S(2)}, u32[]{:S(2)}) collective-permute-start(bf16[48,1152]{1,0:T(8,128)(2,1)S(1)} %get-tuple-element.89), channel_id=1, source_target_pairs={{0,8},{8,0},{16,24},{24,16},{1,9},{9,1},{17,25},{25,17},{2,10},{10... | collective-permute-start | bytes 331784 | tf_op jit(solution)/shard_map/ppermute | solution.py:88
  425.2 43.4 %collective-permute-start.95 = (bf16[48,1152]{1,0:T(8,128)(2,1)S(1)}, bf16[48,1152]{1,0:T(8,128)(2,1)S(1)}, u32[]{:S(2)}, u32[]{:S(2)}) collective-permute-start(bf16[48,1152]{1,0:T(8,128)(2,1)S(1)} %get-tuple-element.89), channel_id=1, source_target_pairs={{0,16},{8,24},{16,0},{24,8},{1,17},{9,25},{17,1},{25,9},{2,18},{10... | collective-permute-start | bytes 331784 | tf_op jit(solution)/shard_map/ppermute | solution.py:88
  428.2 41.1 %collective-permute-start.96 = (bf16[48,1152]{1,0:T(8,128)(2,1)S(1)}, bf16[48,1152]{1,0:T(8,128)(2,1)S(1)}, u32[]{:S(2)}, u32[]{:S(2)}) collective-permute-start(bf16[48,1152]{1,0:T(8,128)(2,1)S(1)} %get-tuple-element.89), channel_id=1, source_target_pairs={{0,24},{8,16},{16,8},{24,0},{1,25},{9,17},{17,9},{25,1},{2,26},{10... | collective-permute-start | bytes 331784 | tf_op jit(solution)/shard_map/ppermute | solution.py:88
  429.6 41.3 %collective-permute-start.91 = (bf16[48,1152]{1,0:T(8,128)(2,1)S(1)}, bf16[48,1152]{1,0:T(8,128)(2,1)S(1)}, u32[]{:S(2)}, u32[]{:S(2)}) collective-permute-start(bf16[48,1152]{1,0:T(8,128)(2,1)S(1)} %get-tuple-element.91), channel_id=1, source_target_pairs={{0,8},{8,0},{16,24},{24,16},{1,9},{9,1},{17,25},{25,17},{2,10},{10... | collective-permute-start | bytes 331784 | tf_op jit(solution)/shard_map/ppermute | solution.py:88
  (124 other events, 1594.4 us)
Sparse Core Ops, SparseCore 0:
  214.0 90.3 reduce-scatter.7
  306.9 49.9 reduce-scatter.5
  359.2 49.4 reduce-scatter.3

commit v2 on v1

v2 whole, which is shorter than its diff:
```python
import functools
import math

import jax
import jax.numpy as jnp
import numpy as np
from jax import lax
from jax.experimental import pallas as pl
from jax.experimental.pallas import tpu as pltpu
from jax.sharding import PartitionSpec as P

D = 384
HEADS = 6
HDIM = 64
FF = 1536
NTOK = 256
PIN = 16
FREQ = 256
CLASSES = 1000
TSTEPS = 1000
STEP = 10
POUT = 32

beta_one = 0.9
beta_two = 0.999
adam_eps = 1e-08
learn_rate = 0.05
weight_decay = 0.1
clip_level = 0.005
ln_eps = 1e-06

F32 = jnp.float32
BF16 = jnp.bfloat16
STRIDE = 10 * D + FF
TOKW = 3 * D + D + FF + FF
CHUNKS = 4
CW = TOKW // CHUNKS
GELU_C = math.sqrt(2.0 / math.pi)
VMEM_LIMIT = 60 * 1024 * 1024


def plan_table():
    j = np.arange(TSTEPS, dtype=np.float64)
    beta = 0.0001 + (0.02 - 0.0001) * j / (TSTEPS - 1)
    abar = np.cumprod(1.0 - beta)
    prev = np.concatenate([[1.0], abar[:-1]])
    out = np.zeros((TSTEPS, 5), np.float64)
    out[:, 0] = np.sqrt(abar)
    out[:, 1] = np.sqrt(1.0 - abar)
    out[1:, 2] = np.log(beta[1:])
    out[1:, 3] = np.log(beta[1:] * (1.0 - prev[1:]) / (1.0 - abar[1:]))
    out[1:, 4] = prev[1:] * beta[1:] ** 2 / ((1.0 - abar[1:]) * abar[1:])
    full = np.zeros((TSTEPS, 128), np.float32)
    full[:, 0:2] = out[:, 0:2]
    for k in range(3):
        left = out[:, 2 + k].astype(np.float32)
        for part in range(3):
            full[:, 8 + 3 * k + part] = bf16_of(left)
            left = left - full[:, 8 + 3 * k + part]
    return full


def bf16_of(val):
    return val.astype(jnp.bfloat16).astype(np.float32)


def feature_table():
    half = FREQ // 2
    rates = np.exp(-math.log(10000.0) * np.arange(half) / half)
    angles = np.arange(1024)[:, None] * rates[None, :]
    return np.concatenate([np.cos(angles), np.sin(angles)], axis=1).astype(jnp.bfloat16)


def position_table():
    half = D // 2
    rates = np.exp(-math.log(10000.0) * 2.0 * np.arange(half) / D)
    angles = np.arange(NTOK)[:, None] * rates[None, :]
    return np.concatenate([np.sin(angles), np.cos(angles)], axis=1).astype(np.float32)


def stages(size, pair_first):
    out, stride = [], 1
    if pair_first and size % 2 == 0:
        out.append((1, 2))
        stride, size = 2, size // 2
    while size > 1:
        step = 4 if size % 4 == 0 else 2
        out.append((stride, step))
        stride, size = stride * step, size // step
    return out


def axis_stages(axis):
    return stages(lax.axis_size(axis), axis == "fsdp")


def swap(val, axis, mask):
    size = lax.axis_size(axis)
    return lax.ppermute(val, axis, [(i, i ^ mask) for i in range(size)])


def place(axis, stride, size):
    return (lax.axis_index(axis) // stride) % size


def in_order(parts, pos):
    size = len(parts)
    if size == 2:
        return jnp.stack([lax.select(pos == 1, parts[1 - j], parts[j]) for j in range(2)])
    return jnp.stack([lax.select_n(pos, *[parts[j ^ p] for p in range(size)]) for j in range(size)])


def gather_open(val, axis, level):
    stride, size = list(reversed(axis_stages(axis)))[level]
    return [val] + [swap(val, axis, k * stride) for k in range(1, size)]


def gather_close(parts, axis, level):
    stride, size = list(reversed(axis_stages(axis)))[level]
    return in_order(parts, place(axis, stride, size))


def gather_shape(val, axis, shape):
    n = len(axis_stages(axis))
    order = tuple(reversed(range(n))) + tuple(range(n, n + len(shape)))
    return val.transpose(order).reshape((lax.axis_size(axis),) + shape)


def gather(val, axis):
    shape = val.shape
    for level in range(len(axis_stages(axis))):
        val = gather_close(gather_open(val, axis, level), axis, level)
    return gather_shape(val, axis, shape)


def reduce_stage(val, dim, axis, stride, size, send_type):
    pos = place(axis, stride, size)
    total = lax.dynamic_index_in_dim(val, pos, dim, keepdims=False).astype(F32)
    for k in range(1, size):
        piece = lax.dynamic_index_in_dim(val, pos ^ k, dim, keepdims=False)
        total = total + swap(piece.astype(send_type), axis, k * stride).astype(F32)
    return total


def reduce_open(val, axis, send_type):
    plan = axis_stages(axis)
    sizes = [s for _, s in reversed(plan)]
    val = val.reshape(tuple(sizes) + val.shape[1:])
    for dim in range(len(sizes) - 1, 0, -1):
        stride, size = plan[len(sizes) - 1 - dim]
        val = reduce_stage(val, dim, axis, stride, size, send_type)
    stride, size = plan[-1]
    pos = place(axis, stride, size)
    out = [lax.dynamic_index_in_dim(val, pos ^ k, 0, keepdims=False) for k in range(size)]
    return [out[0]] + [swap(out[k].astype(send_type), axis, k * stride) for k in range(1, size)]


def total_of(parts):
    return sum(p.astype(F32) for p in parts)


def reduce_parts(val, axis, send_type):
    return total_of(reduce_open(val, axis, send_type))


def after(val, *deps):
    return lax.optimization_barrier((val,) + deps)[0]


def tie(parts, *deps):
    return list(lax.optimization_barrier(tuple(parts) + deps)[: len(parts)])


def sum_all(val, axes):
    for axis in axes:
        for stride, size in axis_stages(axis):
            parts = [val] + [swap(val, axis, k * stride) for k in range(1, size)]
            while len(parts) > 1:
                parts = [parts[i] + parts[i + 1] for i in range(0, len(parts), 2)]
            val = parts[0]
    return val


def small_mesh(rows):
    return rows == 48 and lax.axis_size("dp") == CHUNKS and lax.axis_size("fsdp") == 8


def gather_z(whole):
    width = whole.shape[1] // CHUNKS
    chunk = lax.dynamic_slice_in_dim(whole, lax.axis_index("dp") * width, width, 1)
    parts = [chunk] + [swap(chunk, "fsdp", 2 * k) for k in (1, 2, 3)]
    return in_order(parts, place("fsdp", 2, 4))


def gather_dp(mine):
    return jnp.stack([mine] + [swap(mine, "dp", k) for k in (1, 2, 3)])


def gather_core(mine):
    return [mine, swap(mine, "fsdp", 1)]


def gather_whole(whole):
    return [lax.all_gather(whole, "fsdp", axis=0, tiled=True)]


def dot(a, b):
    return jnp.dot(a, b, preferred_element_type=F32)


def dot_nt(a, b):
    return lax.dot_general(a, b, (((1,), (1,)), ((), ())), preferred_element_type=F32)


def dot_tn(a, b):
    return lax.dot_general(a, b, (((0,), (0,)), ((), ())), preferred_element_type=F32)


def layer_norm(v):
    c = v - jnp.mean(v, axis=-1, keepdims=True)
    r = lax.rsqrt(jnp.mean(c * c, axis=-1, keepdims=True) + ln_eps)
    return c * r, r


def norm_grad(dm, y, r, scale):
    dy = dm * (1.0 + scale)
    dv = r * (dy - jnp.mean(dy, axis=-1, keepdims=True) - y * jnp.mean(dy * y, axis=-1, keepdims=True))
    return dv, jnp.sum(dm, axis=0, keepdims=True), jnp.sum(dm * y, axis=0, keepdims=True)


def wpart(w, j, lo, hi):
    if len(w.shape) == 2:
        width = w.shape[1] // CHUNKS
        return w[:, j * width + lo : j * width + hi]
    return w[j, :, :, :, lo:hi].reshape(D, hi - lo)


def head_masks():
    lane = lax.broadcasted_iota(jnp.int32, (1, 2 * HDIM), 1)
    low = (lane < HDIM).astype(F32)
    return low, 1.0 - low


def block_forward(h, mod, w, bias, sv):
    qkv_ref, p_ref, o_ref, g_ref, gp_ref, att_ref, mlp_ref, h2_ref = sv
    y1, _ = layer_norm(h)
    n1 = (y1 * (1.0 + mod(1)) + mod(0)).astype(BF16)
    qkv_ref[...] = dot(n1, wpart(w, 0, 0, CW)).astype(BF16)
    masks = head_masks()
    for j in range(3):
        q2 = qkv_ref[:, 128 * j : 128 * j + 128]
        k2 = qkv_ref[:, D + 128 * j : D + 128 * j + 128]
        v2 = qkv_ref[:, 2 * D + 128 * j : 2 * D + 128 * j + 128]
        o2 = None
        for a in range(2):
            s = dot_nt(q2, k2 * (masks[a] * 0.125).astype(BF16))
            if bias is not None:
                s = s + bias
            e = jnp.exp(s - jnp.max(s, axis=-1, keepdims=True))
            p = (e * (1.0 / jnp.sum(e, axis=-1, keepdims=True))).astype(BF16)
            p_ref[2 * j + a] = p
            part = dot(p, v2 * masks[a].astype(BF16))
            o2 = part if o2 is None else o2 + part
        o_ref[:, 128 * j : 128 * j + 128] = o2.astype(BF16)
    att = dot(o_ref[...], wpart(w, 1, 0, D))
    att_ref[...] = att.astype(BF16)
    h2 = h + mod(2) * att
    h2_ref[...] = h2
    y2, _ = layer_norm(h2)
    n2 = (y2 * (1.0 + mod(4)) + mod(3)).astype(BF16)
    for j, lo, hi, at in ((1, D, CW, 0), (2, 0, 2 * D, 2 * D)):
        u = dot(n2, wpart(w, j, lo, hi))
        u2 = u * u
        t = jnp.tanh(u * (GELU_C + (GELU_C * 0.044715) * u2))
        half = 0.5 * t + 0.5
        g_ref[:, at : at + 2 * D] = (u * half).astype(BF16)
        gp = half + (u * (0.5 - 0.5 * t * t)) * (GELU_C + (3.0 * GELU_C * 0.044715) * u2)
        gp_ref[:, at : at + 2 * D] = gp.astype(BF16)
    mlp = dot_nt(g_ref[:, 0:D], wpart(w, 2, 2 * D, CW)) + dot_nt(g_ref[:, D:], wpart(w, 3, 0, CW))
    mlp_ref[...] = mlp.astype(BF16)
    return h2 + mod(5) * mlp


def block_backward(d3, h, mod, w, sv, dw, du_ref, dqkv_ref, dmod):
    qkv_ref, p_ref, o_ref, g_ref, gp_ref, att_ref, mlp_ref, h2_ref = sv
    dmlp = (d3 * mod(5)).astype(BF16)
    dmod(5, jnp.sum(d3 * mlp_ref[...].astype(F32), axis=0, keepdims=True))
    du_ref[:, 0:D] = (dot(dmlp, wpart(w, 2, 2 * D, CW)) * gp_ref[:, 0:D].astype(F32)).astype(BF16)
    du_ref[:, D:] = (dot(dmlp, wpart(w, 3, 0, CW)) * gp_ref[:, D:].astype(F32)).astype(BF16)
    dw[2, :, 2 * D : CW] += dot_tn(dmlp, g_ref[:, 0:D])
    dw[3, :, 0:CW] += dot_tn(dmlp, g_ref[:, D:])
    dn2 = dot_nt(du_ref[:, 0 : 2 * D], wpart(w, 1, D, CW)) + dot_nt(du_ref[:, 2 * D :], wpart(w, 2, 0, 2 * D))
    y2, r2 = layer_norm(h2_ref[...])
    n2 = (y2 * (1.0 + mod(4)) + mod(3)).astype(BF16)
    dw[1, :, D:CW] += dot_tn(n2, du_ref[:, 0 : 2 * D])
    dw[2, :, 0 : 2 * D] += dot_tn(n2, du_ref[:, 2 * D :])
    dv, dshift, dscale = norm_grad(dn2, y2, r2, mod(4))
    dmod(3, dshift)
    dmod(4, dscale)
    d2 = d3 + dv
    datt = (d2 * mod(2)).astype(BF16)
    dmod(2, jnp.sum(d2 * att_ref[...].astype(F32), axis=0, keepdims=True))
    do = dot_nt(datt, wpart(w, 1, 0, D)).astype(BF16)
    dw[1, :, 0:D] += dot_tn(o_ref[...], datt)
    masks = head_masks()
    for j in range(3):
        q2 = qkv_ref[:, 128 * j : 128 * j + 128]
        k2 = qkv_ref[:, D + 128 * j : D + 128 * j + 128]
        v2 = qkv_ref[:, 2 * D + 128 * j : 2 * D + 128 * j + 128]
        do2 = do[:, 128 * j : 128 * j + 128]
        dq2, dk2, dv2 = 0.0, 0.0, 0.0
        for a in range(2):
            one = masks[a].astype(BF16)
            eighth = (masks[a] * 0.125).astype(BF16)
            pb = p_ref[2 * j + a]
            p = pb.astype(F32)
            dp = dot_nt(do2, v2 * one)
            ds = (p * (dp - jnp.sum(p * dp, axis=-1, keepdims=True))).astype(BF16)
            dq2 += dot(ds, k2 * eighth)
            dk2 += dot_tn(ds, q2 * eighth)
            dv2 += dot_tn(pb, do2 * one)
        dqkv_ref[:, 128 * j : 128 * j + 128] = dq2.astype(BF16)
        dqkv_ref[:, D + 128 * j : D + 128 * j + 128] = dk2.astype(BF16)
        dqkv_ref[:, 2 * D + 128 * j : 2 * D + 128 * j + 128] = dv2.astype(BF16)
    dn1 = dot_nt(dqkv_ref[...], wpart(w, 0, 0, CW))
    y1, r1 = layer_norm(h)
    n1 = (y1 * (1.0 + mod(1)) + mod(0)).astype(BF16)
    dw[0, :, 0:CW] += dot_tn(n1, dqkv_ref[...])
    dv, dshift, dscale = norm_grad(dn1, y1, r1, mod(1))
    dmod(0, dshift)
    dmod(1, dscale)
    return d2 + dv


def load_weights(ids, pieces, w, sems, base=0):
    @pl.when(pl.program_id(0) == 0)
    def _():
        copies = []
        if len(pieces) == 1:
            copies.append(pltpu.make_async_copy(pieces[0].at[:, base : base + w.shape[1]], w, sems.at[0]))
        else:
            for c in range(2):
                for k in range(4):
                    target = w.at[ids[1] ^ k, :, ids[2] ^ c]
                    copies.append(pltpu.make_async_copy(pieces[c].at[k], target, sems.at[4 * c + k]))
        for copy in copies:
            copy.start()
        for copy in copies:
            copy.wait()


def mod_row(mods, base, step):
    return lambda i: mods[pl.ds(step, 1), base + D * i : base + D * i + D]


def row_writer(dmod, step):
    def write(i, val):
        dmod[pl.ds(step, 1), D * i : D * i + D] = val

    return write


def token_row(misc):
    lane = lax.broadcasted_iota(jnp.int32, (8, 128), 1)
    return dot_nt((lane == PIN).astype(BF16), misc[...])[0:1, :]


def enc_forward_kernel(n, ids, xin, pe, mods, bias, *rest):
    pieces, (misc, h0, h3), sv, (w, sems) = rest[:n], rest[n : n + 3], rest[n + 3 : n + 11], rest[n + 11 :]
    load_weights(ids, pieces, w, sems)
    step = pl.program_id(0)

    @pl.when(step == 0)
    def _():
        misc[...] = wpart(w, 0, CW, CW + 128)

    @pl.when(step < ids[0])
    def _():
        h = dot_nt(xin[...], misc[...]) + pe[...]
        h0[...] = h
        h3[...] = block_forward(h, mod_row(mods, 0, step), w, bias[...], sv)


def side_forward_kernel(n, ids, h_in, mask, pe, misc, mods, *rest):
    pieces, (hs, h3), sv, (w, sems) = rest[:n], rest[n : n + 2], rest[n + 2 : n + 10], rest[n + 10 :]
    load_weights(ids, pieces, w, sems)
    step = pl.program_id(0)

    @pl.when(step < ids[0])
    def _():
        m = mask[...]
        h = h_in[...] * (1.0 - m) + m * (token_row(misc) + pe[...])
        hs[...] = h
        h3[...] = block_forward(h, mod_row(mods, 0, step), w, None, sv)


def store_grads(ids, dw, outs):
    if len(outs) == 1:
        for j in range(CHUNKS):
            outs[0][j] = dw[j].astype(BF16)
        return
    for side in range(2):
        for z in range(4):
            at = pl.multiple_of((2 * z + (ids[2] ^ side)) * (D // 8), 16)
            for j in range(CHUNKS):
                outs[side][j, z] = dw[j, pl.ds(at, D // 8), :].astype(BF16)


def dec_kernel(n, m, ids, coef, h_in, noise, misc, mods, *rest):
    pieces = rest[:n]
    d_in, dmod, dmisc, loss = rest[n : n + 4]
    dw_out = rest[n + 4 : n + 4 + m]
    w, sems, dw, du, dqkv = rest[n + 4 + m : n + 9 + m]
    sv = rest[n + 9 + m :]
    load_weights(ids, pieces, w, sems, TOKW)
    step = pl.program_id(0)

    @pl.when(step == 0)
    def _():
        dw[...] = jnp.zeros_like(dw)
        dmisc[...] = jnp.zeros_like(dmisc)
        loss[...] = jnp.zeros_like(loss)
        dmod[...] = jnp.zeros_like(dmod)

    @pl.when(step < ids[0])
    def _():
        row = mod_row(mods, 6 * D, step)
        put = row_writer(dmod, step)
        h = h_in[...]
        h_dec = block_forward(h, row, w, None, sv)
        yf, rf = layer_norm(h_dec)
        nf = (yf * (1.0 + row(7)) + row(6)).astype(BF16)
        out = dot(nf, misc[...])
        ln_b, ln_pv, wmean = coef[step, 0], coef[step, 1], coef[step, 2]
        lane = lax.broadcasted_iota(jnp.int32, (1, 128), 1)
        live = (lane >= 32) & (lane < 32 + PIN)
        d = jnp.where(live, out - noise[...], 0.0)
        vf = (pltpu.roll(out, 128 - 32, 1) + 1.0) * 0.5
        vf = jnp.where(live, vf, 0.0)
        lv = vf * ln_b + (1.0 - vf) * ln_pv
        first = jnp.exp(ln_pv - lv)
        second = wmean * jnp.exp(-lv)
        inv = 0.5 / math.log(2.0)
        dd = d * d
        kl = inv * (-1.0 + lv - ln_pv + first + dd * second)
        term = jnp.where(live, dd + kl, 0.0)
        loss[...] += jnp.sum(term.reshape(NTOK // 8, 8, 128), axis=0)
        deps = d * (2.0 + (2.0 * inv) * second)
        dlog = inv * (1.0 - first - dd * second) * (0.5 * (ln_b - ln_pv))
        dlog = jnp.where(live, dlog, 0.0)
        dout = (deps + pltpu.roll(dlog, 32, 1)).astype(BF16)
        dmisc[...] += dot_tn(nf, dout)
        dnf = dot_nt(dout, misc[...])
        d3, dshift, dscale = norm_grad(dnf, yf, rf, row(7))
        put(6, dshift)
        put(7, dscale)
        d_in[...] = block_backward(d3, h, row, w, sv, dw, du, dqkv, put)

    @pl.when(step == pl.num_programs(0) - 1)
    def _():
        store_grads(ids, dw, dw_out)


def side_backward_kernel(n, m, ids, d_out, h_in, mask, mods, *rest):
    sv, pieces, rest = rest[:8], rest[8 : 8 + n], rest[8 + n :]
    d_enc, dmod, dtok = rest[:3]
    dw_out = rest[3 : 3 + m]
    w, sems, dw, du, dqkv = rest[3 + m :]
    load_weights(ids, pieces, w, sems)
    step = pl.program_id(0)

    @pl.when(step == 0)
    def _():
        dw[...] = jnp.zeros_like(dw)
        dtok[...] = jnp.zeros_like(dtok)
        dmod[...] = jnp.zeros_like(dmod)

    @pl.when(step < ids[0])
    def _():
        hidden = mask[...]
        dh = block_backward(d_out[...], h_in[...], mod_row(mods, 0, step), w, sv, dw, du, dqkv, row_writer(dmod, step))
        dm = dh * hidden
        dtok[...] += jnp.sum(dm.reshape(NTOK // 8, 8, D), axis=0)
        d_enc[...] = dh - dm

    @pl.when(step == pl.num_programs(0) - 1)
    def _():
        store_grads(ids, dw, dw_out)


def enc_backward_kernel(n, m, ids, d_out, h_in, xin, mods, dmisc, dtok, *rest):
    sv, pieces, rest = rest[:8], rest[8 : 8 + n], rest[8 + n :]
    dmod = rest[0]
    dw_out = rest[1 : 1 + m]
    w, sems, dw, du, dqkv = rest[1 + m :]
    load_weights(ids, pieces, w, sems)
    step = pl.program_id(0)

    @pl.when(step == 0)
    def _():
        dw[...] = jnp.zeros_like(dw)
        dmod[...] = jnp.zeros_like(dmod)
        lane = lax.broadcasted_iota(jnp.int32, (8, 128), 1)
        token = lax.dot_general(
            dtok[...], (lane == PIN).astype(F32), (((0,), (0,)), ((), ())), precision=lax.Precision.HIGHEST, preferred_element_type=F32
        )
        dw[0, :, CW : CW + 128] = dmisc[...] + token

    @pl.when(step < ids[0])
    def _():
        dh = block_backward(d_out[...], h_in[...], mod_row(mods, 0, step), w, sv, dw, du, dqkv, row_writer(dmod, step))
        dw[0, :, CW : CW + 128] += dot_tn(dh.astype(BF16), xin[...])

    @pl.when(step == pl.num_programs(0) - 1)
    def _():
        store_grads(ids, dw, dw_out)


def assign_kernel(nf, slots, me, packed, features, tone, ttwo, classes, mine, info_out, c_part, c_own, a_pre_out, a_out, feat_out, hot_out, pick_out):
    lats = packed.shape[0]
    info = packed[:, NTOK * PIN + NTOK :]
    used = info[:, 0:1]
    src = lax.broadcasted_iota(jnp.int32, (lats, lats), 0)
    dst = lax.broadcasted_iota(jnp.int32, (lats, lats), 1)
    before = dot((dst < src).astype(BF16), jnp.broadcast_to(used, (lats, 128)))[:, 0:1]
    turn = jnp.floor((before + 0.5) * (1.0 / nf))
    target = (before - nf * turn) * 8.0 + turn
    live = used.astype(F32) > 0.5
    pick = jnp.where(live & (target == dst.astype(F32)), 1.0, 0.0).astype(BF16)
    moved = dot_tn(pick, info)
    step_of = moved[:, 1:2] * 32.0 + moved[:, 2:3]
    label_of = moved[:, 3:4] * 32.0 + moved[:, 4:5]
    wide = lax.broadcasted_iota(jnp.int32, (lats, 1024), 1).astype(F32)
    hot_t = jnp.where(wide == step_of, 1.0, 0.0).astype(BF16)
    hot_l = jnp.where(wide == label_of, 1.0, 0.0).astype(BF16)
    feat = dot(hot_t, features[...]).astype(BF16)
    a_pre = dot_nt(tone[...], feat)
    a_act = (a_pre * jax.nn.sigmoid(a_pre)).astype(BF16)
    c_part[...] = dot_tn(ttwo[...], a_act)
    c_own[...] = dot_nt(classes[...], hot_l)
    a_pre_out[...] = a_pre
    a_out[...] = a_act
    feat_out[...] = feat
    hot_out[...] = hot_l
    lane8 = lax.broadcasted_iota(jnp.int32, (lats, 8), 1) + me[0] * 8
    pick_me = jnp.where(live & (target == lane8.astype(F32)), 1.0, 0.0).astype(BF16)
    mine[...] = dot_tn(pick_me, packed[:, : NTOK * PIN + NTOK]).astype(BF16)
    info_out[...] = dot_tn(pick_me, info)
    pick_out[...] = pick_me


SMEM = pl.BlockSpec(memory_space=pltpu.SMEM)
ANY = pl.BlockSpec(memory_space=pl.ANY)


def slot_spec(*shape):
    return pl.BlockSpec((None,) + shape, lambda s, ids: (jnp.minimum(s, jnp.maximum(ids[0] - 1, 0)),) + (0,) * len(shape))


def fixed_spec(*shape):
    return pl.BlockSpec(shape, lambda s, ids: (0,) * len(shape))


SAVES = (
    ((NTOK, 3 * D), BF16),
    ((HEADS, NTOK, NTOK), BF16),
    ((NTOK, D), BF16),
    ((NTOK, FF), BF16),
    ((NTOK, FF), BF16),
    ((NTOK, D), BF16),
    ((NTOK, D), BF16),
    ((NTOK, D), F32),
)


def weight_scratch(pieces, width):
    shape = (D, CHUNKS * width) if len(pieces) == 1 else (CHUNKS, 4, 2, D // 8, width)
    return [pltpu.VMEM(shape, BF16), pltpu.SemaphoreType.DMA((8,))]


def grad_scratch(width):
    return [
        pltpu.VMEM((CHUNKS, D, width), F32),
        pltpu.VMEM((NTOK, FF), BF16),
        pltpu.VMEM((NTOK, 3 * D), BF16),
    ]


def grad_outs(split, width):
    if split:
        return [fixed_out((CHUNKS, 4, D // 8, width), BF16)] * 2
    return [fixed_out((CHUNKS, D, width), BF16)]


def call(kernel, slots, ids, in_specs, args, pieces, outs, scratch, macs):
    specs = list(in_specs) + [ANY] * len(pieces)
    return pl.pallas_call(
        functools.partial(kernel, len(pieces)),
        grid_spec=pltpu.PrefetchScalarGridSpec(
            num_scalar_prefetch=1,
            grid=(slots,),
            in_specs=specs,
            out_specs=[o[0] for o in outs],
            scratch_shapes=scratch,
        ),
        out_shape=[jax.ShapeDtypeStruct(o[1], o[2]) for o in outs],
        compiler_params=pltpu.CompilerParams(vmem_limit_bytes=VMEM_LIMIT, dimension_semantics=("arbitrary",)),
        cost_estimate=pl.CostEstimate(flops=int(macs * slots // 2), bytes_accessed=int(4e6), transcendentals=0),
    )(ids, *args, *pieces)


def slot_out(slots, shape, kind):
    return (slot_spec(*shape), (slots,) + shape, kind)


def fixed_out(shape, kind):
    return (fixed_spec(*shape), shape, kind)


BLOCK_MACS = NTOK * (D * TOKW + 2 * NTOK * D)
MODS_E = (8, 6 * D)
MODS_R = (8, 14 * D)


def enc_forward(slots, ids, xin, pe, mods, bias, pieces):
    return call(
        enc_forward_kernel,
        slots,
        ids,
        [slot_spec(NTOK, 128), fixed_spec(NTOK, D), fixed_spec(*MODS_E), slot_spec(1, NTOK)],
        [xin, pe, mods, bias],
        pieces,
        [fixed_out((D, 128), BF16)] + [slot_out(slots, (NTOK, D), F32)] * 2 + [slot_out(slots, s, k) for s, k in SAVES],
        weight_scratch(pieces, CW + 128),
        BLOCK_MACS,
    )


def side_forward(slots, ids, h_in, mask, pe, misc, mods, pieces):
    return call(
        side_forward_kernel,
        slots,
        ids,
        [slot_spec(NTOK, D), slot_spec(NTOK, 1), fixed_spec(NTOK, D), fixed_spec(D, 128), fixed_spec(*MODS_R)],
        [h_in, mask, pe, misc, mods],
        pieces,
        [slot_out(slots, (NTOK, D), F32)] * 2 + [slot_out(slots, s, k) for s, k in SAVES],
        weight_scratch(pieces, CW),
        BLOCK_MACS,
    )


def dec_both(slots, ids, coef, h_in, noise, misc, mods, pieces, split):
    outs = grad_outs(split, CW)
    return call(
        lambda n, *refs: dec_kernel(n, len(outs), *refs),
        slots,
        ids,
        [SMEM, slot_spec(NTOK, D), slot_spec(NTOK, 128), fixed_spec(D, 128), fixed_spec(*MODS_R)],
        [coef, h_in, noise, misc, mods],
        pieces,
        [slot_out(slots, (NTOK, D), F32), fixed_out((8, 8 * D), F32), fixed_out((D, 128), F32), fixed_out((8, 128), F32)] + outs,
        weight_scratch(pieces, CW) + grad_scratch(CW) + [pltpu.VMEM(s, k) for s, k in SAVES],
        3 * BLOCK_MACS,
    )


def side_backward(slots, ids, d_out, h_in, mask, mods, saves, pieces, split):
    outs = grad_outs(split, CW)
    return call(
        lambda n, *refs: side_backward_kernel(n, len(outs), *refs),
        slots,
        ids,
        [slot_spec(NTOK, D), slot_spec(NTOK, D), slot_spec(NTOK, 1), fixed_spec(*MODS_R)] + [slot_spec(*s) for s, _ in SAVES],
        [d_out, h_in, mask, mods] + list(saves),
        pieces,
        [slot_out(slots, (NTOK, D), F32), fixed_out((8, 6 * D), F32), fixed_out((8, D), F32)] + outs,
        weight_scratch(pieces, CW) + grad_scratch(CW),
        2 * BLOCK_MACS,
    )


def enc_backward(slots, ids, d_out, h_in, xin, mods, dmisc, dtok, saves, pieces, split):
    outs = grad_outs(split, CW + 128)
    return call(
        lambda n, *refs: enc_backward_kernel(n, len(outs), *refs),
        slots,
        ids,
        [slot_spec(NTOK, D), slot_spec(NTOK, D), slot_spec(NTOK, 128), fixed_spec(*MODS_E), fixed_spec(D, 128), fixed_spec(8, D)]
        + [slot_spec(*s) for s, _ in SAVES],
        [d_out, h_in, xin, mods, dmisc, dtok] + list(saves),
        pieces,
        [fixed_out((8, 6 * D), F32)] + outs,
        weight_scratch(pieces, CW + 128) + grad_scratch(CW + 128),
        2 * BLOCK_MACS,
    )


def assign(nf, slots, me, packed, tone, ttwo, classes):
    lats, rows = packed.shape[0], tone.shape[0]
    out = [
        ((8, NTOK * PIN + NTOK), BF16),
        ((8, 128), F32),
        ((D, lats), F32),
        ((rows, lats), F32),
        ((rows, lats), F32),
        ((rows, lats), BF16),
        ((lats, FREQ), BF16),
        ((lats, 1024), BF16),
        ((lats, 8), BF16),
    ]
    vmem = pl.BlockSpec(memory_space=pltpu.VMEM)
    return pl.pallas_call(
        functools.partial(assign_kernel, nf, slots),
        in_specs=[SMEM] + [vmem] * 5,
        out_specs=[vmem] * len(out),
        out_shape=[jax.ShapeDtypeStruct(s, k) for s, k in out],
        compiler_params=pltpu.CompilerParams(vmem_limit_bytes=VMEM_LIMIT),
    )(me, packed, jnp.asarray(feature_table()), tone, ttwo, classes)


def silu_slope(val):
    s = jax.nn.sigmoid(val)
    return s * (1.0 + val * (1.0 - s))


def adam(master, first_m, second, grad_in):
    first_new = beta_one * first_m + (1.0 - beta_one) * grad_in
    second_new = beta_two * second + (1.0 - beta_two) * grad_in * grad_in
    first_hat = first_new / (1.0 - beta_one**STEP)
    second_hat = second_new / (1.0 - beta_two**STEP)
    master_new = master - learn_rate * (first_hat / (jnp.sqrt(second_hat) + adam_eps) + weight_decay * master)
    return [master_new, first_new, second_new]


def grad_core(dw, *deps):
    if len(dw) == 1:
        return dw
    keep, send = dw
    if deps:
        send = after(send, *deps)
    return [keep, swap(send, "fsdp", 1)]


def grad_dp(parts):
    if len(parts) == 1:
        return parts
    keep, got = parts
    me = lax.axis_index("dp")

    def piece(k):
        return lax.dynamic_index_in_dim(keep, me ^ k, 0, False).astype(F32) + lax.dynamic_index_in_dim(got, me ^ k, 0, False).astype(F32)

    return [piece(0).astype(BF16)] + [swap(piece(k).astype(BF16), "dp", k) for k in (1, 2, 3)]


def grad_sum(parts):
    if len(parts) == 1:
        return parts[0]
    return sum(p.astype(F32) for p in parts)


def grad_z(part):
    if part.shape[0] == CHUNKS and part.shape[1] == D:
        part = lax.psum_scatter(part, "fsdp", scatter_dimension=1, tiled=True)
        return reduce_stage(part, 0, "dp", 1, CHUNKS, BF16).astype(BF16)
    return reduce_stage(part, 0, "fsdp", 2, 4, BF16).astype(BF16)


def dp_share(val):
    rows = val.shape[0]
    return reduce_stage(val.reshape(rows, CHUNKS, -1).transpose(1, 0, 2), 0, "dp", 1, CHUNKS, BF16).astype(BF16)


def columns(parts, lo, hi):
    return jnp.concatenate([parts[j, :, lo:hi] for j in range(CHUNKS)], axis=1)


def on_device(latents, noise, timesteps, labels, patch_mask, counts, owners, tables_w, tables_m, tables_v, rows_w, rows_m, rows_v, down_w, down_m, down_v):
    nd, nf = lax.axis_size("dp"), lax.axis_size("fsdp")
    me_d, me_f = lax.axis_index("dp"), lax.axis_index("fsdp")
    rows = tables_w.shape[0]
    micro, per = latents.shape[0], latents.shape[1]
    slots = micro * per
    split = small_mesh(rows)

    steps = timesteps.reshape(slots)
    names = labels.reshape(slots)
    plan = jnp.take(jnp.asarray(plan_table()), steps, axis=0)
    used = (jnp.arange(per)[None, :] < counts).astype(jnp.int32).reshape(slots)
    x_zero, eps = latents.reshape(slots, NTOK * PIN), noise.reshape(slots, NTOK * PIN)
    x_in = (plan[:, 0:1] * x_zero + plan[:, 1:2] * eps).astype(BF16)
    words = jnp.stack([used, steps // 32, steps % 32, names // 32, names % 32], axis=1).astype(BF16)
    words = jnp.concatenate([words, jnp.zeros((slots, 3), BF16), plan[:, 8:].astype(BF16)], axis=1)
    packed = jnp.concatenate([x_in, patch_mask.reshape(slots, NTOK).astype(BF16), words], axis=1)
    packed = jnp.pad(packed, ((0, 8 - slots), (0, 0)))
    eps = jnp.pad(eps.astype(BF16), ((0, 8 - slots), (0, 0)))
    packed = gather(packed, "fsdp").reshape(nf * 8, -1)
    wholes = []

    rows_b, down_b, tables_b = rows_w.astype(BF16), down_w.astype(BF16), tables_w.astype(BF16)
    head_at = D + 3 * STRIDE + 2 * D
    gap = jnp.zeros((rows, 16), BF16)
    misc_own = jnp.concatenate(
        [tables_b[:, : PIN + 1], gap[:, :15], rows_b[:, head_at : head_at + PIN], gap, rows_b[:, head_at + PIN : head_at + 2 * PIN], gap, gap, gap],
        axis=1,
    )
    for b in range(3):
        at = D + b * STRIDE
        row_part, down_part = rows_b[:, at : at + 4 * D + FF], down_b[:, b * FF : (b + 1) * FF]
        cols = [row_part[:, :CW], row_part[:, CW : 2 * CW], row_part[:, 2 * CW :], down_part[:, :D], down_part[:, D:]]
        if b == 0:
            cols = [cols[0], misc_own, cols[1], misc_own, cols[2], cols[3], misc_own, cols[4], misc_own]
        whole = jnp.concatenate(cols, axis=1)
        wholes.append(whole)
    enc_z = gather_z(wholes[0]) if split else None
    late_w = gather_whole(jnp.concatenate(wholes[1:], axis=1))

    w_tone = tables_b[:, PIN + 1 : PIN + 1 + FREQ]
    class_tab = jnp.pad(tables_b[:, PIN + 1 + FREQ :], ((0, 0), (0, 1024 - CLASSES)))
    w_ttwo = rows_b[:, :D]
    ada_at = [D + b * STRIDE + 4 * D + FF for b in range(3)]
    fin_at = D + 3 * STRIDE
    w_ada = jnp.concatenate([rows_b[:, a : a + 6 * D] for a in ada_at] + [rows_b[:, fin_at : fin_at + 2 * D]], axis=1)
    me = me_f.astype(jnp.int32).reshape(1)
    mine, info, c_part, c_own, a_pre, a_act, feat, hot, pick = assign(nf, slots, me, packed, w_tone, w_ttwo, class_tab)
    cond = reduce_parts(c_part.reshape(nf, rows, nf * 8), "fsdp", F32) + c_own
    s_cond = jax.nn.silu(cond).astype(BF16)
    mods_e = reduce_parts(dot_tn(s_cond, w_ada[:, : 6 * D]).reshape(nf, 8, 6 * D), "fsdp", BF16)
    if split:
        enc_w = gather_core(after(gather_dp(after(enc_z, c_part)), s_cond))
    else:
        enc_w = gather_whole(wholes[0])
    mods_r = reduce_open(dot_tn(s_cond, w_ada[:, 6 * D :]).reshape(nf, 8, 14 * D), "fsdp", BF16)

    work = jnp.sum(info[:, 0]).astype(jnp.int32)
    ids = jnp.stack([work, me_d.astype(jnp.int32), (me_f % 2).astype(jnp.int32)])
    coef = jnp.stack([info[:, 8 + 3 * k] + info[:, 9 + 3 * k] + info[:, 10 + 3 * k] for k in range(3)], axis=1)
    size = NTOK * PIN
    x_in = jnp.pad(mine[:slots, :size].reshape(slots, NTOK, PIN), ((0, 0), (0, 0), (0, 128 - PIN)))
    masked = mine[:slots, size:].astype(F32)
    bias = (-1e9 * masked)[:, None, :]
    mask_col = masked[:, :, None]
    pe = jnp.asarray(position_table())

    last = len(axis_stages("fsdp")) - 1
    misc, h0, h_enc, *save_e = enc_forward(slots, ids, x_in, pe, mods_e, bias, enc_w)
    mods_r = total_of(tie(mods_r, misc))
    level = gather_open(after(eps, mods_r), "fsdp", 0)
    hs, h_side, *save_s = side_forward(slots, ids, h_enc, mask_col, pe, misc, mods_r, late_w)
    level = tie(level, hs)
    for at in range(last):
        level = gather_open(gather_close(level, "fsdp", at), "fsdp", at + 1)
    eps = gather_shape(gather_close(level, "fsdp", last), "fsdp", (8, size)).reshape(nf * 8, size)
    eps = dot_tn(pick, eps)[:slots].reshape(slots, NTOK, PIN)
    eps = jnp.pad(eps, ((0, 0), (0, 0), (32, 96 - PIN)))

    d_side, dmod_d, dmisc, loss, *dw_d = dec_both(slots, ids, coef, h_side, eps, misc, mods_r, late_w, False)
    mine_d = lax.psum_scatter(dw_d[0], "fsdp", scatter_dimension=1, tiled=True)
    d_enc, dmod_s, dtok, *dw_s = side_backward(slots, ids, d_side, hs, mask_col, mods_r, save_s, late_w, split)
    part_s = grad_dp(grad_core(dw_s))
    d_enc = after(d_enc, part_s[0])
    dmod_e, *dw_e = enc_backward(slots, ids, d_enc, h0, x_in, mods_e, dmisc, dtok, save_e, enc_w, split)
    total_s = grad_sum(tie(part_s, dmod_e, mine_d))
    dmods = jnp.concatenate([dmod_e, dmod_s, dmod_d], axis=1).astype(BF16)
    core_e = grad_core(dw_e, total_s)
    part_d = reduce_open(after(mine_d, total_s), "dp", BF16)
    part_e = grad_dp(core_e)

    dm_all = gather(after(dmods, part_e[0]), "fsdp").reshape(nf * 8, -1)
    g_side = grad_z(after(total_s, dm_all)) if split else grad_z(total_s)
    g_dec = total_of(tie(part_d, part_e[0])).astype(BF16)
    d_cond = dot_nt(w_ada, dm_all) * silu_slope(cond)
    d_cond_all = gather(d_cond.astype(BF16), "fsdp").reshape(D, nf * 8)
    d_apre = (dot(w_ttwo, d_cond_all) * silu_slope(a_pre)).astype(BF16)
    g_class = jnp.dot(d_cond, hot.astype(F32), precision=lax.Precision.HIGHEST, preferred_element_type=F32)
    kinds = [dot(s_cond, dm_all), dot_nt(a_act, d_cond_all), dot(d_apre, feat), g_class, jnp.zeros((rows, 128), F32)]
    kinds = jnp.concatenate([k.astype(BF16) for k in kinds], axis=1).reshape(rows, CHUNKS, -1).transpose(1, 0, 2)

    total_e = grad_sum(tie(part_e, dm_all, g_dec))
    g_enc = grad_z(total_e)
    first = after(jnp.concatenate([g_side, g_dec], axis=1), total_e)
    full = gather_open(first, "dp", 0)
    g_other = total_of(reduce_open(after(kinds, full[0]), "dp", BF16)).astype(BF16)
    second = after(jnp.concatenate([g_enc, g_other], axis=1), *full)
    full = gather_shape(gather_close(full, "dp", 0), "dp", first.shape)
    squares = jnp.sum(jnp.square(first.astype(F32))) + jnp.sum(jnp.square(second.astype(F32)))
    norm_sq, loss_sum, count = sum_all(jnp.stack([squares, jnp.sum(loss), jnp.sum(used).astype(F32)]), ("fsdp", "dp"))
    rest = gather(second, "dp")
    scale = 1.0 / (count * (NTOK * PIN))
    loss_out = loss_sum * scale
    grad_norm = jnp.sqrt(norm_sq) * scale
    factor = scale * jnp.minimum(1.0, clip_level / (grad_norm + 1e-06))

    up = 4 * D + FF
    wide_e = CW + 128
    f_side, f_dec = columns(full, 0, CW), columns(full, CW, 2 * CW)
    f_enc, small = columns(rest, 0, CW), rest[0, :, CW:wide_e]
    f_rest = columns(rest, wide_e, rest.shape[2])
    at = 20 * D
    ttwo, tone, klass = f_rest[:, at : at + D], f_rest[:, at + D : at + D + FREQ], f_rest[:, at + D + FREQ : at + D + FREQ + CLASSES]
    rows_g = [ttwo, f_enc[:, :up], f_rest[:, : 6 * D], f_side[:, :up], f_rest[:, 6 * D : 12 * D], f_dec[:, :up], f_rest[:, 12 * D : 20 * D]]
    rows_g = jnp.concatenate(rows_g + [small[:, 32 : 32 + PIN], small[:, 64 : 64 + PIN]], axis=1)
    down_g = jnp.concatenate([blk[:, up:] for blk in (f_enc, f_side, f_dec)], axis=1)
    tables_g = jnp.concatenate([small[:, : PIN + 1], tone, klass], axis=1)
    results = adam(tables_w, tables_m, tables_v, factor * tables_g.astype(F32))

    def own(val):
        size = val.shape[1] // nd
        return lax.dynamic_slice_in_dim(val, me_d * size, size, 1)

    results += adam(own(rows_w), own(rows_m), own(rows_v), factor * own(rows_g).astype(F32))
    results += adam(own(down_w), own(down_m), own(down_v), factor * own(down_g).astype(F32))
    return tuple([loss_out, grad_norm] + results)


def solution(mesh):
    lat = P(None, ("dp", "fsdp"), None)
    num = P(None, ("dp", "fsdp"))
    row = P("fsdp", None)
    both = P("fsdp", "dp")
    return jax.shard_map(
        on_device,
        mesh=mesh,
        in_specs=(lat, lat, num, num, lat, num, P()) + (row,) * 9,
        out_specs=(P(), P()) + (row,) * 3 + (both,) * 6,
        check_vma=False,
    )
```

time: 502 us -> 401 us (0.80)
  starting transfers between devices: 200 us -> 77.5 us
  Pallas kernels: 106 us -> 148 us
  waiting for transfers between devices: 82.6 us -> 67 us
  local copies, waits for them, and re-layouts: 42.2 us -> 32.2 us
  other arithmetic: 36 us -> 43.6 us
    ppermute x97 -> x68, starting transfers between devices: 199 us -> 77.4 us  [swap(): return lax.ppermute(val, axis, [(i, i ^ mask) for i in range(size)])]
    pallas_call x5 -> x6, Pallas kernels: 106 us -> 148 us  [the longest x5 145 us: call(): pl.pallas_call(functools.partial(kernel, len(pieces)), grid_spec=pltpu.Pr...]
    ppermute x97 -> x68, waiting for transfers between devices: 82.5 us -> 67 us  [swap(): return lax.ppermute(val, axis, [(i, i ^ mask) for i in range(size)])]
    convert_element_type x4 -> x9, other arithmetic: 2.73 us -> 10.4 us  [the longest x2 5.68 us: grad_dp(): piece(k).astype(BF16)]
  transfers between devices with their start and end apart: 100 -> 70, of which waited for: 28 -> 25; matrix products, arithmetic and copies ran while one was open for 13% -> 11% of each run, Pallas kernels for 16% -> 26%
where the time goes in v2:
time: 401 us; the launch traced here: 394 us
  Pallas kernels  148 us (37%)
  starting transfers between devices  77.5 us (19%)
  waiting for transfers between devices  67 us (17%)
  other arithmetic  43.6 us (11%)
  local copies, waits for them, and re-layouts  32.2 us (8%)
  between operations  22.6 us (6%)
    pallas_call x5, Pallas kernels, call(): pl.pallas_call(functools.partial(kernel, len(pieces)), grid_spec=pltpu.Pr...  145 us
    ppermute x68, starting transfers between devices, swap(): return lax.ppermute(val, axis, [(i, i ^ mask) for i in range(size)])  77.4 us
    ppermute x68, waiting for transfers between devices, swap(): return lax.ppermute(val, axis, [(i, i ^ mask) for i in range(size)])  67 us
    sub x3, other arithmetic, adam(): master - learn_rate * (first_hat / (jnp.sqrt(second_hat) + adam_eps) + we...  8.56 us
  transfers between devices with their start and end apart: 70, of which 25 were waited for; matrix products, arithmetic and copies ran while one was open for 11% of the time, Pallas kernels for 26%

profile of v2, /device:TPU:0, one launch (start us, length us, event | category | flops | bytes accessed | tf_op | source)
XLA Modules:
  0.0 393.7 jit_solution(1444253163131233649)
XLA Ops:
  16.3 4.0 %collective-permute-start.1 = (bf16[8,4480]{1,0:T(8,128)(2,1)}, bf16[8,4480]{1,0:T(8,128)(2,1)}, u32[]{:S(2)}, u32[]{:S(2)}) collective-permute-start(bf16[8,4480]{1,0:T(8,128)(2,1)} %pad.20), channel_id=1, source_target_pairs={{0,4},{1,5},{2,6},{3,7},{4,0},{5,1},{6,2},{7,3},{8,12},{9,13},{10,... | collective-permute-start | bytes 215048 | tf_op jit(solution)/shard_map/ppermute | solution.py:99
  26.6 2.8 collective-permute-start.13
  36.2 2.5 collective-permute-done.13
  42.5 3.2 shard_map.257
  45.7 2.5 collective-permute-start.17
  54.3 2.7 collective-permute-start.7
  66.2 2.5 collective-permute-start.11
  70.7 2.5 collective-permute-done.11
  76.8 8.5 %collective-permute-done.15 = bf16[4,48,1280]{2,1,0:T(8,128)(2,1)S(1)} collective-permute-done((bf16[4,48,1280]{2,1,0:T(8,128)(2,1)S(1)}, bf16[4,48,1280]{2,1,0:T(8,128)(2,1)S(1)}, u32[]{:S(2)}, u32[]{:S(2)}) %collective-permute-start.15) | collective-permute-done | bytes 491552 | tf_op jit(solution)/shard_map/ppermute | solution.py:99
  87.1 2.9 collective-permute-start.21
  91.5 22.7 %shard_map.258 = (bf16[384,128]{1,0:T(8,128)(2,1)}, f32[6,256,384]{2,1,0:T(8,128)}, f32[6,256,384]{2,1,0:T(8,128)}, bf16[6,256,1152]{2,1,0:T(8,128)(2,1)}, bf16[...) custom-call(s32[3]{0:T(128)} %pad_add_fusion.ids.refs_0_, ...), custom_call_target="tpu_custom_call" | custom-call | flops 1509949440 | bytes 4000000 | tf_op jit(solution)/shard_map/pallas_call | solution.py:597
  116.6 2.8 collective-permute-start.25
  119.4 23.2 %shard_map.259 = (f32[6,256,384]{2,1,0:T(8,128)}, f32[6,256,384]{2,1,0:T(8,128)}, bf16[6,256,1152]{2,1,0:T(8,128)(2,1)}, bf16[6,6,256,256]{3,2,1,0:T(8,128)(2,1)...) custom-call(s32[3]{0:T(128)} %pad_add_fusion.ids.refs_0_, ...), custom_call_target="tpu_custom_call" | custom-call | flops 1509949440 | bytes 4000000 | tf_op jit(solution)/shard_map/pallas_call | solution.py:597
  146.2 43.6 %shard_map.260 = (f32[6,256,384]{2,1,0:T(8,128)}, f32[8,3072]{1,0:T(8,128)}, f32[384,128]{1,0:T(8,128)}, f32[8,128]{1,0:T(8,128)}, bf16[4,384,1152]{2,1,0:T(8,128)(2,1)}) custom-call(s32[3]{0:T(128)} %pad_add_fusion.ids.refs_0_, f32[8,3]{1,0:T(8,128)} %pad_maximum_fusion.18.refs_1_, f32[6,256,384]{2,1,0:T(8,128)} %get-tuple-element.97.refs_2_, ...), custom_call_target="tpu_custom_call" | custom-call | flops 4529848320 | bytes 4000000 | tf_op jit(solution)/shard_map/pallas_call | solution.py:597
  189.8 27.7 %shard_map.261 = (f32[6,256,384]{2,1,0:T(8,128)}, f32[8,2304]{1,0:T(8,128)}, f32[8,384]{1,0:T(8,128)}, bf16[4,4,48,1152]{3,2,1,0:T(8,128)(2,1)}, bf16[4,4,48,1152]{3,2,1,0:T(8,128)(2,1)}) custom-call(s32[3]{0:T(128)} %pad_add_fusion.ids.refs_0_, f32[6,256,384]{2,1,0:T(8,128)} %get-tuple-element.105.refs_1_, f32[6,256,384]{2,1,0:T(8,128)} %get-tuple-element.100.refs_2_, ...), custom_call_target="tpu_custom_call" | custom-call | flops 3019898880 | bytes 4000000 | tf_op jit(solution)/shard_map/pallas_call | solution.py:597
  217.7 3.8 collective-permute-done.27
  221.5 2.8 fusion.27
  227.7 27.5 %shard_map.262 = (f32[8,2304]{1,0:T(8,128)}, bf16[4,4,48,1280]{3,2,1,0:T(8,128)(2,1)}, bf16[4,4,48,1280]{3,2,1,0:T(8,128)(2,1)}) custom-call(s32[3]{0:T(128)} %pad_add_fusion.ids.refs_0_, f32[6,256,384]{2,1,0:T(8,128)} %get-tuple-element.117.refs_1_, f32[6,256,384]{2,1,0:T(8,128)} %get-tuple-element.118.refs_2_, bf16[6,256,128]{2,1,0:T(8,128)(2,1)} %pad.22.xin.refs_3_, ...), custom_call_target="tpu_custom_call" | custom-call | flops 3019898880 | bytes 4000000 | tf_op jit(solution)/shard_map/pallas_call | solution.py:597
  258.1 3.2 collective-permute-done.31
  261.3 2.9 fusion.20
  271.5 2.8 collective-permute-done.33
  289.3 5.3 %collective-permute-done.42 = bf16[4,48,1280]{2,1,0:T(8,128)(2,1)S(1)} collective-permute-done((bf16[4,48,1280]{2,1,0:T(8,128)(2,1)}, bf16[4,48,1280]{2,1,0:T(8,128)(2,1)S(1)}, u32[]{:S(2)}, u32[]{:S(2)}) %collective-permute-start.42) | collective-permute-done | bytes 491552 | tf_op jit(solution)/shard_map/ppermute | solution.py:99
  294.6 9.7 %collective-permute-done.43 = bf16[4,48,1280]{2,1,0:T(8,128)(2,1)S(1)} collective-permute-done((bf16[4,48,1280]{2,1,0:T(8,128)(2,1)}, bf16[4,48,1280]{2,1,0:T(8,128)(2,1)S(1)}, u32[]{:S(2)}, u32[]{:S(2)}) %collective-permute-start.43) | collective-permute-done | bytes 491552 | tf_op jit(solution)/shard_map/ppermute | solution.py:99
  304.3 2.3 collective-permute-start.37
  314.8 3.0 collective-permute-start.45
  319.0 3.8 collective-permute-start.56
  329.6 7.7 %collective-permute-done.56 = bf16[48,2304]{1,0:T(8,128)(2,1)S(1)} collective-permute-done((bf16[48,2304]{1,0:T(8,128)(2,1)S(1)}, bf16[48,2304]{1,0:T(8,128)(2,1)S(1)}, u32[]{:S(2)}, u32[]{:S(2)}) %collective-permute-start.56) | collective-permute-done | bytes 221216 | tf_op jit(solution)/shard_map/ppermute | solution.py:99
  342.5 2.6 collective-permute-start.67
  351.9 2.4 collective-permute-done.60
  355.3 2.6 collective-permute-done.59
  375.3 2.7 concatenate.90
  378.0 4.1 %multiply_subtract_fusion = (f32[48,4328]{1,0:T(8,128)}, f32[48,4328]{1,0:T(8,128)}, f32[48,4328]{1,0:T(8,128)}) fusion(f32[48,17312]{1,0:T(8,128)} %param.28, s32[]{:T(128)S(6)} %select_n.889, bf16[48,17312]{1,0:T(8,128)(2,1)S(1)} %concatenate.90, f32[]{:T(128)S(6)} %mul.214, f32[48,17312]{1,0:T(8,128)} %param.29, f32[48,17312]{1,0:T(8,128)} %param.30), kind=kLoop, calls=%fused_computation.28 | loop fusion | flops 3531648 | bytes 5401352 | tf_op jit(solution)/shard_map/sub | solution.py:732
  (339 shorter events, 127.8 us)
Async XLA Ops:
  7.2 112.2 %all-gather.2.cloned.1.call-start = ((), (), s32[]{:S(2)}) async-start(), calls=%async_computation.1 | async-start | bytes 7962624 | tf_op jit(solution)/shard_map/all_gather | solution.py:204
  16.3 18.6 %collective-permute-start.1 = (bf16[8,4480]{1,0:T(8,128)(2,1)}, bf16[8,4480]{1,0:T(8,128)(2,1)}, u32[]{:S(2)}, u32[]{:S(2)}) collective-permute-start(bf16[8,4480]{1,0:T(8,128)(2,1)} %pad.20), channel_id=1, source_target_pairs={{0,4},{1,5},{2,6},{3,7},{4,0},{5,1},{6,2},{7,3},{8,12},{9,13},{10,... | collective-permute-start | bytes 215048 | tf_op jit(solution)/shard_map/ppermute | solution.py:99
  20.4 14.7 %collective-permute-start.2 = (bf16[8,4480]{1,0:T(8,128)(2,1)}, bf16[8,4480]{1,0:T(8,128)(2,1)}, u32[]{:S(2)}, u32[]{:S(2)}) collective-permute-start(bf16[8,4480]{1,0:T(8,128)(2,1)} %pad.20), channel_id=1, source_target_pairs={{0,6},{1,7},{2,4},{3,5},{4,2},{5,3},{6,0},{7,1},{8,14},{9,15},{10,... | collective-permute-start | bytes 215048 | tf_op jit(solution)/shard_map/ppermute | solution.py:99
  32.0 223.3 %reduce-scatter.2.cloned.1.call-start = ((), (), s32[]{:S(2)}) async-start(), calls=%async_computation.2 | async-start | bytes 3981312 | tf_op jit(solution)/shard_map/reduce_scatter | solution.py:859
  45.7 31.2 %collective-permute-start.17 = (bf16[4,48,1280]{2,1,0:T(8,128)(2,1)S(1)}, bf16[4,48,1280]{2,1,0:T(8,128)(2,1)}, u32[]{:S(2)}, u32[]{:S(2)}) collective-permute-start(bf16[4,48,1280]{2,1,0:T(8,128)(2,1)S(1)} %pad_maximum_fusion.2), channel_id=1, source_target_pairs={{0,24},{8,16},{16,8},{24,0},{1,25},{9,17},{17,9},{25,1},{2,26},{10... | collective-permute-start | bytes 1474568 | tf_op jit(solution)/shard_map/ppermute | solution.py:99
  48.2 28.7 %collective-permute-start.16 = (bf16[4,48,1280]{2,1,0:T(8,128)(2,1)S(1)}, bf16[4,48,1280]{2,1,0:T(8,128)(2,1)}, u32[]{:S(2)}, u32[]{:S(2)}) collective-permute-start(bf16[4,48,1280]{2,1,0:T(8,128)(2,1)S(1)} %pad_maximum_fusion.2), channel_id=1, source_target_pairs={{0,16},{8,24},{16,0},{24,8},{1,17},{9,25},{17,1},{25,9},{2,18},{10... | collective-permute-start | bytes 1474568 | tf_op jit(solution)/shard_map/ppermute | solution.py:99
  87.0 27.2 %collective-permute-start.20 = (bf16[8,5376]{1,0:T(8,128)(2,1)S(1)}, bf16[8,5376]{1,0:T(8,128)(2,1)S(1)}, u32[]{:S(2)}, u32[]{:S(2)}) collective-permute-start(bf16[8,5376]{1,0:T(8,128)(2,1)S(1)} %get-tuple-element.212), channel_id=1, source_target_pairs={{0,2},{1,3},{2,0},{3,1},{4,6},{5,7},{6,4},{7,5},{8,10},{9,11},{10,... | collective-permute-start | bytes 258056 | tf_op jit(solution)/shard_map/ppermute | solution.py:99
  87.1 27.2 %collective-permute-start.21 = (bf16[8,5376]{1,0:T(8,128)(2,1)S(1)}, bf16[8,5376]{1,0:T(8,128)(2,1)S(1)}, u32[]{:S(2)}, u32[]{:S(2)}) collective-permute-start(bf16[8,5376]{1,0:T(8,128)(2,1)S(1)} %get-tuple-element.211), channel_id=1, source_target_pairs={{0,4},{1,5},{2,6},{3,7},{4,0},{5,1},{6,2},{7,3},{8,12},{9,13},{10,... | collective-permute-start | bytes 258056 | tf_op jit(solution)/shard_map/ppermute | solution.py:99
  90.0 24.3 %collective-permute-start.22 = (bf16[8,5376]{1,0:T(8,128)(2,1)S(1)}, bf16[8,5376]{1,0:T(8,128)(2,1)S(1)}, u32[]{:S(2)}, u32[]{:S(2)}) collective-permute-start(bf16[8,5376]{1,0:T(8,128)(2,1)S(1)} %get-tuple-element.210), channel_id=1, source_target_pairs={{0,6},{1,7},{2,4},{3,5},{4,2},{5,3},{6,0},{7,1},{8,14},{9,15},{10,... | collective-permute-start | bytes 258056 | tf_op jit(solution)/shard_map/ppermute | solution.py:99
  115.0 27.6 %collective-permute-start.23 = (bf16[8,4096]{1,0:T(8,128)(2,1)S(1)}, bf16[8,4096]{1,0:T(8,128)(2,1)S(1)}, u32[]{:S(2)}, u32[]{:S(2)}) collective-permute-start(bf16[8,4096]{1,0:T(8,128)(2,1)S(1)} %pad.23), channel_id=1, source_target_pairs={{0,2},{1,3},{2,0},{3,1},{4,6},{5,7},{6,4},{7,5},{8,10},{9,11},{10,... | collective-permute-start | bytes 196616 | tf_op jit(solution)/shard_map/ppermute | solution.py:99
  115.0 27.6 %collective-permute-start.24 = (bf16[8,4096]{1,0:T(8,128)(2,1)S(1)}, bf16[8,4096]{1,0:T(8,128)(2,1)S(1)}, u32[]{:S(2)}, u32[]{:S(2)}) collective-permute-start(bf16[8,4096]{1,0:T(8,128)(2,1)S(1)} %pad.23), channel_id=1, source_target_pairs={{0,4},{1,5},{2,6},{3,7},{4,0},{5,1},{6,2},{7,3},{8,12},{9,13},{10,... | collective-permute-start | bytes 196616 | tf_op jit(solution)/shard_map/ppermute | solution.py:99
  116.6 26.1 %collective-permute-start.25 = (bf16[8,4096]{1,0:T(8,128)(2,1)S(1)}, bf16[8,4096]{1,0:T(8,128)(2,1)S(1)}, u32[]{:S(2)}, u32[]{:S(2)}) collective-permute-start(bf16[8,4096]{1,0:T(8,128)(2,1)S(1)} %pad.23), channel_id=1, source_target_pairs={{0,6},{1,7},{2,4},{3,5},{4,2},{5,3},{6,0},{7,1},{8,14},{9,15},{10,... | collective-permute-start | bytes 196616 | tf_op jit(solution)/shard_map/ppermute | solution.py:99
  224.2 31.0 %collective-permute-start.28 = (bf16[4,48,1152]{2,1,0:T(8,128)(2,1)}, bf16[4,48,1152]{2,1,0:T(8,128)(2,1)}, u32[]{:S(2)}, u32[]{:S(2)}) collective-permute-start(bf16[4,48,1152]{2,1,0:T(8,128)(2,1)} %get-tuple-element.180), channel_id=1, source_target_pairs={{0,8},{8,0},{16,24},{24,16},{1,9},{9,1},{17,25},{25,17},{2,10},{10... | collective-permute-start | bytes 1327112 | tf_op jit(solution)/shard_map/ppermute | solution.py:99
  225.7 29.6 %collective-permute-start.29 = (bf16[4,48,1152]{2,1,0:T(8,128)(2,1)}, bf16[4,48,1152]{2,1,0:T(8,128)(2,1)}, u32[]{:S(2)}, u32[]{:S(2)}) collective-permute-start(bf16[4,48,1152]{2,1,0:T(8,128)(2,1)} %get-tuple-element.179), channel_id=1, source_target_pairs={{0,16},{8,24},{16,0},{24,8},{1,17},{9,25},{17,1},{25,9},{2,18},{10... | collective-permute-start | bytes 1327112 | tf_op jit(solution)/shard_map/ppermute | solution.py:99
  227.2 28.1 %collective-permute-start.30 = (bf16[4,48,1152]{2,1,0:T(8,128)(2,1)S(1)}, bf16[4,48,1152]{2,1,0:T(8,128)(2,1)}, u32[]{:S(2)}, u32[]{:S(2)}) collective-permute-start(bf16[4,48,1152]{2,1,0:T(8,128)(2,1)S(1)} %get-tuple-element.178), channel_id=1, source_target_pairs={{0,24},{8,16},{16,8},{24,0},{1,25},{9,17},{17,9},{25,1},{2,26},{10... | collective-permute-start | bytes 1327112 | tf_op jit(solution)/shard_map/ppermute | solution.py:99
  280.2 14.4 %collective-permute-start.42 = (bf16[4,48,1280]{2,1,0:T(8,128)(2,1)}, bf16[4,48,1280]{2,1,0:T(8,128)(2,1)S(1)}, u32[]{:S(2)}, u32[]{:S(2)}) collective-permute-start(bf16[4,48,1280]{2,1,0:T(8,128)(2,1)} %get-tuple-element.176), channel_id=1, source_target_pairs={{0,8},{8,0},{16,24},{24,16},{1,9},{9,1},{17,25},{25,17},{2,10},{10... | collective-permute-start | bytes 1474568 | tf_op jit(solution)/shard_map/ppermute | solution.py:99
  281.6 22.7 %collective-permute-start.43 = (bf16[4,48,1280]{2,1,0:T(8,128)(2,1)}, bf16[4,48,1280]{2,1,0:T(8,128)(2,1)S(1)}, u32[]{:S(2)}, u32[]{:S(2)}) collective-permute-start(bf16[4,48,1280]{2,1,0:T(8,128)(2,1)} %get-tuple-element.175), channel_id=1, source_target_pairs={{0,16},{8,24},{16,0},{24,8},{1,17},{9,25},{17,1},{25,9},{2,18},{10... | collective-permute-start | bytes 1474568 | tf_op jit(solution)/shard_map/ppermute | solution.py:99
  282.8 21.5 %collective-permute-start.44 = (bf16[4,48,1280]{2,1,0:T(8,128)(2,1)S(1)}, bf16[4,48,1280]{2,1,0:T(8,128)(2,1)S(1)}, u32[]{:S(2)}, u32[]{:S(2)}) collective-permute-start(bf16[4,48,1280]{2,1,0:T(8,128)(2,1)S(1)} %copy-done.11), channel_id=1, source_target_pairs={{0,24},{8,16},{16,8},{24,0},{1,25},{9,17},{17,9},{25,1},{2,26},{10... | collective-permute-start | bytes 1474568 | tf_op jit(solution)/shard_map/ppermute | solution.py:99
  286.5 20.7 %collective-permute-start.49 = (bf16[48,64]{1,0:T(8,128)(2,1)S(1)}, bf16[48,64]{1,0:T(8,128)(2,1)S(1)}, u32[]{:S(2)}, u32[]{:S(2)}) collective-permute-start(bf16[48,64]{1,0:T(8,128)(2,1)S(1)} %get-tuple-element.277), channel_id=1, source_target_pairs={{0,4},{1,5},{2,6},{3,7},{4,0},{5,1},{6,2},{7,3},{8,12},{9,13},{10,... | collective-permute-start | bytes 18440 | tf_op jit(solution)/shard_map/ppermute | solution.py:99
  286.6 22.8 %collective-permute-start.50 = (bf16[48,64]{1,0:T(8,128)(2,1)S(1)}, bf16[48,64]{1,0:T(8,128)(2,1)S(1)}, u32[]{:S(2)}, u32[]{:S(2)}) collective-permute-start(bf16[48,64]{1,0:T(8,128)(2,1)S(1)} %get-tuple-element.277), channel_id=1, source_target_pairs={{0,6},{1,7},{2,4},{3,5},{4,2},{5,3},{6,0},{7,1},{8,14},{9,15},{10,... | collective-permute-start | bytes 18440 | tf_op jit(solution)/shard_map/ppermute | solution.py:99
  294.6 14.8 %collective-permute-start.48 = (bf16[48,64]{1,0:T(8,128)(2,1)S(1)}, bf16[48,64]{1,0:T(8,128)(2,1)S(1)}, u32[]{:S(2)}, u32[]{:S(2)}) collective-permute-start(bf16[48,64]{1,0:T(8,128)(2,1)S(1)} %get-tuple-element.277), channel_id=1, source_target_pairs={{0,2},{1,3},{2,0},{3,1},{4,6},{5,7},{6,4},{7,5},{8,10},{9,11},{10,... | collective-permute-start | bytes 18440 | tf_op jit(solution)/shard_map/ppermute | solution.py:99
  304.3 13.5 %collective-permute-start.37 = (bf16[48,1152]{1,0:T(8,128)(2,1)}, bf16[48,1152]{1,0:T(8,128)(2,1)}, u32[]{:S(2)}, u32[]{:S(2)}) collective-permute-start(bf16[48,1152]{1,0:T(8,128)(2,1)} %get-tuple-element.209), channel_id=1, source_target_pairs={{0,4},{1,5},{2,6},{3,7},{4,0},{5,1},{6,2},{7,3},{8,12},{9,13},{10,... | collective-permute-start | bytes 331784 | tf_op jit(solution)/shard_map/ppermute | solution.py:99
  310.2 13.4 %collective-permute-start.47 = (bf16[48,1280]{1,0:T(8,128)(2,1)}, bf16[48,1280]{1,0:T(8,128)(2,1)S(1)}, u32[]{:S(2)}, u32[]{:S(2)}) collective-permute-start(bf16[48,1280]{1,0:T(8,128)(2,1)} %get-tuple-element.196), channel_id=1, source_target_pairs={{0,6},{1,7},{2,4},{3,5},{4,2},{5,3},{6,0},{7,1},{8,14},{9,15},{10,... | collective-permute-start | bytes 368648 | tf_op jit(solution)/shard_map/ppermute | solution.py:99
  310.7 14.4 %collective-permute-start.46 = (bf16[48,1280]{1,0:T(8,128)(2,1)}, bf16[48,1280]{1,0:T(8,128)(2,1)}, u32[]{:S(2)}, u32[]{:S(2)}) collective-permute-start(bf16[48,1280]{1,0:T(8,128)(2,1)} %get-tuple-element.197), channel_id=1, source_target_pairs={{0,4},{1,5},{2,6},{3,7},{4,0},{5,1},{6,2},{7,3},{8,12},{9,13},{10,... | collective-permute-start | bytes 368648 | tf_op jit(solution)/shard_map/ppermute | solution.py:99
  319.0 18.3 %collective-permute-start.56 = (bf16[48,2304]{1,0:T(8,128)(2,1)S(1)}, bf16[48,2304]{1,0:T(8,128)(2,1)S(1)}, u32[]{:S(2)}, u32[]{:S(2)}) collective-permute-start(bf16[48,2304]{1,0:T(8,128)(2,1)S(1)} %pad_maximum_fusion.14), channel_id=1, source_target_pairs={{0,16},{8,24},{16,0},{24,8},{1,17},{9,25},{17,1},{25,9},{2,18},{10... | collective-permute-start | bytes 663560 | tf_op jit(solution)/shard_map/ppermute | solution.py:99
  323.6 13.7 %collective-permute-start.57 = (bf16[48,2304]{1,0:T(8,128)(2,1)S(1)}, bf16[48,2304]{1,0:T(8,128)(2,1)S(1)}, u32[]{:S(2)}, u32[]{:S(2)}) collective-permute-start(bf16[48,2304]{1,0:T(8,128)(2,1)S(1)} %pad_maximum_fusion.14), channel_id=1, source_target_pairs={{0,24},{8,16},{16,8},{24,0},{1,25},{9,17},{17,9},{25,1},{2,26},{10... | collective-permute-start | bytes 663560 | tf_op jit(solution)/shard_map/ppermute | solution.py:99
  325.1 14.2 %collective-permute-start.54 = (bf16[48,2368]{1,0:T(8,128)(2,1)S(1)}, bf16[48,2368]{1,0:T(8,128)(2,1)S(1)}, u32[]{:S(2)}, u32[]{:S(2)}) collective-permute-start(bf16[48,2368]{1,0:T(8,128)(2,1)S(1)} %get-tuple-element.201), channel_id=1, source_target_pairs={{0,24},{8,16},{16,8},{24,0},{1,25},{9,17},{17,9},{25,1},{2,26},{10... | collective-permute-start | bytes 681992 | tf_op jit(solution)/shard_map/ppermute | solution.py:99
  326.6 14.9 %collective-permute-start.53 = (bf16[48,2368]{1,0:T(8,128)(2,1)S(1)}, bf16[48,2368]{1,0:T(8,128)(2,1)S(1)}, u32[]{:S(2)}, u32[]{:S(2)}) collective-permute-start(bf16[48,2368]{1,0:T(8,128)(2,1)S(1)} %get-tuple-element.202), channel_id=1, source_target_pairs={{0,16},{8,24},{16,0},{24,8},{1,17},{9,25},{17,1},{25,9},{2,18},{10... | collective-permute-start | bytes 681992 | tf_op jit(solution)/shard_map/ppermute | solution.py:99
  328.1 13.4 %collective-permute-start.52 = (bf16[48,2368]{1,0:T(8,128)(2,1)S(1)}, bf16[48,2368]{1,0:T(8,128)(2,1)S(1)}, u32[]{:S(2)}, u32[]{:S(2)}) collective-permute-start(bf16[48,2368]{1,0:T(8,128)(2,1)S(1)} %get-tuple-element.200), channel_id=1, source_target_pairs={{0,8},{8,0},{16,24},{24,16},{1,9},{9,1},{17,25},{25,17},{2,10},{10... | collective-permute-start | bytes 681992 | tf_op jit(solution)/shard_map/ppermute | solution.py:99
  342.5 25.1 %collective-permute-start.67 = (bf16[48,3648]{1,0:T(8,128)(2,1)S(1)}, bf16[48,3648]{1,0:T(8,128)(2,1)S(1)}, u32[]{:S(2)}, u32[]{:S(2)}) collective-permute-start(bf16[48,3648]{1,0:T(8,128)(2,1)S(1)} %pad_maximum_fusion.4), channel_id=1, source_target_pairs={{0,24},{8,16},{16,8},{24,0},{1,25},{9,17},{17,9},{25,1},{2,26},{10... | collective-permute-start | bytes 1050632 | tf_op jit(solution)/shard_map/ppermute | solution.py:99
  345.0 22.5 %collective-permute-start.66 = (bf16[48,3648]{1,0:T(8,128)(2,1)S(1)}, bf16[48,3648]{1,0:T(8,128)(2,1)S(1)}, u32[]{:S(2)}, u32[]{:S(2)}) collective-permute-start(bf16[48,3648]{1,0:T(8,128)(2,1)S(1)} %pad_maximum_fusion.4), channel_id=1, source_target_pairs={{0,16},{8,24},{16,0},{24,8},{1,17},{9,25},{17,1},{25,9},{2,18},{10... | collective-permute-start | bytes 1050632 | tf_op jit(solution)/shard_map/ppermute | solution.py:99
  345.2 22.4 %collective-permute-start.65 = (bf16[48,3648]{1,0:T(8,128)(2,1)S(1)}, bf16[48,3648]{1,0:T(8,128)(2,1)S(1)}, u32[]{:S(2)}, u32[]{:S(2)}) collective-permute-start(bf16[48,3648]{1,0:T(8,128)(2,1)S(1)} %pad_maximum_fusion.4), channel_id=1, source_target_pairs={{0,8},{8,0},{16,24},{24,16},{1,9},{9,1},{17,25},{25,17},{2,10},{10... | collective-permute-start | bytes 1050632 | tf_op jit(solution)/shard_map/ppermute | solution.py:99
  (67 other events, 537.0 us)
Sparse Core Ops, SparseCore 0:
  32.1 83.7 all-gather.1
  189.9 41.7 reduce-scatter.1

commit v3 on v2

--- a/solution.py
+++ b/solution.py
@@ -222,17 +222,10 @@
     return c * r, r
 
 
-def norm_grad(dm, y, r, scale):
-    dy = dm * (1.0 + scale)
-    dv = r * (dy - jnp.mean(dy, axis=-1, keepdims=True) - y * jnp.mean(dy * y, axis=-1, keepdims=True))
-    return dv, jnp.sum(dm, axis=0, keepdims=True), jnp.sum(dm * y, axis=0, keepdims=True)
-
-
-def wpart(w, j, lo, hi):
+def wcols(w, lo, hi):
     if len(w.shape) == 2:
-        width = w.shape[1] // CHUNKS
-        return w[:, j * width + lo : j * width + hi]
-    return w[j, :, :, :, lo:hi].reshape(D, hi - lo)
+        return w[:, lo:hi]
+    return w[:, :, :, lo:hi].reshape(D, hi - lo)
 
 
 def head_masks():
@@ -241,121 +234,162 @@
     return low, 1.0 - low
 
 
+def each(fn, *vals):
+    outs = [fn(t, *[v[t * NTOK : (t + 1) * NTOK] for v in vals]) for t in range(vals[0].shape[0] // NTOK)]
+    return jnp.concatenate(outs, axis=0)
+
+
+def flat(ref):
+    return ref[...].reshape(ref.shape[0] * NTOK, ref.shape[-1])
+
+
+def flat_cols(ref, lo, hi):
+    return ref[:, :, lo:hi].reshape(ref.shape[0] * NTOK, hi - lo)
+
+
+def unflat(val):
+    return val.reshape(val.shape[0] // NTOK, NTOK, val.shape[-1])
+
+
+QKV, OUT, UP, DOWN = (0, 3 * D), (3 * D, 4 * D), (4 * D, 4 * D + FF), (4 * D + FF, TOKW)
+HALF = FF // 2
+
+
 def block_forward(h, mod, w, bias, sv):
     qkv_ref, p_ref, o_ref, g_ref, gp_ref, att_ref, mlp_ref, h2_ref = sv
     y1, _ = layer_norm(h)
-    n1 = (y1 * (1.0 + mod(1)) + mod(0)).astype(BF16)
-    qkv_ref[...] = dot(n1, wpart(w, 0, 0, CW)).astype(BF16)
+    n1 = each(lambda t, y: (y * (1.0 + mod(t, 1)) + mod(t, 0)).astype(BF16), y1)
+    qkv_ref[...] = unflat(dot(n1, wcols(w, *QKV)).astype(BF16))
     masks = head_masks()
     for j in range(3):
-        q2 = qkv_ref[:, 128 * j : 128 * j + 128]
-        k2 = qkv_ref[:, D + 128 * j : D + 128 * j + 128]
-        v2 = qkv_ref[:, 2 * D + 128 * j : 2 * D + 128 * j + 128]
-        o2 = None
-        for a in range(2):
-            s = dot_nt(q2, k2 * (masks[a] * 0.125).astype(BF16))
-            if bias is not None:
-                s = s + bias
-            e = jnp.exp(s - jnp.max(s, axis=-1, keepdims=True))
-            p = (e * (1.0 / jnp.sum(e, axis=-1, keepdims=True))).astype(BF16)
-            p_ref[2 * j + a] = p
-            part = dot(p, v2 * masks[a].astype(BF16))
-            o2 = part if o2 is None else o2 + part
-        o_ref[:, 128 * j : 128 * j + 128] = o2.astype(BF16)
-    att = dot(o_ref[...], wpart(w, 1, 0, D))
-    att_ref[...] = att.astype(BF16)
-    h2 = h + mod(2) * att
-    h2_ref[...] = h2
+        for t in range(h.shape[0] // NTOK):
+            q2 = qkv_ref[t, :, 128 * j : 128 * j + 128]
+            k2 = qkv_ref[t, :, D + 128 * j : D + 128 * j + 128]
+            v2 = qkv_ref[t, :, 2 * D + 128 * j : 2 * D + 128 * j + 128]
+            o2 = None
+            for a in range(2):
+                s = dot_nt(q2, k2 * (masks[a] * 0.125).astype(BF16))
+                if bias is not None:
+                    s = s + bias[t]
+                e = jnp.exp(s - jnp.max(s, axis=-1, keepdims=True))
+                p = (e * (1.0 / jnp.sum(e, axis=-1, keepdims=True))).astype(BF16)
+                p_ref[t, 2 * j + a] = p
+                part = dot(p, v2 * masks[a].astype(BF16))
+                o2 = part if o2 is None else o2 + part
+            o_ref[t, :, 128 * j : 128 * j + 128] = o2.astype(BF16)
+    att = dot(flat(o_ref), wcols(w, *OUT))
+    att_ref[...] = unflat(att.astype(BF16))
+    h2 = each(lambda t, x, y: x + mod(t, 2) * y, h, att)
+    h2_ref[...] = unflat(h2)
     y2, _ = layer_norm(h2)
-    n2 = (y2 * (1.0 + mod(4)) + mod(3)).astype(BF16)
-    for j, lo, hi, at in ((1, D, CW, 0), (2, 0, 2 * D, 2 * D)):
-        u = dot(n2, wpart(w, j, lo, hi))
+    n2 = each(lambda t, y: (y * (1.0 + mod(t, 4)) + mod(t, 3)).astype(BF16), y2)
+    for at in range(0, FF, HALF):
+        u = dot(n2, wcols(w, UP[0] + at, UP[0] + at + HALF))
         u2 = u * u
         t = jnp.tanh(u * (GELU_C + (GELU_C * 0.044715) * u2))
         half = 0.5 * t + 0.5
-        g_ref[:, at : at + 2 * D] = (u * half).astype(BF16)
+        g_ref[:, :, at : at + HALF] = unflat((u * half).astype(BF16))
         gp = half + (u * (0.5 - 0.5 * t * t)) * (GELU_C + (3.0 * GELU_C * 0.044715) * u2)
-        gp_ref[:, at : at + 2 * D] = gp.astype(BF16)
-    mlp = dot_nt(g_ref[:, 0:D], wpart(w, 2, 2 * D, CW)) + dot_nt(g_ref[:, D:], wpart(w, 3, 0, CW))
-    mlp_ref[...] = mlp.astype(BF16)
-    return h2 + mod(5) * mlp
-
-
-def block_backward(d3, h, mod, w, sv, dw, du_ref, dqkv_ref, dmod):
+        gp_ref[:, :, at : at + HALF] = unflat(gp.astype(BF16))
+    mlp = dot_nt(flat(g_ref), wcols(w, *DOWN))
+    mlp_ref[...] = unflat(mlp.astype(BF16))
+    return each(lambda t, x, y: x + mod(t, 5) * y, h2, mlp)
+
+
+def put_sums(put, i, val):
+    for t in range(val.shape[0] // NTOK):
+        put(t, i, jnp.sum(val[t * NTOK : (t + 1) * NTOK], axis=0, keepdims=True))
+
+
+def norm_grad(dm, y, r, mod, i, put):
+    put_sums(put, i, dm)
+    put_sums(put, i + 1, dm * y)
+    dy = each(lambda t, x: x * (1.0 + mod(t, i + 1)), dm)
+    return r * (dy - jnp.mean(dy, axis=-1, keepdims=True) - y * jnp.mean(dy * y, axis=-1, keepdims=True))
+
+
+def block_backward(d3, h, mod, w, sv, dw, du_ref, dqkv_ref, put):
     qkv_ref, p_ref, o_ref, g_ref, gp_ref, att_ref, mlp_ref, h2_ref = sv
-    dmlp = (d3 * mod(5)).astype(BF16)
-    dmod(5, jnp.sum(d3 * mlp_ref[...].astype(F32), axis=0, keepdims=True))
-    du_ref[:, 0:D] = (dot(dmlp, wpart(w, 2, 2 * D, CW)) * gp_ref[:, 0:D].astype(F32)).astype(BF16)
-    du_ref[:, D:] = (dot(dmlp, wpart(w, 3, 0, CW)) * gp_ref[:, D:].astype(F32)).astype(BF16)
-    dw[2, :, 2 * D : CW] += dot_tn(dmlp, g_ref[:, 0:D])
-    dw[3, :, 0:CW] += dot_tn(dmlp, g_ref[:, D:])
-    dn2 = dot_nt(du_ref[:, 0 : 2 * D], wpart(w, 1, D, CW)) + dot_nt(du_ref[:, 2 * D :], wpart(w, 2, 0, 2 * D))
-    y2, r2 = layer_norm(h2_ref[...])
-    n2 = (y2 * (1.0 + mod(4)) + mod(3)).astype(BF16)
-    dw[1, :, D:CW] += dot_tn(n2, du_ref[:, 0 : 2 * D])
-    dw[2, :, 0 : 2 * D] += dot_tn(n2, du_ref[:, 2 * D :])
-    dv, dshift, dscale = norm_grad(dn2, y2, r2, mod(4))
-    dmod(3, dshift)
-    dmod(4, dscale)
-    d2 = d3 + dv
-    datt = (d2 * mod(2)).astype(BF16)
-    dmod(2, jnp.sum(d2 * att_ref[...].astype(F32), axis=0, keepdims=True))
-    do = dot_nt(datt, wpart(w, 1, 0, D)).astype(BF16)
-    dw[1, :, 0:D] += dot_tn(o_ref[...], datt)
+    dmlp = each(lambda t, x: (x * mod(t, 5)).astype(BF16), d3)
+    put_sums(put, 5, d3 * flat(mlp_ref).astype(F32))
+    for at in range(0, FF, HALF):
+        dg = dot(dmlp, wcols(w, DOWN[0] + at, DOWN[0] + at + HALF))
+        du_ref[:, at : at + HALF] = (dg * flat_cols(gp_ref, at, at + HALF).astype(F32)).astype(BF16)
+    dw[:, DOWN[0] : DOWN[1]] += dot_tn(dmlp, flat(g_ref))
+    dn2 = dot_nt(du_ref[...], wcols(w, *UP))
+    y2, r2 = layer_norm(flat(h2_ref))
+    n2 = each(lambda t, y: (y * (1.0 + mod(t, 4)) + mod(t, 3)).astype(BF16), y2)
+    dw[:, UP[0] : UP[1]] += dot_tn(n2, du_ref[...])
+    d2 = d3 + norm_grad(dn2, y2, r2, mod, 3, put)
+    datt = each(lambda t, x: (x * mod(t, 2)).astype(BF16), d2)
+    put_sums(put, 2, d2 * flat(att_ref).astype(F32))
+    do = dot_nt(datt, wcols(w, *OUT)).astype(BF16)
+    dw[:, OUT[0] : OUT[1]] += dot_tn(flat(o_ref), datt)
     masks = head_masks()
     for j in range(3):
-        q2 = qkv_ref[:, 128 * j : 128 * j + 128]
-        k2 = qkv_ref[:, D + 128 * j : D + 128 * j + 128]
-        v2 = qkv_ref[:, 2 * D + 128 * j : 2 * D + 128 * j + 128]
-        do2 = do[:, 128 * j : 128 * j + 128]
-        dq2, dk2, dv2 = 0.0, 0.0, 0.0
-        for a in range(2):
-            one = masks[a].astype(BF16)
-            eighth = (masks[a] * 0.125).astype(BF16)
-            pb = p_ref[2 * j + a]
-            p = pb.astype(F32)
-            dp = dot_nt(do2, v2 * one)
-            ds = (p * (dp - jnp.sum(p * dp, axis=-1, keepdims=True))).astype(BF16)
-            dq2 += dot(ds, k2 * eighth)
-            dk2 += dot_tn(ds, q2 * eighth)
-            dv2 += dot_tn(pb, do2 * one)
-        dqkv_ref[:, 128 * j : 128 * j + 128] = dq2.astype(BF16)
-        dqkv_ref[:, D + 128 * j : D + 128 * j + 128] = dk2.astype(BF16)
-        dqkv_ref[:, 2 * D + 128 * j : 2 * D + 128 * j + 128] = dv2.astype(BF16)
-    dn1 = dot_nt(dqkv_ref[...], wpart(w, 0, 0, CW))
+        for t in range(h.shape[0] // NTOK):
+            rows = slice(t * NTOK, (t + 1) * NTOK)
+            q2 = qkv_ref[t, :, 128 * j : 128 * j + 128]
+            k2 = qkv_ref[t, :, D + 128 * j : D + 128 * j + 128]
+            v2 = qkv_ref[t, :, 2 * D + 128 * j : 2 * D + 128 * j + 128]
+            do2 = do[rows, 128 * j : 128 * j + 128]
+            dq2, dk2, dv2 = 0.0, 0.0, 0.0
+            for a in range(2):
+                one = masks[a].astype(BF16)
+                eighth = (masks[a] * 0.125).astype(BF16)
+                pb = p_ref[t, 2 * j + a]
+                p = pb.astype(F32)
+                dp = dot_nt(do2, v2 * one)
+                ds = (p * (dp - jnp.sum(p * dp, axis=-1, keepdims=True))).astype(BF16)
+                dq2 += dot(ds, k2 * eighth)
+                dk2 += dot_tn(ds, q2 * eighth)
+                dv2 += dot_tn(pb, do2 * one)
+            dqkv_ref[rows, 128 * j : 128 * j + 128] = dq2.astype(BF16)
+            dqkv_ref[rows, D + 128 * j : D + 128 * j + 128] = dk2.astype(BF16)
+            dqkv_ref[rows, 2 * D + 128 * j : 2 * D + 128 * j + 128] = dv2.astype(BF16)
+    dn1 = dot_nt(dqkv_ref[...], wcols(w, *QKV))
     y1, r1 = layer_norm(h)
-    n1 = (y1 * (1.0 + mod(1)) + mod(0)).astype(BF16)
-    dw[0, :, 0:CW] += dot_tn(n1, dqkv_ref[...])
-    dv, dshift, dscale = norm_grad(dn1, y1, r1, mod(1))
-    dmod(0, dshift)
-    dmod(1, dscale)
-    return d2 + dv
-
-
-def load_weights(ids, pieces, w, sems, base=0):
-    @pl.when(pl.program_id(0) == 0)
+    n1 = each(lambda t, y: (y * (1.0 + mod(t, 1)) + mod(t, 0)).astype(BF16), y1)
+    dw[:, QKV[0] : QKV[1]] += dot_tn(n1, dqkv_ref[...])
+    return d2 + norm_grad(dn1, y1, r1, mod, 0, put)
+
+
+def weight_copies(ids, pieces, w, sems, base):
+    copies = []
+    if len(pieces) == 1:
+        for n, (lo, hi) in enumerate((QKV, OUT, UP, (DOWN[0], w.shape[1]))):
+            copies.append(pltpu.make_async_copy(pieces[0].at[:, base + lo : base + hi], w.at[:, lo:hi], sems.at[n]))
+        return [[c] for c in copies]
+    for c in range(2):
+        core = ids[2] ^ c
+        for k in range(4):
+            at = pl.multiple_of((ids[1] ^ k) * CW, 128)
+            copies.append(pltpu.make_async_copy(pieces[c].at[k, :, :, 0:CW], w.at[:, core, :, pl.ds(at, CW)], sems.at[4 * c + k]))
+        copies.append(pltpu.make_async_copy(pieces[c].at[0, :, :, CW:], w.at[:, core, :, TOKW:], sems.at[8 + c]))
+    return [copies, [], [], []]
+
+
+def load_weights(ids, pieces, w, sems, base=0, work=None):
+    first = pl.program_id(0) == 0
+
+    @pl.when(first)
     def _():
-        copies = []
-        if len(pieces) == 1:
-            copies.append(pltpu.make_async_copy(pieces[0].at[:, base : base + w.shape[1]], w, sems.at[0]))
-        else:
-            for c in range(2):
-                for k in range(4):
-                    target = w.at[ids[1] ^ k, :, ids[2] ^ c]
-                    copies.append(pltpu.make_async_copy(pieces[c].at[k], target, sems.at[4 * c + k]))
+        copies = [c for part in weight_copies(ids, pieces, w, sems, base) for c in part]
         for copy in copies:
             copy.start()
+        if work is not None:
+            work()
         for copy in copies:
             copy.wait()
 
 
-def mod_row(mods, base, step):
-    return lambda i: mods[pl.ds(step, 1), base + D * i : base + D * i + D]
-
-
-def row_writer(dmod, step):
-    def write(i, val):
-        dmod[pl.ds(step, 1), D * i : D * i + D] = val
+def mod_row(mods, base, slot):
+    return lambda t, i: mods[pl.ds(slot + t, 1), base + D * i : base + D * i + D]
+
+
+def row_writer(dmod, slot):
+    def write(t, i, val):
+        dmod[pl.ds(slot + t, 1), D * i : D * i + D] = val
 
     return write
 
@@ -369,41 +403,52 @@
     pieces, (misc, h0, h3), sv, (w, sems) = rest[:n], rest[n : n + 3], rest[n + 3 : n + 11], rest[n + 11 :]
     load_weights(ids, pieces, w, sems)
     step = pl.program_id(0)
+    slot = step * xin.shape[0]
 
     @pl.when(step == 0)
     def _():
-        misc[...] = wpart(w, 0, CW, CW + 128)
-
-    @pl.when(step < ids[0])
+        misc[...] = wcols(w, TOKW, TOKW + 128)
+
+    @pl.when(slot < ids[0])
     def _():
-        h = dot_nt(xin[...], misc[...]) + pe[...]
-        h0[...] = h
-        h3[...] = block_forward(h, mod_row(mods, 0, step), w, bias[...], sv)
+        h = each(lambda t, x: x + pe[...], dot_nt(flat(xin), misc[...]))
+        h0[...] = unflat(h)
+        h3[...] = unflat(block_forward(h, mod_row(mods, 0, slot), w, bias, sv))
 
 
 def side_forward_kernel(n, ids, h_in, mask, pe, misc, mods, *rest):
     pieces, (hs, h3), sv, (w, sems) = rest[:n], rest[n : n + 2], rest[n + 2 : n + 10], rest[n + 10 :]
     load_weights(ids, pieces, w, sems)
     step = pl.program_id(0)
-
-    @pl.when(step < ids[0])
+    slot = step * h_in.shape[0]
+
+    @pl.when(slot < ids[0])
     def _():
-        m = mask[...]
-        h = h_in[...] * (1.0 - m) + m * (token_row(misc) + pe[...])
-        hs[...] = h
-        h3[...] = block_forward(h, mod_row(mods, 0, step), w, None, sv)
+        token = token_row(misc) + pe[...]
+        h = each(lambda t, x: x * (1.0 - mask[t]) + mask[t] * token, flat(h_in))
+        hs[...] = unflat(h)
+        h3[...] = unflat(block_forward(h, mod_row(mods, 0, slot), w, None, sv))
 
 
 def store_grads(ids, dw, outs):
+    def cols(rows, j):
+        return dw[rows, j * CW : (j + 1) * CW].astype(BF16)
+
+    extra = dw.shape[1] > TOKW
+    zero = jnp.zeros((D // 8, 128), BF16)
     if len(outs) == 1:
         for j in range(CHUNKS):
-            outs[0][j] = dw[j].astype(BF16)
+            outs[0][j, :, 0:CW] = cols(slice(None), j)
+            if extra:
+                outs[0][j, :, CW:] = dw[:, TOKW:].astype(BF16) if j == 0 else jnp.zeros((D, 128), BF16)
         return
     for side in range(2):
         for z in range(4):
-            at = pl.multiple_of((2 * z + (ids[2] ^ side)) * (D // 8), 16)
+            rows = pl.ds(pl.multiple_of((2 * z + (ids[2] ^ side)) * (D // 8), 16), D // 8)
             for j in range(CHUNKS):
-                outs[side][j, z] = dw[j, pl.ds(at, D // 8), :].astype(BF16)
+                outs[side][j, z, :, 0:CW] = cols(rows, j)
+                if extra:
+                    outs[side][j, z, :, CW:] = dw[rows, TOKW:].astype(BF16) if j == 0 else zero
 
 
 def dec_kernel(n, m, ids, coef, h_in, noise, misc, mods, *rest):
@@ -412,49 +457,50 @@
     dw_out = rest[n + 4 : n + 4 + m]
     w, sems, dw, du, dqkv = rest[n + 4 + m : n + 9 + m]
     sv = rest[n + 9 + m :]
-    load_weights(ids, pieces, w, sems, TOKW)
     step = pl.program_id(0)
-
-    @pl.when(step == 0)
-    def _():
+    slot = step * h_in.shape[0]
+
+    def clear():
         dw[...] = jnp.zeros_like(dw)
         dmisc[...] = jnp.zeros_like(dmisc)
         loss[...] = jnp.zeros_like(loss)
         dmod[...] = jnp.zeros_like(dmod)
 
-    @pl.when(step < ids[0])
+    load_weights(ids, pieces, w, sems, TOKW, clear)
+
+    @pl.when(slot < ids[0])
     def _():
-        row = mod_row(mods, 6 * D, step)
-        put = row_writer(dmod, step)
-        h = h_in[...]
+        row = mod_row(mods, 6 * D, slot)
+        put = row_writer(dmod, slot)
+        h = flat(h_in)
         h_dec = block_forward(h, row, w, None, sv)
         yf, rf = layer_norm(h_dec)
-        nf = (yf * (1.0 + row(7)) + row(6)).astype(BF16)
-        out = dot(nf, misc[...])
-        ln_b, ln_pv, wmean = coef[step, 0], coef[step, 1], coef[step, 2]
+        nf = each(lambda t, y: (y * (1.0 + row(t, 7)) + row(t, 6)).astype(BF16), yf)
         lane = lax.broadcasted_iota(jnp.int32, (1, 128), 1)
-        live = (lane >= 32) & (lane < 32 + PIN)
-        d = jnp.where(live, out - noise[...], 0.0)
-        vf = (pltpu.roll(out, 128 - 32, 1) + 1.0) * 0.5
-        vf = jnp.where(live, vf, 0.0)
-        lv = vf * ln_b + (1.0 - vf) * ln_pv
-        first = jnp.exp(ln_pv - lv)
-        second = wmean * jnp.exp(-lv)
-        inv = 0.5 / math.log(2.0)
-        dd = d * d
-        kl = inv * (-1.0 + lv - ln_pv + first + dd * second)
-        term = jnp.where(live, dd + kl, 0.0)
-        loss[...] += jnp.sum(term.reshape(NTOK // 8, 8, 128), axis=0)
-        deps = d * (2.0 + (2.0 * inv) * second)
-        dlog = inv * (1.0 - first - dd * second) * (0.5 * (ln_b - ln_pv))
-        dlog = jnp.where(live, dlog, 0.0)
-        dout = (deps + pltpu.roll(dlog, 32, 1)).astype(BF16)
+
+        def head(t, out):
+            ln_b, ln_pv, wmean = coef[slot + t, 0], coef[slot + t, 1], coef[slot + t, 2]
+            live = (lane >= 32) & (lane < 32 + PIN) & (slot + t < ids[0])
+            d = jnp.where(live, out - noise[t], 0.0)
+            vf = (pltpu.roll(out, 128 - 32, 1) + 1.0) * 0.5
+            vf = jnp.where(live, vf, 0.0)
+            lv = vf * ln_b + (1.0 - vf) * ln_pv
+            first = jnp.exp(ln_pv - lv)
+            second = wmean * jnp.exp(-lv)
+            inv = 0.5 / math.log(2.0)
+            dd = d * d
+            kl = inv * (-1.0 + lv - ln_pv + first + dd * second)
+            term = jnp.where(live, dd + kl, 0.0)
+            loss[...] += jnp.sum(term.reshape(NTOK // 8, 8, 128), axis=0)
+            deps = d * (2.0 + (2.0 * inv) * second)
+            dlog = inv * (1.0 - first - dd * second) * (0.5 * (ln_b - ln_pv))
+            dlog = jnp.where(live, dlog, 0.0)
+            return (deps + pltpu.roll(dlog, 32, 1)).astype(BF16)
+
+        dout = each(head, dot(nf, misc[...]))
         dmisc[...] += dot_tn(nf, dout)
-        dnf = dot_nt(dout, misc[...])
-        d3, dshift, dscale = norm_grad(dnf, yf, rf, row(7))
-        put(6, dshift)
-        put(7, dscale)
-        d_in[...] = block_backward(d3, h, row, w, sv, dw, du, dqkv, put)
+        d3 = norm_grad(dot_nt(dout, misc[...]), yf, rf, row, 6, put)
+        d_in[...] = unflat(block_backward(d3, h, row, w, sv, dw, du, dqkv, put))
 
     @pl.when(step == pl.num_programs(0) - 1)
     def _():
@@ -466,22 +512,22 @@
     d_enc, dmod, dtok = rest[:3]
     dw_out = rest[3 : 3 + m]
     w, sems, dw, du, dqkv = rest[3 + m :]
-    load_weights(ids, pieces, w, sems)
     step = pl.program_id(0)
-
-    @pl.when(step == 0)
-    def _():
+    slot = step * h_in.shape[0]
+
+    def clear():
         dw[...] = jnp.zeros_like(dw)
         dtok[...] = jnp.zeros_like(dtok)
         dmod[...] = jnp.zeros_like(dmod)
 
-    @pl.when(step < ids[0])
+    load_weights(ids, pieces, w, sems, 0, clear)
+
+    @pl.when(slot < ids[0])
     def _():
-        hidden = mask[...]
-        dh = block_backward(d_out[...], h_in[...], mod_row(mods, 0, step), w, sv, dw, du, dqkv, row_writer(dmod, step))
-        dm = dh * hidden
-        dtok[...] += jnp.sum(dm.reshape(NTOK // 8, 8, D), axis=0)
-        d_enc[...] = dh - dm
+        dh = block_backward(flat(d_out), flat(h_in), mod_row(mods, 0, slot), w, sv, dw, du, dqkv, row_writer(dmod, slot))
+        dm = each(lambda t, x: x * mask[t], dh)
+        dtok[...] += jnp.sum(dm.reshape(-1, 8, D), axis=0)
+        d_enc[...] = unflat(dh - dm)
 
     @pl.when(step == pl.num_programs(0) - 1)
     def _():
@@ -493,23 +539,24 @@
     dmod = rest[0]
     dw_out = rest[1 : 1 + m]
     w, sems, dw, du, dqkv = rest[1 + m :]
-    load_weights(ids, pieces, w, sems)
     step = pl.program_id(0)
-
-    @pl.when(step == 0)
-    def _():
+    slot = step * h_in.shape[0]
+
+    def clear():
         dw[...] = jnp.zeros_like(dw)
         dmod[...] = jnp.zeros_like(dmod)
         lane = lax.broadcasted_iota(jnp.int32, (8, 128), 1)
         token = lax.dot_general(
             dtok[...], (lane == PIN).astype(F32), (((0,), (0,)), ((), ())), precision=lax.Precision.HIGHEST, preferred_element_type=F32
         )
-        dw[0, :, CW : CW + 128] = dmisc[...] + token
-
-    @pl.when(step < ids[0])
+        dw[:, TOKW:] = dmisc[...] + token
+
+    load_weights(ids, pieces, w, sems, 0, clear)
+
+    @pl.when(slot < ids[0])
     def _():
-        dh = block_backward(d_out[...], h_in[...], mod_row(mods, 0, step), w, sv, dw, du, dqkv, row_writer(dmod, step))
-        dw[0, :, CW : CW + 128] += dot_tn(dh.astype(BF16), xin[...])
+        dh = block_backward(flat(d_out), flat(h_in), mod_row(mods, 0, slot), w, sv, dw, du, dqkv, row_writer(dmod, slot))
+        dw[:, TOKW:] += dot_tn(dh.astype(BF16), flat(xin))
 
     @pl.when(step == pl.num_programs(0) - 1)
     def _():
@@ -553,8 +600,11 @@
 ANY = pl.BlockSpec(memory_space=pl.ANY)
 
 
-def slot_spec(*shape):
-    return pl.BlockSpec((None,) + shape, lambda s, ids: (jnp.minimum(s, jnp.maximum(ids[0] - 1, 0)),) + (0,) * len(shape))
+def slot_spec(*shape, together=1):
+    def index(s, ids):
+        return (jnp.minimum(s, jnp.maximum((ids[0] + together - 1) // together - 1, 0)),) + (0,) * len(shape)
+
+    return pl.BlockSpec((together,) + shape, index)
 
 
 def fixed_spec(*shape):
@@ -574,15 +624,15 @@
 
 
 def weight_scratch(pieces, width):
-    shape = (D, CHUNKS * width) if len(pieces) == 1 else (CHUNKS, 4, 2, D // 8, width)
-    return [pltpu.VMEM(shape, BF16), pltpu.SemaphoreType.DMA((8,))]
-
-
-def grad_scratch(width):
+    shape = (D, width) if len(pieces) == 1 else (4, 2, D // 8, width)
+    return [pltpu.VMEM(shape, BF16), pltpu.SemaphoreType.DMA((10,))]
+
+
+def grad_scratch(width, together=1):
     return [
-        pltpu.VMEM((CHUNKS, D, width), F32),
-        pltpu.VMEM((NTOK, FF), BF16),
-        pltpu.VMEM((NTOK, 3 * D), BF16),
+        pltpu.VMEM((D, width), F32),
+        pltpu.VMEM((together * NTOK, FF), BF16),
+        pltpu.VMEM((together * NTOK, 3 * D), BF16),
     ]
 
 
@@ -592,13 +642,13 @@
     return [fixed_out((CHUNKS, D, width), BF16)]
 
 
-def call(kernel, slots, ids, in_specs, args, pieces, outs, scratch, macs):
+def call(kernel, slots, ids, in_specs, args, pieces, outs, scratch, macs, together=1):
     specs = list(in_specs) + [ANY] * len(pieces)
     return pl.pallas_call(
         functools.partial(kernel, len(pieces)),
         grid_spec=pltpu.PrefetchScalarGridSpec(
             num_scalar_prefetch=1,
-            grid=(slots,),
+            grid=(slots // together,),
             in_specs=specs,
             out_specs=[o[0] for o in outs],
             scratch_shapes=scratch,
@@ -609,8 +659,8 @@
     )(ids, *args, *pieces)
 
 
-def slot_out(slots, shape, kind):
-    return (slot_spec(*shape), (slots,) + shape, kind)
+def slot_out(slots, shape, kind, together=1):
+    return (slot_spec(*shape, together=together), (slots,) + shape, kind)
 
 
 def fixed_out(shape, kind):
@@ -631,7 +681,7 @@
         [xin, pe, mods, bias],
         pieces,
         [fixed_out((D, 128), BF16)] + [slot_out(slots, (NTOK, D), F32)] * 2 + [slot_out(slots, s, k) for s, k in SAVES],
-        weight_scratch(pieces, CW + 128),
+        weight_scratch(pieces, TOKW + 128),
         BLOCK_MACS,
     )
 
@@ -645,23 +695,25 @@
         [h_in, mask, pe, misc, mods],
         pieces,
         [slot_out(slots, (NTOK, D), F32)] * 2 + [slot_out(slots, s, k) for s, k in SAVES],
-        weight_scratch(pieces, CW),
+        weight_scratch(pieces, TOKW),
         BLOCK_MACS,
     )
 
 
 def dec_both(slots, ids, coef, h_in, noise, misc, mods, pieces, split):
     outs = grad_outs(split, CW)
+    pair = 2 if slots % 2 == 0 else 1
     return call(
         lambda n, *refs: dec_kernel(n, len(outs), *refs),
         slots,
         ids,
-        [SMEM, slot_spec(NTOK, D), slot_spec(NTOK, 128), fixed_spec(D, 128), fixed_spec(*MODS_R)],
+        [SMEM, slot_spec(NTOK, D, together=pair), slot_spec(NTOK, 128, together=pair), fixed_spec(D, 128), fixed_spec(*MODS_R)],
         [coef, h_in, noise, misc, mods],
         pieces,
-        [slot_out(slots, (NTOK, D), F32), fixed_out((8, 8 * D), F32), fixed_out((D, 128), F32), fixed_out((8, 128), F32)] + outs,
-        weight_scratch(pieces, CW) + grad_scratch(CW) + [pltpu.VMEM(s, k) for s, k in SAVES],
+        [slot_out(slots, (NTOK, D), F32, pair), fixed_out((8, 8 * D), F32), fixed_out((D, 128), F32), fixed_out((8, 128), F32)] + outs,
+        weight_scratch(pieces, TOKW) + grad_scratch(TOKW, pair) + [pltpu.VMEM((pair,) + s, k) for s, k in SAVES],
         3 * BLOCK_MACS,
+        pair,
     )
 
 
@@ -675,7 +727,7 @@
         [d_out, h_in, mask, mods] + list(saves),
         pieces,
         [slot_out(slots, (NTOK, D), F32), fixed_out((8, 6 * D), F32), fixed_out((8, D), F32)] + outs,
-        weight_scratch(pieces, CW) + grad_scratch(CW),
+        weight_scratch(pieces, TOKW) + grad_scratch(TOKW),
         2 * BLOCK_MACS,
     )
 
@@ -691,7 +743,7 @@
         [d_out, h_in, xin, mods, dmisc, dtok] + list(saves),
         pieces,
         [fixed_out((8, 6 * D), F32)] + outs,
-        weight_scratch(pieces, CW + 128) + grad_scratch(CW + 128),
+        weight_scratch(pieces, TOKW + 128) + grad_scratch(TOKW + 128),
         2 * BLOCK_MACS,
     )
 
@@ -809,8 +861,10 @@
         at = D + b * STRIDE
         row_part, down_part = rows_b[:, at : at + 4 * D + FF], down_b[:, b * FF : (b + 1) * FF]
         cols = [row_part[:, :CW], row_part[:, CW : 2 * CW], row_part[:, 2 * CW :], down_part[:, :D], down_part[:, D:]]
-        if b == 0:
+        if b == 0 and split:
             cols = [cols[0], misc_own, cols[1], misc_own, cols[2], cols[3], misc_own, cols[4], misc_own]
+        elif b == 0:
+            cols = cols + [misc_own]
         whole = jnp.concatenate(cols, axis=1)
         wholes.append(whole)
     enc_z = gather_z(wholes[0]) if split else None
@@ -863,13 +917,16 @@
     dmod_e, *dw_e = enc_backward(slots, ids, d_enc, h0, x_in, mods_e, dmisc, dtok, save_e, enc_w, split)
     total_s = grad_sum(tie(part_s, dmod_e, mine_d))
     dmods = jnp.concatenate([dmod_e, dmod_s, dmod_d], axis=1).astype(BF16)
+    level = gather_open(after(dmods, total_s), "fsdp", 0)
     core_e = grad_core(dw_e, total_s)
-    part_d = reduce_open(after(mine_d, total_s), "dp", BF16)
+    if split:
+        core_e[1] = after(core_e[1], *level[1:])
     part_e = grad_dp(core_e)
 
-    dm_all = gather(after(dmods, part_e[0]), "fsdp").reshape(nf * 8, -1)
-    g_side = grad_z(after(total_s, dm_all)) if split else grad_z(total_s)
-    g_dec = total_of(tie(part_d, part_e[0])).astype(BF16)
+    level = tie(level, part_e[0])
+    for at in range(last):
+        level = gather_open(gather_close(level, "fsdp", at), "fsdp", at + 1)
+    dm_all = gather_shape(gather_close(level, "fsdp", last), "fsdp", dmods.shape).reshape(nf * 8, -1)
     d_cond = dot_nt(w_ada, dm_all) * silu_slope(cond)
     d_cond_all = gather(d_cond.astype(BF16), "fsdp").reshape(D, nf * 8)
     d_apre = (dot(w_ttwo, d_cond_all) * silu_slope(a_pre)).astype(BF16)
@@ -877,9 +934,11 @@
     kinds = [dot(s_cond, dm_all), dot_nt(a_act, d_cond_all), dot(d_apre, feat), g_class, jnp.zeros((rows, 128), F32)]
     kinds = jnp.concatenate([k.astype(BF16) for k in kinds], axis=1).reshape(rows, CHUNKS, -1).transpose(1, 0, 2)
 
-    total_e = grad_sum(tie(part_e, dm_all, g_dec))
+    g_side = grad_z(after(total_s, d_cond)) if split else grad_z(total_s)
+    total_e = grad_sum(tie(part_e, d_cond_all))
     g_enc = grad_z(total_e)
-    first = after(jnp.concatenate([g_side, g_dec], axis=1), total_e)
+    g_dec = total_of(reduce_open(after(mine_d, total_e), "dp", BF16)).astype(BF16)
+    first = jnp.concatenate([g_side, g_dec], axis=1)
     full = gather_open(first, "dp", 0)
     g_other = total_of(reduce_open(after(kinds, full[0]), "dp", BF16)).astype(BF16)
     second = after(jnp.concatenate([g_enc, g_other], axis=1), *full)

time: 401 us -> 387 us (0.965)
  waiting for transfers between devices: 67 us -> 56.3 us
  Pallas kernels: 148 us -> 141 us
  starting transfers between devices: 77.5 us -> 83.5 us
    ppermute x68, waiting for transfers between devices: 67 us -> 56.2 us  [swap(): return lax.ppermute(val, axis, [(i, i ^ mask) for i in range(size)])]
    pallas_call x5, Pallas kernels: 145 us -> 138 us  [call(): pl.pallas_call(functools.partial(kernel, len(pieces)), grid_spec=pltpu.Pr...]
    ppermute x68, starting transfers between devices: 77.4 us -> 83.5 us  [swap(): return lax.ppermute(val, axis, [(i, i ^ mask) for i in range(size)])]
  transfers between devices with their start and end apart: 70 -> 70, of which waited for: 25 -> 23; matrix products, arithmetic and copies ran while one was open for 11% -> 11% of each run, Pallas kernels for 26% -> 27%
where the time goes in v3:
time: 387 us; the launch traced here: 381 us
  Pallas kernels  141 us (36%)
  starting transfers between devices  83.5 us (22%)
  waiting for transfers between devices  56.3 us (15%)
  other arithmetic  40.9 us (11%)
  local copies, waits for them, and re-layouts  32.7 us (8%)
  between operations  22.6 us (6%)
    pallas_call x5, Pallas kernels, call(): pl.pallas_call(functools.partial(kernel, len(pieces)), grid_spec=pltpu.Pr...  138 us
    ppermute x68, starting transfers between devices, swap(): return lax.ppermute(val, axis, [(i, i ^ mask) for i in range(size)])  83.5 us
    ppermute x68, waiting for transfers between devices, swap(): return lax.ppermute(val, axis, [(i, i ^ mask) for i in range(size)])  56.2 us
    sub x3, other arithmetic, adam(): master - learn_rate * (first_hat / (jnp.sqrt(second_hat) + adam_eps) + we...  8.56 us
  transfers between devices with their start and end apart: 70, of which 23 were waited for; matrix products, arithmetic and copies ran while one was open for 11% of the time, Pallas kernels for 27%

profile of v3, /device:TPU:0, one launch (start us, length us, event | category | flops | bytes accessed | tf_op | source)
XLA Modules:
  0.0 381.1 jit_solution(11375138088212120144)
XLA Ops:
  16.3 4.0 %collective-permute-start.1 = (bf16[8,4480]{1,0:T(8,128)(2,1)}, bf16[8,4480]{1,0:T(8,128)(2,1)}, u32[]{:S(2)}, u32[]{:S(2)}) collective-permute-start(bf16[8,4480]{1,0:T(8,128)(2,1)} %pad.20), channel_id=1, source_target_pairs={{0,4},{1,5},{2,6},{3,7},{4,0},{5,1},{6,2},{7,3},{8,12},{9,13},{10,... | collective-permute-start | bytes 215048 | tf_op jit(solution)/shard_map/ppermute | solution.py:99
  26.6 2.8 collective-permute-start.13
  36.2 2.5 collective-permute-done.13
  42.5 3.2 shard_map.257
  45.7 2.5 collective-permute-start.17
  54.3 2.7 collective-permute-start.7
  65.6 2.5 collective-permute-start.11
  70.1 2.5 collective-permute-done.11
  76.7 8.0 %collective-permute-done.15 = bf16[4,48,1280]{2,1,0:T(8,128)(2,1)S(1)} collective-permute-done((bf16[4,48,1280]{2,1,0:T(8,128)(2,1)S(1)}, bf16[4,48,1280]{2,1,0:T(8,128)(2,1)S(1)}, u32[]{:S(2)}, u32[]{:S(2)}) %collective-permute-start.15) | collective-permute-done | bytes 491552 | tf_op jit(solution)/shard_map/ppermute | solution.py:99
  86.5 3.0 collective-permute-start.21
  90.9 23.6 %shard_map.258 = (bf16[384,128]{1,0:T(8,128)(2,1)}, f32[6,256,384]{2,1,0:T(8,128)}, f32[6,256,384]{2,1,0:T(8,128)}, bf16[6,256,1152]{2,1,0:T(8,128)(2,1)}, bf16[...) custom-call(s32[3]{0:T(128)} %pad_add_fusion.ids.refs_0_, ...), custom_call_target="tpu_custom_call" | custom-call | flops 1509949440 | bytes 4000000 | tf_op jit(solution)/shard_map/pallas_call | solution.py:647
  115.3 4.4 %collective-permute-start.25 = (bf16[8,4096]{1,0:T(8,128)(2,1)S(1)}, bf16[8,4096]{1,0:T(8,128)(2,1)S(1)}, u32[]{:S(2)}, u32[]{:S(2)}) collective-permute-start(bf16[8,4096]{1,0:T(8,128)(2,1)S(1)} %pad.23), channel_id=1, source_target_pairs={{0,6},{1,7},{2,4},{3,5},{4,2},{5,3},{6,0},{7,1},{8,14},{9,15},{10,... | collective-permute-start | bytes 196616 | tf_op jit(solution)/shard_map/ppermute | solution.py:99
  119.7 23.1 %shard_map.259 = (f32[6,256,384]{2,1,0:T(8,128)}, f32[6,256,384]{2,1,0:T(8,128)}, bf16[6,256,1152]{2,1,0:T(8,128)(2,1)}, bf16[6,6,256,256]{3,2,1,0:T(8,128)(2,1)...) custom-call(s32[3]{0:T(128)} %pad_add_fusion.ids.refs_0_, ...), custom_call_target="tpu_custom_call" | custom-call | flops 1509949440 | bytes 4000000 | tf_op jit(solution)/shard_map/pallas_call | solution.py:647
  146.3 38.6 %shard_map.260 = (f32[6,256,384]{2,1,0:T(8,128)}, f32[8,3072]{1,0:T(8,128)}, f32[384,128]{1,0:T(8,128)}, f32[8,128]{1,0:T(8,128)}, bf16[4,384,1152]{2,1,0:T(8,128)(2,1)}) custom-call(s32[3]{0:T(128)} %pad_add_fusion.ids.refs_0_, f32[8,3]{1,0:T(8,128)} %pad_maximum_fusion.18.refs_1_, f32[6,256,384]{2,1,0:T(8,128)} %get-tuple-element.97.refs_2_, ...), custom_call_target="tpu_custom_call" | custom-call | flops 4529848320 | bytes 4000000 | tf_op jit(solution)/shard_map/pallas_call | solution.py:647
  184.9 26.5 %shard_map.261 = (f32[6,256,384]{2,1,0:T(8,128)}, f32[8,2304]{1,0:T(8,128)}, f32[8,384]{1,0:T(8,128)}, bf16[4,4,48,1152]{3,2,1,0:T(8,128)(2,1)}, bf16[4,4,48,1152]{3,2,1,0:T(8,128)(2,1)}) custom-call(s32[3]{0:T(128)} %pad_add_fusion.ids.refs_0_, f32[6,256,384]{2,1,0:T(8,128)} %get-tuple-element.105.refs_1_, f32[6,256,384]{2,1,0:T(8,128)} %get-tuple-element.100.refs_2_, ...), custom_call_target="tpu_custom_call" | custom-call | flops 3019898880 | bytes 4000000 | tf_op jit(solution)/shard_map/pallas_call | solution.py:647
  211.7 3.9 %collective-permute-done.27 = bf16[4,4,48,1152]{3,2,1,0:T(8,128)(2,1)S(1)} collective-permute-done((bf16[4,4,48,1152]{3,2,1,0:T(8,128)(2,1)}, bf16[4,4,48,1152]{3,2,1,0:T(8,128)(2,1)S(1)}, u32[]{:S(2)}, u32[]{:S(2)}) %collective-permute-start.27) | collective-permute-done | bytes 1769504 | tf_op jit(solution)/shard_map/ppermute | solution.py:99
  215.6 2.8 fusion.27
  221.9 26.4 %shard_map.262 = (f32[8,2304]{1,0:T(8,128)}, bf16[4,4,48,1280]{3,2,1,0:T(8,128)(2,1)}, bf16[4,4,48,1280]{3,2,1,0:T(8,128)(2,1)}) custom-call(s32[3]{0:T(128)} %pad_add_fusion.ids.refs_0_, f32[6,256,384]{2,1,0:T(8,128)} %get-tuple-element.117.refs_1_, f32[6,256,384]{2,1,0:T(8,128)} %get-tuple-element.118.refs_2_, bf16[6,256,128]{2,1,0:T(8,128)(2,1)} %pad.22.xin.refs_3_, ...), custom_call_target="tpu_custom_call" | custom-call | flops 3019898880 | bytes 4000000 | tf_op jit(solution)/shard_map/pallas_call | solution.py:647
  250.4 4.3 %collective-permute-start.33 = (bf16[8,7680]{1,0:T(8,128)(2,1)S(1)}, bf16[8,7680]{1,0:T(8,128)(2,1)S(1)}, u32[]{:S(2)}, u32[]{:S(2)}) collective-permute-start(bf16[8,7680]{1,0:T(8,128)(2,1)S(1)} %pad_maximum_fusion.15), channel_id=1, source_target_pairs={{0,6},{1,7},{2,4},{3,5},{4,2},{5,3},{6,0},{7,1},{8,14},{9,15},{10,... | collective-permute-start | bytes 368648 | tf_op jit(solution)/shard_map/ppermute | solution.py:99
  254.7 2.5 collective-permute-done.31
  257.1 5.5 %collective-permute-done.32 = bf16[8,7680]{1,0:T(8,128)(2,1)S(1)} collective-permute-done((bf16[8,7680]{1,0:T(8,128)(2,1)S(1)}, bf16[8,7680]{1,0:T(8,128)(2,1)S(1)}, u32[]{:S(2)}, u32[]{:S(2)}) %collective-permute-start.32) | collective-permute-done | bytes 122912 | tf_op jit(solution)/shard_map/ppermute | solution.py:99
  270.2 2.6 collective-permute-start.43
  272.9 2.5 collective-permute-start.44
  275.7 2.4 collective-permute-start.41
  284.8 6.7 %collective-permute-done.40 = bf16[4,48,1280]{2,1,0:T(8,128)(2,1)} collective-permute-done((bf16[4,48,1280]{2,1,0:T(8,128)(2,1)S(1)}, bf16[4,48,1280]{2,1,0:T(8,128)(2,1)}, u32[]{:S(2)}, u32[]{:S(2)}) %collective-permute-start.40) | collective-permute-done | bytes 491552 | tf_op jit(solution)/shard_map/ppermute | solution.py:99
  302.2 2.9 collective-permute-start.50
  317.5 5.5 %collective-permute-done.56 = bf16[48,2304]{1,0:T(8,128)(2,1)S(1)} collective-permute-done((bf16[48,2304]{1,0:T(8,128)(2,1)S(1)}, bf16[48,2304]{1,0:T(8,128)(2,1)S(1)}, u32[]{:S(2)}, u32[]{:S(2)}) %collective-permute-start.56) | collective-permute-done | bytes 221216 | tf_op jit(solution)/shard_map/ppermute | solution.py:99
  324.2 4.2 %collective-permute-done.53 = bf16[48,2368]{1,0:T(8,128)(2,1)S(1)} collective-permute-done((bf16[48,2368]{1,0:T(8,128)(2,1)S(1)}, bf16[48,2368]{1,0:T(8,128)(2,1)S(1)}, u32[]{:S(2)}, u32[]{:S(2)}) %collective-permute-start.53) | collective-permute-done | bytes 227360 | tf_op jit(solution)/shard_map/ppermute | solution.py:99
  336.7 2.4 collective-permute-start.60
  339.1 2.5 collective-permute-start.61
  362.7 2.7 concatenate.90
  365.4 4.1 %multiply_subtract_fusion = (f32[48,4328]{1,0:T(8,128)}, f32[48,4328]{1,0:T(8,128)}, f32[48,4328]{1,0:T(8,128)}) fusion(f32[48,17312]{1,0:T(8,128)} %param.28, s32[]{:T(128)S(6)} %select_n.889, bf16[48,17312]{1,0:T(8,128)(2,1)S(1)} %concatenate.90, f32[]{:T(128)S(6)} %mul.214, f32[48,17312]{1,0:T(8,128)} %param.29, f32[48,17312]{1,0:T(8,128)} %param.30), kind=kLoop, calls=%fused_computation.28 | loop fusion | flops 3531648 | bytes 5401352 | tf_op jit(solution)/shard_map/sub | solution.py:784
  (343 shorter events, 124.5 us)
Async XLA Ops:
  7.2 112.5 %all-gather.2.cloned.1.call-start = ((), (), s32[]{:S(2)}) async-start(), calls=%async_computation.1 | async-start | bytes 7962624 | tf_op jit(solution)/shard_map/all_gather | solution.py:204
  16.3 18.6 %collective-permute-start.1 = (bf16[8,4480]{1,0:T(8,128)(2,1)}, bf16[8,4480]{1,0:T(8,128)(2,1)}, u32[]{:S(2)}, u32[]{:S(2)}) collective-permute-start(bf16[8,4480]{1,0:T(8,128)(2,1)} %pad.20), channel_id=1, source_target_pairs={{0,4},{1,5},{2,6},{3,7},{4,0},{5,1},{6,2},{7,3},{8,12},{9,13},{10,... | collective-permute-start | bytes 215048 | tf_op jit(solution)/shard_map/ppermute | solution.py:99
  20.4 14.6 %collective-permute-start.2 = (bf16[8,4480]{1,0:T(8,128)(2,1)}, bf16[8,4480]{1,0:T(8,128)(2,1)}, u32[]{:S(2)}, u32[]{:S(2)}) collective-permute-start(bf16[8,4480]{1,0:T(8,128)(2,1)} %pad.20), channel_id=1, source_target_pairs={{0,6},{1,7},{2,4},{3,5},{4,2},{5,3},{6,0},{7,1},{8,14},{9,15},{10,... | collective-permute-start | bytes 215048 | tf_op jit(solution)/shard_map/ppermute | solution.py:99
  21.7 13.3 %collective-permute-start = (bf16[8,4480]{1,0:T(8,128)(2,1)}, bf16[8,4480]{1,0:T(8,128)(2,1)}, u32[]{:S(2)}, u32[]{:S(2)}) collective-permute-start(bf16[8,4480]{1,0:T(8,128)(2,1)} %pad.20), channel_id=1, source_target_pairs={{0,2},{1,3},{2,0},{3,1},{4,6},{5,7},{6,4},{7,5},{8,10},{9,11},{10,... | collective-permute-start | bytes 215048 | tf_op jit(solution)/shard_map/ppermute | solution.py:99
  32.0 216.4 %reduce-scatter.2.cloned.1.call-start = ((), (), s32[]{:S(2)}) async-start(), calls=%async_computation.2 | async-start | bytes 3981312 | tf_op jit(solution)/shard_map/reduce_scatter | solution.py:913
  45.7 31.1 %collective-permute-start.17 = (bf16[4,48,1280]{2,1,0:T(8,128)(2,1)S(1)}, bf16[4,48,1280]{2,1,0:T(8,128)(2,1)}, u32[]{:S(2)}, u32[]{:S(2)}) collective-permute-start(bf16[4,48,1280]{2,1,0:T(8,128)(2,1)S(1)} %pad_maximum_fusion.2), channel_id=1, source_target_pairs={{0,24},{8,16},{16,8},{24,0},{1,25},{9,17},{17,9},{25,1},{2,26},{10... | collective-permute-start | bytes 1474568 | tf_op jit(solution)/shard_map/ppermute | solution.py:99
  48.2 28.6 %collective-permute-start.16 = (bf16[4,48,1280]{2,1,0:T(8,128)(2,1)S(1)}, bf16[4,48,1280]{2,1,0:T(8,128)(2,1)}, u32[]{:S(2)}, u32[]{:S(2)}) collective-permute-start(bf16[4,48,1280]{2,1,0:T(8,128)(2,1)S(1)} %pad_maximum_fusion.2), channel_id=1, source_target_pairs={{0,16},{8,24},{16,0},{24,8},{1,17},{9,25},{17,1},{25,9},{2,18},{10... | collective-permute-start | bytes 1474568 | tf_op jit(solution)/shard_map/ppermute | solution.py:99
  86.4 28.1 %collective-permute-start.20 = (bf16[8,5376]{1,0:T(8,128)(2,1)S(1)}, bf16[8,5376]{1,0:T(8,128)(2,1)S(1)}, u32[]{:S(2)}, u32[]{:S(2)}) collective-permute-start(bf16[8,5376]{1,0:T(8,128)(2,1)S(1)} %get-tuple-element.212), channel_id=1, source_target_pairs={{0,2},{1,3},{2,0},{3,1},{4,6},{5,7},{6,4},{7,5},{8,10},{9,11},{10,... | collective-permute-start | bytes 258056 | tf_op jit(solution)/shard_map/ppermute | solution.py:99
  86.5 28.1 %collective-permute-start.21 = (bf16[8,5376]{1,0:T(8,128)(2,1)S(1)}, bf16[8,5376]{1,0:T(8,128)(2,1)S(1)}, u32[]{:S(2)}, u32[]{:S(2)}) collective-permute-start(bf16[8,5376]{1,0:T(8,128)(2,1)S(1)} %get-tuple-element.211), channel_id=1, source_target_pairs={{0,4},{1,5},{2,6},{3,7},{4,0},{5,1},{6,2},{7,3},{8,12},{9,13},{10,... | collective-permute-start | bytes 258056 | tf_op jit(solution)/shard_map/ppermute | solution.py:99
  89.4 25.1 %collective-permute-start.22 = (bf16[8,5376]{1,0:T(8,128)(2,1)S(1)}, bf16[8,5376]{1,0:T(8,128)(2,1)S(1)}, u32[]{:S(2)}, u32[]{:S(2)}) collective-permute-start(bf16[8,5376]{1,0:T(8,128)(2,1)S(1)} %get-tuple-element.210), channel_id=1, source_target_pairs={{0,6},{1,7},{2,4},{3,5},{4,2},{5,3},{6,0},{7,1},{8,14},{9,15},{10,... | collective-permute-start | bytes 258056 | tf_op jit(solution)/shard_map/ppermute | solution.py:99
  115.3 27.5 %collective-permute-start.23 = (bf16[8,4096]{1,0:T(8,128)(2,1)S(1)}, bf16[8,4096]{1,0:T(8,128)(2,1)S(1)}, u32[]{:S(2)}, u32[]{:S(2)}) collective-permute-start(bf16[8,4096]{1,0:T(8,128)(2,1)S(1)} %pad.23), channel_id=1, source_target_pairs={{0,2},{1,3},{2,0},{3,1},{4,6},{5,7},{6,4},{7,5},{8,10},{9,11},{10,... | collective-permute-start | bytes 196616 | tf_op jit(solution)/shard_map/ppermute | solution.py:99
  115.3 27.5 %collective-permute-start.24 = (bf16[8,4096]{1,0:T(8,128)(2,1)S(1)}, bf16[8,4096]{1,0:T(8,128)(2,1)S(1)}, u32[]{:S(2)}, u32[]{:S(2)}) collective-permute-start(bf16[8,4096]{1,0:T(8,128)(2,1)S(1)} %pad.23), channel_id=1, source_target_pairs={{0,4},{1,5},{2,6},{3,7},{4,0},{5,1},{6,2},{7,3},{8,12},{9,13},{10,... | collective-permute-start | bytes 196616 | tf_op jit(solution)/shard_map/ppermute | solution.py:99
  115.3 27.5 %collective-permute-start.25 = (bf16[8,4096]{1,0:T(8,128)(2,1)S(1)}, bf16[8,4096]{1,0:T(8,128)(2,1)S(1)}, u32[]{:S(2)}, u32[]{:S(2)}) collective-permute-start(bf16[8,4096]{1,0:T(8,128)(2,1)S(1)} %pad.23), channel_id=1, source_target_pairs={{0,6},{1,7},{2,4},{3,5},{4,2},{5,3},{6,0},{7,1},{8,14},{9,15},{10,... | collective-permute-start | bytes 196616 | tf_op jit(solution)/shard_map/ppermute | solution.py:99
  218.4 29.9 %collective-permute-start.28 = (bf16[4,48,1152]{2,1,0:T(8,128)(2,1)}, bf16[4,48,1152]{2,1,0:T(8,128)(2,1)}, u32[]{:S(2)}, u32[]{:S(2)}) collective-permute-start(bf16[4,48,1152]{2,1,0:T(8,128)(2,1)} %get-tuple-element.180), channel_id=1, source_target_pairs={{0,8},{8,0},{16,24},{24,16},{1,9},{9,1},{17,25},{25,17},{2,10},{10... | collective-permute-start | bytes 1327112 | tf_op jit(solution)/shard_map/ppermute | solution.py:99
  219.6 28.8 %collective-permute-start.29 = (bf16[4,48,1152]{2,1,0:T(8,128)(2,1)}, bf16[4,48,1152]{2,1,0:T(8,128)(2,1)}, u32[]{:S(2)}, u32[]{:S(2)}) collective-permute-start(bf16[4,48,1152]{2,1,0:T(8,128)(2,1)} %get-tuple-element.179), channel_id=1, source_target_pairs={{0,16},{8,24},{16,0},{24,8},{1,17},{9,25},{17,1},{25,9},{2,18},{10... | collective-permute-start | bytes 1327112 | tf_op jit(solution)/shard_map/ppermute | solution.py:99
  219.6 28.8 %collective-permute-start.30 = (bf16[4,48,1152]{2,1,0:T(8,128)(2,1)S(1)}, bf16[4,48,1152]{2,1,0:T(8,128)(2,1)}, u32[]{:S(2)}, u32[]{:S(2)}) collective-permute-start(bf16[4,48,1152]{2,1,0:T(8,128)(2,1)S(1)} %get-tuple-element.178), channel_id=1, source_target_pairs={{0,24},{8,16},{16,8},{24,0},{1,25},{9,17},{17,9},{25,1},{2,26},{10... | collective-permute-start | bytes 1327112 | tf_op jit(solution)/shard_map/ppermute | solution.py:99
  250.0 12.7 %collective-permute-start.34 = (bf16[4,4,48,1280]{3,2,1,0:T(8,128)(2,1)}, bf16[4,4,48,1280]{3,2,1,0:T(8,128)(2,1)S(1)}, u32[]{:S(2)}, u32[]{:S(2)}) collective-permute-start(bf16[4,4,48,1280]{3,2,1,0:T(8,128)(2,1)} %get-tuple-element.140), channel_id=1, source_target_pairs={{0,1},{1,0},{2,3},{3,2},{4,5},{5,4},{6,7},{7,6},{8,9},{9,8},{10,11... | collective-permute-start | bytes 5898248 | tf_op jit(solution)/shard_map/ppermute | solution.py:99
  250.3 12.4 %collective-permute-start.32 = (bf16[8,7680]{1,0:T(8,128)(2,1)S(1)}, bf16[8,7680]{1,0:T(8,128)(2,1)S(1)}, u32[]{:S(2)}, u32[]{:S(2)}) collective-permute-start(bf16[8,7680]{1,0:T(8,128)(2,1)S(1)} %pad_maximum_fusion.15), channel_id=1, source_target_pairs={{0,4},{1,5},{2,6},{3,7},{4,0},{5,1},{6,2},{7,3},{8,12},{9,13},{10,... | collective-permute-start | bytes 368648 | tf_op jit(solution)/shard_map/ppermute | solution.py:99
  250.4 12.3 %collective-permute-start.33 = (bf16[8,7680]{1,0:T(8,128)(2,1)S(1)}, bf16[8,7680]{1,0:T(8,128)(2,1)S(1)}, u32[]{:S(2)}, u32[]{:S(2)}) collective-permute-start(bf16[8,7680]{1,0:T(8,128)(2,1)S(1)} %pad_maximum_fusion.15), channel_id=1, source_target_pairs={{0,6},{1,7},{2,4},{3,5},{4,2},{5,3},{6,0},{7,1},{8,14},{9,15},{10,... | collective-permute-start | bytes 368648 | tf_op jit(solution)/shard_map/ppermute | solution.py:99
  266.8 16.0 %collective-permute-start.39 = (bf16[4,48,1280]{2,1,0:T(8,128)(2,1)}, bf16[4,48,1280]{2,1,0:T(8,128)(2,1)}, u32[]{:S(2)}, u32[]{:S(2)}) collective-permute-start(bf16[4,48,1280]{2,1,0:T(8,128)(2,1)} %get-tuple-element.176), channel_id=1, source_target_pairs={{0,8},{8,0},{16,24},{24,16},{1,9},{9,1},{17,25},{25,17},{2,10},{10... | collective-permute-start | bytes 1474568 | tf_op jit(solution)/shard_map/ppermute | solution.py:99
  268.0 23.6 %collective-permute-start.40 = (bf16[4,48,1280]{2,1,0:T(8,128)(2,1)S(1)}, bf16[4,48,1280]{2,1,0:T(8,128)(2,1)}, u32[]{:S(2)}, u32[]{:S(2)}) collective-permute-start(bf16[4,48,1280]{2,1,0:T(8,128)(2,1)S(1)} %copy-done.12), channel_id=1, source_target_pairs={{0,16},{8,24},{16,0},{24,8},{1,17},{9,25},{17,1},{25,9},{2,18},{10... | collective-permute-start | bytes 1474568 | tf_op jit(solution)/shard_map/ppermute | solution.py:99
  275.7 15.8 %collective-permute-start.41 = (bf16[4,48,1280]{2,1,0:T(8,128)(2,1)S(1)}, bf16[4,48,1280]{2,1,0:T(8,128)(2,1)}, u32[]{:S(2)}, u32[]{:S(2)}) collective-permute-start(bf16[4,48,1280]{2,1,0:T(8,128)(2,1)S(1)} %copy-done.11), channel_id=1, source_target_pairs={{0,24},{8,16},{16,8},{24,0},{1,25},{9,17},{17,9},{25,1},{2,26},{10... | collective-permute-start | bytes 1474568 | tf_op jit(solution)/shard_map/ppermute | solution.py:99
  279.9 19.0 %collective-permute-start.38 = (bf16[48,1152]{1,0:T(8,128)(2,1)}, bf16[48,1152]{1,0:T(8,128)(2,1)S(1)}, u32[]{:S(2)}, u32[]{:S(2)}) collective-permute-start(bf16[48,1152]{1,0:T(8,128)(2,1)} %get-tuple-element.208), channel_id=1, source_target_pairs={{0,6},{1,7},{2,4},{3,5},{4,2},{5,3},{6,0},{7,1},{8,14},{9,15},{10,... | collective-permute-start | bytes 331784 | tf_op jit(solution)/shard_map/ppermute | solution.py:99
  281.7 19.2 %collective-permute-start.37 = (bf16[48,1152]{1,0:T(8,128)(2,1)}, bf16[48,1152]{1,0:T(8,128)(2,1)}, u32[]{:S(2)}, u32[]{:S(2)}) collective-permute-start(bf16[48,1152]{1,0:T(8,128)(2,1)} %get-tuple-element.209), channel_id=1, source_target_pairs={{0,4},{1,5},{2,6},{3,7},{4,0},{5,1},{6,2},{7,3},{8,12},{9,13},{10,... | collective-permute-start | bytes 331784 | tf_op jit(solution)/shard_map/ppermute | solution.py:99
  282.9 19.4 %collective-permute-start.36 = (bf16[48,1152]{1,0:T(8,128)(2,1)}, bf16[48,1152]{1,0:T(8,128)(2,1)}, u32[]{:S(2)}, u32[]{:S(2)}) collective-permute-start(bf16[48,1152]{1,0:T(8,128)(2,1)} %get-tuple-element.207), channel_id=1, source_target_pairs={{0,2},{1,3},{2,0},{3,1},{4,6},{5,7},{6,4},{7,5},{8,10},{9,11},{10,... | collective-permute-start | bytes 331784 | tf_op jit(solution)/shard_map/ppermute | solution.py:99
  293.9 12.4 %collective-permute-start.48 = (bf16[48,1152]{1,0:T(8,128)(2,1)}, bf16[48,1152]{1,0:T(8,128)(2,1)S(1)}, u32[]{:S(2)}, u32[]{:S(2)}) collective-permute-start(bf16[48,1152]{1,0:T(8,128)(2,1)} %get-tuple-element.226), channel_id=1, source_target_pairs={{0,24},{8,16},{16,8},{24,0},{1,25},{9,17},{17,9},{25,1},{2,26},{10... | collective-permute-start | bytes 331784 | tf_op jit(solution)/shard_map/ppermute | solution.py:99
  308.4 14.7 %collective-permute-start.56 = (bf16[48,2304]{1,0:T(8,128)(2,1)S(1)}, bf16[48,2304]{1,0:T(8,128)(2,1)S(1)}, u32[]{:S(2)}, u32[]{:S(2)}) collective-permute-start(bf16[48,2304]{1,0:T(8,128)(2,1)S(1)} %pad_maximum_fusion.14), channel_id=1, source_target_pairs={{0,16},{8,24},{16,0},{24,8},{1,17},{9,25},{17,1},{25,9},{2,18},{10... | collective-permute-start | bytes 663560 | tf_op jit(solution)/shard_map/ppermute | solution.py:99
  310.3 12.8 %collective-permute-start.57 = (bf16[48,2304]{1,0:T(8,128)(2,1)S(1)}, bf16[48,2304]{1,0:T(8,128)(2,1)S(1)}, u32[]{:S(2)}, u32[]{:S(2)}) collective-permute-start(bf16[48,2304]{1,0:T(8,128)(2,1)S(1)} %pad_maximum_fusion.14), channel_id=1, source_target_pairs={{0,24},{8,16},{16,8},{24,0},{1,25},{9,17},{17,9},{25,1},{2,26},{10... | collective-permute-start | bytes 663560 | tf_op jit(solution)/shard_map/ppermute | solution.py:99
  315.6 12.8 %collective-permute-start.53 = (bf16[48,2368]{1,0:T(8,128)(2,1)S(1)}, bf16[48,2368]{1,0:T(8,128)(2,1)S(1)}, u32[]{:S(2)}, u32[]{:S(2)}) collective-permute-start(bf16[48,2368]{1,0:T(8,128)(2,1)S(1)} %get-tuple-element.202), channel_id=1, source_target_pairs={{0,16},{8,24},{16,0},{24,8},{1,17},{9,25},{17,1},{25,9},{2,18},{10... | collective-permute-start | bytes 681992 | tf_op jit(solution)/shard_map/ppermute | solution.py:99
  329.4 25.6 %collective-permute-start.67 = (bf16[48,3648]{1,0:T(8,128)(2,1)S(1)}, bf16[48,3648]{1,0:T(8,128)(2,1)S(1)}, u32[]{:S(2)}, u32[]{:S(2)}) collective-permute-start(bf16[48,3648]{1,0:T(8,128)(2,1)S(1)} %pad_maximum_fusion.4), channel_id=1, source_target_pairs={{0,24},{8,16},{16,8},{24,0},{1,25},{9,17},{17,9},{25,1},{2,26},{10... | collective-permute-start | bytes 1050632 | tf_op jit(solution)/shard_map/ppermute | solution.py:99
  330.5 24.5 %collective-permute-start.66 = (bf16[48,3648]{1,0:T(8,128)(2,1)S(1)}, bf16[48,3648]{1,0:T(8,128)(2,1)S(1)}, u32[]{:S(2)}, u32[]{:S(2)}) collective-permute-start(bf16[48,3648]{1,0:T(8,128)(2,1)S(1)} %pad_maximum_fusion.4), channel_id=1, source_target_pairs={{0,16},{8,24},{16,0},{24,8},{1,17},{9,25},{17,1},{25,9},{2,18},{10... | collective-permute-start | bytes 1050632 | tf_op jit(solution)/shard_map/ppermute | solution.py:99
  331.6 23.4 %collective-permute-start.65 = (bf16[48,3648]{1,0:T(8,128)(2,1)S(1)}, bf16[48,3648]{1,0:T(8,128)(2,1)S(1)}, u32[]{:S(2)}, u32[]{:S(2)}) collective-permute-start(bf16[48,3648]{1,0:T(8,128)(2,1)S(1)} %pad_maximum_fusion.4), channel_id=1, source_target_pairs={{0,8},{8,0},{16,24},{24,16},{1,9},{9,1},{17,25},{25,17},{2,10},{10... | collective-permute-start | bytes 1050632 | tf_op jit(solution)/shard_map/ppermute | solution.py:99
  (69 other events, 542.7 us)
Sparse Core Ops, SparseCore 0:
  32.1 83.7 all-gather.1
  185.1 40.9 reduce-scatter.1
